TPU v7x, 32 devices: a whole 2x2x4 slice. The times are simulated.
32 devices in a mesh: dp: 16 (over z, y, x), mp: 2 (over core).
Axes of the slice: x: 2, y: 2, z: 4, core: 2. Of those that a mesh axis runs over, the one named last changes fastest.
Arguments:
- tokens: bfloat16 [32, 512, 1024], P('dp'), may hold values from -6 to 6
- text_states: bfloat16 [32, 256, 768], P('dp', 'mp'), may hold values from -6 to 6
- text_len: int32 [32], P('dp'), may hold values from 1 to 256, as said below
- frame_valid: int32 [32], P('dp'), may hold values from 256 to 512, as said below
- ln1_gain: bfloat16 [1024], replicated, may hold values from 0.5 to 1.5
- ln1_bias: bfloat16 [1024], replicated, may hold values from -1 to 1
- ln2_gain: bfloat16 [1024], replicated, may hold values from 0.5 to 1.5
- ln2_bias: bfloat16 [1024], replicated, may hold values from -1 to 1
- ln3_gain: bfloat16 [1024], replicated, may hold values from 0.5 to 1.5
- ln3_bias: bfloat16 [1024], replicated, may hold values from -1 to 1
- w_query: bfloat16 [1024, 1024], P(None, 'mp'), may hold values from -0.1875 to 0.1875
- w_key: bfloat16 [1024, 1024], P(None, 'mp'), may hold values from -0.1875 to 0.1875
- w_value: bfloat16 [1024, 1024], P(None, 'mp'), may hold values from -0.1875 to 0.1875
- w_out: bfloat16 [1024, 1024], P('mp'), may hold values from -0.75 to 0.75
- c_query: bfloat16 [1024, 1024], P(None, 'mp'), may hold values from -0.1875 to 0.1875
- c_key: bfloat16 [768, 1024], P(None, 'mp'), may hold values from -0.21875 to 0.21875
- c_value: bfloat16 [768, 1024], P(None, 'mp'), may hold values from -0.21875 to 0.21875
- c_out: bfloat16 [1024, 1024], P('mp'), may hold values from -0.5 to 0.5
- w_up: bfloat16 [1024, 4096], P(None, 'mp'), may hold values from -0.1875 to 0.1875
- w_down: bfloat16 [4096, 1024], P('mp'), may hold values from -0.09375 to 0.09375
- grad_out: bfloat16 [32, 512, 1024], P('dp', 'mp'), may hold values from -6 to 6
Outputs:
- out: bfloat16 [32, 512, 1024], P('dp', 'mp')
- d_tokens: float32 [32, 512, 1024], P('dp', 'mp')
- d_text_states: float32 [32, 256, 768], P('dp', 'mp')
- d_ln1_gain: float32 [1024], replicated
- d_ln1_bias: float32 [1024], replicated
- d_ln2_gain: float32 [1024], replicated
- d_ln2_bias: float32 [1024], replicated
- d_ln3_gain: float32 [1024], replicated
- d_ln3_bias: float32 [1024], replicated
- d_w_query: float32 [1024, 1024], P(None, 'mp')
- d_w_key: float32 [1024, 1024], P(None, 'mp')
- d_w_value: float32 [1024, 1024], P(None, 'mp')
- d_w_out: float32 [1024, 1024], P('mp')
- d_c_query: float32 [1024, 1024], P(None, 'mp')
- d_c_key: float32 [768, 1024], P(None, 'mp')
- d_c_value: float32 [768, 1024], P(None, 'mp')
- d_c_out: float32 [1024, 1024], P('mp')
- d_w_up: float32 [1024, 4096], P(None, 'mp')
- d_w_down: float32 [4096, 1024], P('mp')
- rms_stats: float32 [4], replicated
Inputs may be any that keep to these rules, and one draw needn't show every extreme that they name: `text_len`: mostly short; the first item of each aligned block of 8 items has 256 tokens. `frame_valid`: the first item of each aligned block of 8 items has all 512 frames valid.
All inputs are finite; a program needn't handle non-finite values.
Results may differ from a plain program's by a relative error of at most 0.023.
Values may be sent and summed in bfloat16 or wider, within the bound.
No kernel may reach another device: no remote copies, remote signals or barrier semaphores. Data moves between devices by JAX's collectives and lax.ppermute only.
A program may use at most 256 MiB of HBM per device.

v0:
```python
from functools import partial

import jax
import jax.numpy as jnp
from jax import lax
from jax.sharding import PartitionSpec as P

HD = 64


norm_eps = 1e-05
score_scale = 0.125
masked_fill = -1e30


def layer_norm(values, gain_vec, offset):
    average = jnp.mean(values, -1, keepdims=True)
    centered = values - average
    variance = jnp.mean(centered * centered, -1, keepdims=True)
    return centered * lax.rsqrt(variance + norm_eps) * gain_vec + offset


def project(inputs, weight):
    return jnp.einsum("bfd,de->bfe", inputs, weight, preferred_element_type=jnp.float32)


def project_back(gradients, weight):
    return jnp.einsum("bfe,de->bfd", gradients, weight, preferred_element_type=jnp.float32)


def weight_grad(inputs, gradients):
    return jnp.einsum("bfd,bfe->de", inputs, gradients, preferred_element_type=jnp.float32)


def block_scores(query_rows, key_rows, allowed):
    scores = (
        jnp.einsum("fhd,jhd->hfj", query_rows, key_rows, preferred_element_type=jnp.float32)
        * score_scale
    )
    return jnp.where(allowed[None], scores, masked_fill)


def attend_forward(query_rows, key_rows, value_rows, allowed):
    scores = block_scores(query_rows, key_rows, allowed)
    highest = jnp.max(scores, -1, keepdims=True)
    powers = jnp.exp(scores - highest)
    row_total = jnp.sum(powers, -1, keepdims=True)
    attn_probs = powers / row_total
    mixture = jnp.einsum(
        "hfj,jhd->fhd",
        attn_probs.astype(jnp.bfloat16),
        value_rows,
        preferred_element_type=jnp.float32,
    )
    return (mixture.astype(jnp.bfloat16), highest + jnp.log(row_total), attn_probs)


def probs_again(query_rows, key_rows, allowed, log_total):
    return jnp.exp(block_scores(query_rows, key_rows, allowed) - log_total)


def attend_backward(query_rows, key_rows, value_rows, attn_probs, grad_mixture):
    grad_probs = jnp.einsum(
        "fhd,jhd->hfj", grad_mixture, value_rows, preferred_element_type=jnp.float32
    )
    grad_values = jnp.einsum(
        "hfj,fhd->jhd",
        attn_probs.astype(jnp.bfloat16),
        grad_mixture,
        preferred_element_type=jnp.float32,
    )
    inner_sum = jnp.sum(grad_probs * attn_probs, -1, keepdims=True)
    grad_scores = (attn_probs * (grad_probs - inner_sum)).astype(jnp.bfloat16)
    grad_queries = (
        jnp.einsum("hfj,jhd->fhd", grad_scores, key_rows, preferred_element_type=jnp.float32)
        * score_scale
    )
    grad_keys = (
        jnp.einsum("hfj,fhd->jhd", grad_scores, query_rows, preferred_element_type=jnp.float32)
        * score_scale
    )
    return (
        grad_queries.astype(jnp.bfloat16),
        grad_keys.astype(jnp.bfloat16),
        grad_values.astype(jnp.bfloat16),
    )


def per_device(
    tokens,
    text_states,
    text_len,
    frame_valid,
    ln1_gain,
    ln1_bias,
    ln2_gain,
    ln2_bias,
    ln3_gain,
    ln3_bias,
    w_query,
    w_key,
    w_value,
    w_out,
    c_query,
    c_key,
    c_value,
    c_out,
    w_up,
    w_down,
    grad_out,
):
    items, frames, width = tokens.shape
    parts = lax.axis_size("mp")
    rank = lax.axis_index("mp")
    shard_rows = frames // parts
    text_rows = text_states.shape[1] * parts
    local_width = w_query.shape[1]
    heads_here = local_width // HD
    gain_one = ln1_gain.astype(jnp.float32)
    bias_one = ln1_bias.astype(jnp.float32)
    gain_two = ln2_gain.astype(jnp.float32)
    bias_two = ln2_bias.astype(jnp.float32)
    gain_three = ln3_gain.astype(jnp.float32)
    bias_three = ln3_bias.astype(jnp.float32)
    positions = jnp.arange(frames)
    causal = positions[None, :] <= positions[:, None]
    text_positions = jnp.arange(text_rows)

    def self_allowed(valid_count):
        return causal & (positions[None, :] < valid_count)

    def cross_allowed(length):
        return jnp.broadcast_to(text_positions[None, :] < length, (frames, text_rows))

    def self_forward(block):
        results = attend_forward(block[0], block[1], block[2], self_allowed(block[3]))
        return results[:2]

    def cross_forward(block):
        results = attend_forward(block[0], block[1], block[2], cross_allowed(block[3]))
        return results[:2]

    def self_backward(block):
        attn_probs = probs_again(block[0], block[1], self_allowed(block[3]), block[4])
        return attend_backward(block[0], block[1], block[2], attn_probs, block[5])

    def cross_backward(block):
        attn_probs = probs_again(block[0], block[1], cross_allowed(block[3]), block[4])
        return attend_backward(block[0], block[1], block[2], attn_probs, block[5])

    def to_heads(values, rows):
        return values.reshape(items, rows, heads_here, HD)

    tokens_full = tokens.astype(jnp.float32)
    normed_one = layer_norm(tokens_full, gain_one, bias_one).astype(jnp.bfloat16)
    w_joined = jnp.concatenate([w_query, w_key, w_value], 1)
    joined_rows = project(normed_one, w_joined).astype(jnp.bfloat16)
    query_self = to_heads(joined_rows[..., :local_width], frames)
    key_self = to_heads(joined_rows[..., local_width : 2 * local_width], frames)
    value_self = to_heads(joined_rows[..., 2 * local_width :], frames)
    self_saved = lax.map(self_forward, (query_self, key_self, value_self, frame_valid))
    mix_self = self_saved[0].reshape(items, frames, local_width)
    attn_out = lax.psum_scatter(project(mix_self, w_out), "mp", scatter_dimension=1, tiled=True)
    first_row = rank * shard_rows
    own_rows = lax.dynamic_slice_in_dim(tokens_full, first_row, shard_rows, 1)
    hidden_one = own_rows + attn_out
    normed_two_own = layer_norm(hidden_one, gain_two, bias_two).astype(jnp.bfloat16)
    normed_two, text_full = (
        lax.all_gather(normed_two_own, "mp", axis=1, tiled=True),
        lax.all_gather(text_states, "mp", axis=1, tiled=True),
    )
    query_cross = to_heads(project(normed_two, c_query).astype(jnp.bfloat16), frames)
    c_joined = jnp.concatenate([c_key, c_value], 1)
    text_joined = project(text_full, c_joined).astype(jnp.bfloat16)
    key_cross = to_heads(text_joined[..., :local_width], text_rows)
    value_cross = to_heads(text_joined[..., local_width:], text_rows)
    cross_saved = lax.map(cross_forward, (query_cross, key_cross, value_cross, text_len))
    mix_cross = cross_saved[0].reshape(items, frames, local_width)
    cross_out = lax.psum_scatter(project(mix_cross, c_out), "mp", scatter_dimension=1, tiled=True)
    hidden_two = hidden_one + cross_out
    normed_three = lax.all_gather(
        layer_norm(hidden_two, gain_three, bias_three).astype(jnp.bfloat16),
        "mp",
        axis=1,
        tiled=True,
    )
    up_rows = project(normed_three, w_up)
    activated = jax.nn.gelu(up_rows, approximate=False).astype(jnp.bfloat16)
    ff_out = lax.psum_scatter(
        project(activated, w_down).astype(jnp.bfloat16), "mp", scatter_dimension=1, tiled=True
    ).astype(jnp.float32)
    result_full = hidden_two + ff_out
    result = result_full.astype(jnp.bfloat16)
    row_valid = ((first_row + jnp.arange(shard_rows))[None, :] < frame_valid[:, None]).astype(
        jnp.float32
    )[:, :, None]

    def masked_square(values):
        return jnp.sum(row_valid * values * values)

    stat_terms = jnp.stack(
        [
            masked_square(result_full),
            masked_square(attn_out),
            masked_square(cross_out),
            masked_square(ff_out),
            jnp.sum(row_valid),
        ]
    )
    stat_totals = lax.psum(stat_terms, ("dp", "mp"))
    stat_extra = jnp.zeros((0,), jnp.float32)
    grad_ff = lax.all_gather(grad_out, "mp", axis=1, tiled=True)
    grad_act = project_back(grad_ff, w_down)
    d_w_down = weight_grad(activated, grad_ff)
    gelu_pull = jax.vjp(partial(jax.nn.gelu, approximate=False), up_rows)[1]
    grad_up = gelu_pull(grad_act)[0].astype(jnp.bfloat16)
    d_w_up = weight_grad(normed_three, grad_up)
    grad_n3 = lax.psum_scatter(
        project_back(grad_up, w_up).astype(jnp.bfloat16), "mp", scatter_dimension=1, tiled=True
    ).astype(jnp.float32)
    norm_pull = jax.vjp(layer_norm, hidden_two, gain_three, bias_three)[1]
    grad_h2_norm, d_gain_three, d_bias_three = norm_pull(grad_n3)
    grad_h2 = grad_out.astype(jnp.float32) + grad_h2_norm
    grad_cross = lax.all_gather(grad_h2.astype(jnp.bfloat16), "mp", axis=1, tiled=True)
    d_c_out = weight_grad(mix_cross, grad_cross)
    grad_mix_cross = to_heads(project_back(grad_cross, c_out).astype(jnp.bfloat16), frames)
    cross_kept = cross_saved[1]
    cross_grads = lax.map(
        cross_backward, (query_cross, key_cross, value_cross, text_len, cross_kept, grad_mix_cross)
    )
    grad_q_cross = cross_grads[0].reshape(items, frames, local_width)
    grad_kv_cross = jnp.concatenate(
        [
            cross_grads[1].reshape(items, text_rows, local_width),
            cross_grads[2].reshape(items, text_rows, local_width),
        ],
        -1,
    )
    d_c_query = weight_grad(normed_two, grad_q_cross)
    d_c_joined = weight_grad(text_full, grad_kv_cross)
    grad_n2, d_text_part = (
        lax.psum_scatter(
            project_back(grad_q_cross, c_query).astype(jnp.bfloat16),
            "mp",
            scatter_dimension=1,
            tiled=True,
        ).astype(jnp.float32),
        lax.psum_scatter(
            project_back(grad_kv_cross, c_joined).astype(jnp.bfloat16),
            "mp",
            scatter_dimension=1,
            tiled=True,
        ).astype(jnp.float32),
    )
    norm_pull = jax.vjp(layer_norm, hidden_one, gain_two, bias_two)[1]
    grad_h1_norm, d_gain_two, d_bias_two = norm_pull(grad_n2)
    grad_h1 = grad_h2 + grad_h1_norm
    grad_attn = lax.all_gather(grad_h1.astype(jnp.bfloat16), "mp", axis=1, tiled=True)
    d_w_out = weight_grad(mix_self, grad_attn)
    grad_mix_self = to_heads(project_back(grad_attn, w_out).astype(jnp.bfloat16), frames)
    self_kept = self_saved[1]
    self_grads = lax.map(
        self_backward, (query_self, key_self, value_self, frame_valid, self_kept, grad_mix_self)
    )
    grad_joined = jnp.concatenate(
        [
            self_grads[0].reshape(items, frames, local_width),
            self_grads[1].reshape(items, frames, local_width),
            self_grads[2].reshape(items, frames, local_width),
        ],
        -1,
    )
    d_w_joined = weight_grad(normed_one, grad_joined)
    grad_n1 = lax.psum_scatter(
        project_back(grad_joined, w_joined).astype(jnp.bfloat16),
        "mp",
        scatter_dimension=1,
        tiled=True,
    ).astype(jnp.float32)
    norm_pull = jax.vjp(layer_norm, own_rows, gain_one, bias_one)[1]
    grad_x_norm, d_gain_one, d_bias_one = norm_pull(grad_n1)
    d_tokens = grad_h1 + grad_x_norm
    summed = lax.psum((d_w_joined, d_w_out, d_c_query, d_c_joined, d_c_out, d_w_up, d_w_down), "dp")
    small = lax.psum(
        (d_gain_one, d_bias_one, d_gain_two, d_bias_two, d_gain_three, d_bias_three, stat_extra),
        ("dp", "mp"),
    )
    rms_stats = jnp.sqrt(stat_totals[:4] / (stat_totals[4] * width))
    joined_sum = summed[0]
    key_value_sum = summed[3]
    return (
        result,
        d_tokens,
        d_text_part,
        small[0],
        small[1],
        small[2],
        small[3],
        small[4],
        small[5],
        joined_sum[:, :local_width],
        joined_sum[:, local_width : 2 * local_width],
        joined_sum[:, 2 * local_width :],
        summed[1],
        summed[2],
        key_value_sum[:, :local_width],
        key_value_sum[:, local_width:],
        summed[4],
        summed[5],
        summed[6],
        rms_stats,
    )


def solution(mesh):
    return jax.shard_map(
        per_device,
        mesh=mesh,
        in_specs=(
            P("dp", None, None),
            P("dp", "mp", None),
            P("dp"),
            P("dp"),
            P(),
            P(),
            P(),
            P(),
            P(),
            P(),
            P(None, "mp"),
            P(None, "mp"),
            P(None, "mp"),
            P("mp", None),
            P(None, "mp"),
            P(None, "mp"),
            P(None, "mp"),
            P("mp", None),
            P(None, "mp"),
            P("mp", None),
            P("dp", "mp", None),
        ),
        out_specs=(
            P("dp", "mp", None),
            P("dp", "mp", None),
            P("dp", "mp", None),
            P(),
            P(),
            P(),
            P(),
            P(),
            P(),
            P(None, "mp"),
            P(None, "mp"),
            P(None, "mp"),
            P("mp", None),
            P(None, "mp"),
            P(None, "mp"),
            P(None, "mp"),
            P("mp", None),
            P(None, "mp"),
            P("mp", None),
            P(),
        ),
        check_vma=False,
    )
```

profile of v0, /device:TPU:0, one launch (start us, length us, event | category | flops | bytes accessed | tf_op | source)
XLA Modules:
  0.0 1289.3 jit_solution(2374021280429876912)
XLA Ops:
  25.4 16.3 %while.56 = (s32[]{:T(128)}, bf16[2,512,8,64]{1,3,2,0:T(8,128)(2,1)}, f32[2,8,512,1]{2,1,3,0:T(8,128)S(1)}, bf16[2,512,8,64]{1,3,2,0:T(8,128)(2,1)}, s32[2]{0:T(...) while((s32[]{:T(128)}, ...), condition=%wide.region_5.6_spmd.clone, body=%wide.region_2.5_spmd.clone.sunk | while | flops 562819584 | bytes 41028804 | solution.py:161
  51.7 10.5 reduce-scatter.8.cloned.1.call-done
  85.6 13.3 %while.57 = (s32[]{:T(128)}, bf16[2,512,8,64]{1,3,2,0:T(8,128)(2,1)}, f32[2,8,512,1]{2,1,3,0:T(8,128)S(1)}, bf16[2,256,8,64]{1,3,2,0:T(8,128)(2,1)}, s32[2]{0:T(...) while((s32[]{:T(128)}, ...), condition=%wide.region_12.13_spmd.clone, body=%wide.region_9.12_spmd.clone.sunk | while | flops 281276672 | bytes 24776132 | solution.py:177
  103.6 13.3 %reduce-scatter.10.cloned.1.call-done = f32[2,256,1024]{2,1,0:T(8,128)} async-done(((f32[2,512,1024]{2,1,0:T(8,128)}), f32[2,256,1024]{2,1,0:T(8,128)}) %reduce-scatter.10.cloned.1.call-update) | async-done | bytes 2097168 | tf_op jit(solution)/shard_map/reduce_scatter | solution.py:179
  122.5 11.0 all-gather.8.cloned.1.call-done
  133.5 9.9 fusion.162
  146.8 20.2 %multiply_convert_fusion.2 = (bf16[2,512,2048]{2,1,0:T(8,128)(2,1)}, f32[2,512,2048]{2,1,0:T(8,128)}) fusion(f32[2,512,2048]{2,1,0:T(8,128)S(1)} %get-tuple-element.534, u8[512,2048]{1,0:T(8,128)(4,1)S(1)} %get-tuple-element.400, u8[512,2048]{1,0:T(8,128)(4,1)S(1)} %get-tuple-element.399), kind=kLoop, calls=%fused_computation.146 | loop fusion | flops 146800640 | bytes 23068672 | tf_op jit(solution)/shard_map/convert_element_type | solution.py:188
  167.0 12.8 add_convert_fusion
  181.9 5.7 fusion.163
  187.8 9.3 fusion.166
  198.5 13.8 %reduce-scatter.12.cloned.1.call-done = bf16[2,256,1024]{2,1,0:T(8,128)(2,1)} async-done(((bf16[2,512,1024]{2,1,0:T(8,128)(2,1)}), bf16[2,256,1024]{2,1,0:T(8,128)(2,1)}) %reduce-scatter.12.cloned.1.call-update) | async-done | bytes 1048592 | tf_op jit(solution)/shard_map/reduce_scatter | solution.py:189
  212.3 6.0 fusion.159
  221.9 11.8 all-gather.12.cloned.1.call-done
  238.6 19.8 %while.58 = (s32[]{:T(128)}, bf16[2,512,8,64]{1,3,2,0:T(8,128)(2,1)}, bf16[2,256,8,64]{1,3,2,0:T(8,128)(2,1)}, bf16[2,256,8,64]{1,3,2,0:T(8,128)(2,1)}, bf16[2,2...) while((s32[]{:T(128)}, ...), condition=%wide.region_22.23_spmd.clone, body=%wide.region_20.22_spmd.clone.sunk | while | flops 687730944 | bytes 64871328 | solution.py:228
  262.7 10.9 reduce-scatter.16.cloned.1.call-done
  301.4 28.6 %while.59 = (s32[]{:T(128)}, bf16[2,512,8,64]{1,3,2,0:T(8,128)(2,1)}, bf16[2,512,8,64]{1,3,2,0:T(8,128)(2,1)}, bf16[2,512,8,64]{1,3,2,0:T(8,128)(2,1)}, bf16[2,5...) while((s32[]{:T(128)}, ...), condition=%wide.region_28.29_spmd.clone, body=%wide.region_26.28_spmd.clone.sunk | while | flops 1375465984 | bytes 98687320 | solution.py:262
  334.4 6.9 convolution_convert_fusion.1
  341.6 10.9 convolution_bitcast_fusion.1
  352.6 6.8 convolution_bitcast_fusion
  370.1 6.5 convolution_bitcast_fusion.2
  389.8 46.2 %all-reduce = (f32[1024]{0:T(1024)}, f32[1024]{0:T(1024)}, f32[1024]{0:T(1024)}, f32[1024]{0:T(1024)}, f32[1024]{0:T(1024)}, /*index=5*/f32[1024]{0:T(1024)}, f32[5]{0:T(128)S(1)}) all-reduce(f32[1024]{0:T(1024)S(1)} %get-tuple-element.401, f32[1024]{0:T(1024)S(1)} %get-tuple-element.413, ...), channel_id=1, replica_groups=mesh['dp'=16,'mp'=2] {'dp','mp'}, use_global_device_ids=true, to_apply=%region_36.37 | all-reduce | flops 6149 | bytes 49192 | tf_op jit(solution)/shard_map/psum | solution.py:284
  441.4 811.3 %all-reduce.4.cloned.1.call-done = (f32[1024,1536]{1,0:T(8,128)}, f32[512,1024]{1,0:T(8,128)}, f32[1024,512]{1,0:T(8,128)}, f32[768,1024]{0,1:T(8,128)}, f32[512...) async-done(((f32[1024,1536]{1,0:T(8,128)}, f32[512,1024]{1,0:T(8,128)}, f32[1024,512]{1,0:T(8,128)}, f32[768,1024]{0,1:T(8,128)}, f32[512,1024]{1,0:T(8,128)}, ...) | async-done | bytes 32505872 | tf_op jit(solution)/shard_map/psum | solution.py:283
  1252.7 5.9 fusion.197
  1270.5 8.6 copy.222
  (429 shorter events, 234.7 us)
Async XLA Ops:
  7.2 91.7 %copy-start = (bf16[512,1024]{1,0:T(8,128)(2,1)S(1)}, bf16[512,1024]{1,0:T(8,128)(2,1)}, u32[]{:S(2)}) copy-start(bf16[512,1024]{1,0:T(8,128)(2,1)} %param.46) | copy-start | bytes 3145732
  7.2 55.0 %reduce-scatter.8.cloned.1.call-start = ((), (), s32[]{:S(2)}) async-start(), calls=%async_computation.7 | async-start | bytes 6291456 | tf_op jit(solution)/shard_map/reduce_scatter | solution.py:163
  47.4 33.0 %all-gather.6.cloned.1.call-start = ((), (), s32[]{:S(2)}) async-start(), calls=%async_computation.8 | async-start | bytes 3145728 | tf_op jit(solution)/shard_map/all_gather | solution.py:169
  51.7 14.7 %copy-start.61 = (f32[1024]{0:T(1024)}, f32[1024]{0:T(1024)S(1)}, u32[]{:S(2)}) copy-start(f32[1024]{0:T(1024)S(1)} %convert_element_type.182) | copy-start | bytes 12292
  68.4 48.5 %reduce-scatter.10.cloned.1.call-start = ((), (), s32[]{:S(2)}) async-start(), calls=%async_computation.9 | async-start | bytes 6291456 | tf_op jit(solution)/shard_map/reduce_scatter | solution.py:179
  103.5 30.0 %all-gather.8.cloned.1.call-start = ((), (), s32[]{:S(2)}) async-start(), calls=%async_computation.10 | async-start | bytes 3145728 | tf_op jit(solution)/shard_map/all_gather | solution.py:181
  121.5 45.5 %all-gather.10.cloned.1.call-start = ((), (), s32[]{:S(2)}) async-start(), calls=%async_computation.12 | async-start | bytes 3145728 | tf_op jit(solution)/shard_map/all_gather | solution.py:212
  122.1 76.5 %reduce-scatter.14.cloned.1.call-start = ((), (), s32[]{:S(2)}) async-start(), calls=%async_computation.13 | async-start | bytes 3145728 | tf_op jit(solution)/shard_map/reduce_scatter | solution.py:218
  167.0 14.9 %copy-start.89 = (bf16[1024,2048]{1,0:T(8,128)(2,1)S(1)}, bf16[1024,2048]{1,0:T(8,128)(2,1)}, u32[]{:S(2)}) copy-start(bf16[1024,2048]{1,0:T(8,128)(2,1)} %param.47) | copy-start | bytes 12582916
  187.6 24.7 %reduce-scatter.12.cloned.1.call-start = ((), (), s32[]{:S(2)}) async-start(), calls=%async_computation.11 | async-start | bytes 3145728 | tf_op jit(solution)/shard_map/reduce_scatter | solution.py:189
  197.1 36.6 %all-gather.12.cloned.1.call-start = ((), (), s32[]{:S(2)}) async-start(), calls=%async_computation.14 | async-start | bytes 3145728 | tf_op jit(solution)/shard_map/all_gather | solution.py:224
  221.8 51.7 %reduce-scatter.16.cloned.1.call-start = ((), (), s32[]{:S(2)}) async-start(), calls=%async_computation.15 | async-start | bytes 3145728 | tf_op jit(solution)/shard_map/reduce_scatter | solution.py:242
  258.4 15.2 %copy-start.62 = (f32[1024]{0:T(1024)S(1)}, f32[1024]{0:T(1024)}, u32[]{:S(2)}) copy-start(f32[1024]{0:T(1024)} %copy-done.61) | copy-start | bytes 12292
  258.4 15.2 %copy-start.64 = (f32[2,256]{1,0:T(2,128)S(1)}, f32[2,256]{1,0:T(2,128)}, u32[]{:S(2)}) copy-start(f32[2,256]{1,0:T(2,128)} %copy-done.63) | copy-start | bytes 6148
  258.4 17.8 %copy-start.70 = (f32[2,256]{1,0:T(2,128)S(1)}, f32[2,256]{1,0:T(2,128)}, u32[]{:S(2)}) copy-start(f32[2,256]{1,0:T(2,128)} %copy-done.69) | copy-start | bytes 6148
  258.4 17.8 %copy-start.68 = (f32[2,256]{1,0:T(2,128)S(1)}, f32[2,256]{1,0:T(2,128)}, u32[]{:S(2)}) copy-start(f32[2,256]{1,0:T(2,128)} %copy-done.67) | copy-start | bytes 6148
  262.6 16.6 %copy-start.14 = (bf16[2,256,1024]{2,1,0:T(8,128)(2,1)S(1)}, bf16[2,256,1024]{2,1,0:T(8,128)(2,1)}, u32[]{:S(2)}) copy-start(bf16[2,256,1024]{2,1,0:T(8,128)(2,1)} %reduce-scatter.14.cloned.1.call-done) | copy-start | bytes 3145732
  262.6 31.4 %all-gather.14.cloned.1.call-start = ((), (), s32[]{:S(2)}) async-start(), calls=%async_computation.16 | async-start | bytes 3145728 | tf_op jit(solution)/shard_map/all_gather | solution.py:258
  282.1 99.1 %reduce-scatter.20.cloned.1.call-start = ((), (), s32[]{:S(2)}) async-start(), calls=%async_computation.18 | async-start | bytes 1179648 | tf_op jit(solution)/shard_map/reduce_scatter | solution.py:248
  288.3 13.0 %copy-start.6 = (bf16[2,512,8,64]{1,3,2,0:T(8,128)(2,1)S(1)}, bf16[2,512,8,64]{1,3,2,0:T(8,128)(2,1)}, u32[]{:S(2)}) copy-start(bf16[2,512,8,64]{1,3,2,0:T(8,128)(2,1)} %copy-done.5) | copy-start | bytes 3145732
  288.4 94.7 %reduce-scatter.18.cloned.1.call-start = ((), (), s32[]{:S(2)}) async-start(), calls=%async_computation.17 | async-start | bytes 3145728 | tf_op jit(solution)/shard_map/reduce_scatter | solution.py:274
  341.4 911.3 %all-reduce.4.cloned.1.call-start = ((), (), s32[]{:S(2)}) async-start(), calls=%async_computation.19 | async-start | bytes 65011712 | tf_op jit(solution)/shard_map/psum | solution.py:283
  377.2 60.6 %copy-start.22 = (f32[2,256,1024]{2,1,0:T(8,128)S(1)}, f32[2,256,1024]{2,1,0:T(8,128)}, u32[]{:S(2)}) copy-start(f32[2,256,1024]{2,1,0:T(8,128)} %get-tuple-element.505) | copy-start | bytes 6291460
  383.1 54.7 %copy-start.20 = (bf16[2,256,1024]{2,1,0:T(8,128)(2,1)S(1)}, bf16[2,256,1024]{2,1,0:T(8,128)(2,1)}, u32[]{:S(2)}) copy-start(bf16[2,256,1024]{2,1,0:T(8,128)(2,1)} %reduce-scatter.18.cloned.1.call-done) | copy-start | bytes 3145732
  (112 other events, 446.8 us)
Sparse Core Ops, SparseCore 0:
  47.4 14.7 reduce-scatter.7
  68.5 11.8 all-gather.5
  103.6 13.1 reduce-scatter.9
  121.6 11.8 all-gather.7
  134.9 11.7 all-gather.9
  187.7 10.7 reduce-scatter.13
  201.4 10.8 reduce-scatter.11
  221.9 11.7 all-gather.11
  262.7 10.7 reduce-scatter.15
  282.2 11.7 all-gather.13
  296.4 9.3 reduce-scatter.19
  341.5 10.8 reduce-scatter.17
  376.7 875.8 all-reduce.3
where the time goes:
time: 1300 us; the launch traced here: 1290 us
  waiting for transfers between devices  890 us (68%)
  matrix products  160 us (12%)
  other arithmetic  89.7 us (7%)
  local copies, waits for them, and re-layouts  82.6 us (6%)
  blocking collectives  48.5 us (4%)
  between operations  15.5 us (1%)
    psum x1, waiting for transfers between devices, per_device(): lax.psum((d_w_joined, d_w_out, d_c_query, d_c_joined, d_c_out, d_w_up, d_...  811 us
    psum x1, blocking collectives, per_device(): lax.psum((d_gain_one, d_bias_one, d_gain_two, d_bias_two, d_gain_three, d...  46.2 us
    dot_general x7, matrix products, project_back(): jnp.einsum('bfe,de->bfd', gradients, weight, preferred_element_type=jnp.f...  41.1 us
    dot_general x7, matrix products, project(): jnp.einsum('bfd,de->bfe', inputs, weight, preferred_element_type=jnp.floa...  40.8 us
    unnamed x163, local copies, waits for them, and re-layouts  36.9 us
    dot_general x7, matrix products, weight_grad(): jnp.einsum('bfd,bfe->de', inputs, gradients, preferred_element_type=jnp.f...  34.8 us
  transfers between devices with their start and end apart: 13, of which 10 were waited for; matrix products, arithmetic and copies ran while one was open for 12% of the time, Pallas kernels for 0%

commit v1 on v0

--- a/solution.py
+++ b/solution.py
@@ -84,6 +84,83 @@
         grad_keys.astype(jnp.bfloat16),
         grad_values.astype(jnp.bfloat16),
     )
+
+
+SWAP = [(0, 1), (1, 0)]
+
+
+def swap_cores(values):
+    return lax.ppermute(values, "mp", SWAP)
+
+
+def sum_scatter(partial):
+    rank = lax.axis_index("mp")
+    half = partial.shape[1] // 2
+    other = lax.dynamic_slice_in_dim(partial, (1 - rank) * half, half, 1)
+    own = lax.dynamic_slice_in_dim(partial, rank * half, half, 1)
+    received = swap_cores(other.astype(jnp.bfloat16))
+    return own.astype(jnp.float32) + received.astype(jnp.float32)
+
+
+def gather_halves(own):
+    first = lax.axis_index("mp") == 0
+    received = swap_cores(own)
+    return jnp.concatenate(
+        [jnp.where(first, own, received), jnp.where(first, received, own)], 1
+    )
+
+
+def bit_orders():
+    bits = lax.axis_size("dp").bit_length() - 1
+    along_x = (bits - 2) // 2
+    x_bits = list(range(along_x))
+    y_bits = list(range(along_x, bits - 2))
+    z_bits = [bits - 2, bits - 1]
+    return (x_bits + y_bits + z_bits, y_bits + x_bits + z_bits, z_bits + x_bits + y_bits)
+
+
+def exchange(values, bit):
+    pairs = [(d, d ^ (1 << bit)) for d in range(lax.axis_size("dp"))]
+    return lax.ppermute(values, "dp", pairs)
+
+
+def my_bit(bit):
+    return (lax.axis_index("dp") >> bit) & 1
+
+
+def sum_over_items(values, order):
+    kept = values.astype(jnp.bfloat16)
+    for bit in order:
+        half = kept.shape[0] // 2
+        side = my_bit(bit)
+        send = lax.dynamic_slice_in_dim(kept, (1 - side) * half, half, 0)
+        keep = lax.dynamic_slice_in_dim(kept, side * half, half, 0)
+        received = exchange(send, bit)
+        kept = (keep.astype(jnp.float32) + received.astype(jnp.float32)).astype(jnp.bfloat16)
+    for bit in reversed(order):
+        received = exchange(kept, bit)
+        lower = my_bit(bit) == 0
+        kept = jnp.concatenate(
+            [jnp.where(lower, kept, received), jnp.where(lower, received, kept)], 0
+        )
+    return kept.astype(jnp.float32)
+
+
+def sum_small(values):
+    total = values + swap_cores(values)
+    for bit in bit_orders()[0]:
+        total = total + exchange(total, bit)
+    return total
+
+
+def fold_rows(values):
+    half = values.shape[0] // 2
+    return jnp.concatenate([values[:half], values[half:]], 1)
+
+
+def unfold_rows(values):
+    half = values.shape[1] // 2
+    return jnp.concatenate([values[:, :half], values[:, half:]], 0)
 
 
 def per_device(
@@ -160,15 +237,12 @@
     value_self = to_heads(joined_rows[..., 2 * local_width :], frames)
     self_saved = lax.map(self_forward, (query_self, key_self, value_self, frame_valid))
     mix_self = self_saved[0].reshape(items, frames, local_width)
-    attn_out = lax.psum_scatter(project(mix_self, w_out), "mp", scatter_dimension=1, tiled=True)
+    attn_out = sum_scatter(project(mix_self, w_out))
     first_row = rank * shard_rows
     own_rows = lax.dynamic_slice_in_dim(tokens_full, first_row, shard_rows, 1)
     hidden_one = own_rows + attn_out
     normed_two_own = layer_norm(hidden_one, gain_two, bias_two).astype(jnp.bfloat16)
-    normed_two, text_full = (
-        lax.all_gather(normed_two_own, "mp", axis=1, tiled=True),
-        lax.all_gather(text_states, "mp", axis=1, tiled=True),
-    )
+    normed_two, text_full = gather_halves(normed_two_own), gather_halves(text_states)
     query_cross = to_heads(project(normed_two, c_query).astype(jnp.bfloat16), frames)
     c_joined = jnp.concatenate([c_key, c_value], 1)
     text_joined = project(text_full, c_joined).astype(jnp.bfloat16)
@@ -176,19 +250,14 @@
     value_cross = to_heads(text_joined[..., local_width:], text_rows)
     cross_saved = lax.map(cross_forward, (query_cross, key_cross, value_cross, text_len))
     mix_cross = cross_saved[0].reshape(items, frames, local_width)
-    cross_out = lax.psum_scatter(project(mix_cross, c_out), "mp", scatter_dimension=1, tiled=True)
+    cross_out = sum_scatter(project(mix_cross, c_out))
     hidden_two = hidden_one + cross_out
-    normed_three = lax.all_gather(
-        layer_norm(hidden_two, gain_three, bias_three).astype(jnp.bfloat16),
-        "mp",
-        axis=1,
-        tiled=True,
+    normed_three = gather_halves(
+        layer_norm(hidden_two, gain_three, bias_three).astype(jnp.bfloat16)
     )
     up_rows = project(normed_three, w_up)
     activated = jax.nn.gelu(up_rows, approximate=False).astype(jnp.bfloat16)
-    ff_out = lax.psum_scatter(
-        project(activated, w_down).astype(jnp.bfloat16), "mp", scatter_dimension=1, tiled=True
-    ).astype(jnp.float32)
+    ff_out = sum_scatter(project(activated, w_down))
     result_full = hidden_two + ff_out
     result = result_full.astype(jnp.bfloat16)
     row_valid = ((first_row + jnp.arange(shard_rows))[None, :] < frame_valid[:, None]).astype(
@@ -207,21 +276,17 @@
             jnp.sum(row_valid),
         ]
     )
-    stat_totals = lax.psum(stat_terms, ("dp", "mp"))
-    stat_extra = jnp.zeros((0,), jnp.float32)
-    grad_ff = lax.all_gather(grad_out, "mp", axis=1, tiled=True)
+    grad_ff = gather_halves(grad_out)
     grad_act = project_back(grad_ff, w_down)
     d_w_down = weight_grad(activated, grad_ff)
     gelu_pull = jax.vjp(partial(jax.nn.gelu, approximate=False), up_rows)[1]
     grad_up = gelu_pull(grad_act)[0].astype(jnp.bfloat16)
     d_w_up = weight_grad(normed_three, grad_up)
-    grad_n3 = lax.psum_scatter(
-        project_back(grad_up, w_up).astype(jnp.bfloat16), "mp", scatter_dimension=1, tiled=True
-    ).astype(jnp.float32)
+    grad_n3 = sum_scatter(project_back(grad_up, w_up))
     norm_pull = jax.vjp(layer_norm, hidden_two, gain_three, bias_three)[1]
     grad_h2_norm, d_gain_three, d_bias_three = norm_pull(grad_n3)
     grad_h2 = grad_out.astype(jnp.float32) + grad_h2_norm
-    grad_cross = lax.all_gather(grad_h2.astype(jnp.bfloat16), "mp", axis=1, tiled=True)
+    grad_cross = gather_halves(grad_h2.astype(jnp.bfloat16))
     d_c_out = weight_grad(mix_cross, grad_cross)
     grad_mix_cross = to_heads(project_back(grad_cross, c_out).astype(jnp.bfloat16), frames)
     cross_kept = cross_saved[1]
@@ -238,24 +303,12 @@
     )
     d_c_query = weight_grad(normed_two, grad_q_cross)
     d_c_joined = weight_grad(text_full, grad_kv_cross)
-    grad_n2, d_text_part = (
-        lax.psum_scatter(
-            project_back(grad_q_cross, c_query).astype(jnp.bfloat16),
-            "mp",
-            scatter_dimension=1,
-            tiled=True,
-        ).astype(jnp.float32),
-        lax.psum_scatter(
-            project_back(grad_kv_cross, c_joined).astype(jnp.bfloat16),
-            "mp",
-            scatter_dimension=1,
-            tiled=True,
-        ).astype(jnp.float32),
-    )
+    grad_n2 = sum_scatter(project_back(grad_q_cross, c_query))
+    d_text_part = sum_scatter(project_back(grad_kv_cross, c_joined))
     norm_pull = jax.vjp(layer_norm, hidden_one, gain_two, bias_two)[1]
     grad_h1_norm, d_gain_two, d_bias_two = norm_pull(grad_n2)
     grad_h1 = grad_h2 + grad_h1_norm
-    grad_attn = lax.all_gather(grad_h1.astype(jnp.bfloat16), "mp", axis=1, tiled=True)
+    grad_attn = gather_halves(grad_h1.astype(jnp.bfloat16))
     d_w_out = weight_grad(mix_self, grad_attn)
     grad_mix_self = to_heads(project_back(grad_attn, w_out).astype(jnp.bfloat16), frames)
     self_kept = self_saved[1]
@@ -271,23 +324,51 @@
         -1,
     )
     d_w_joined = weight_grad(normed_one, grad_joined)
-    grad_n1 = lax.psum_scatter(
-        project_back(grad_joined, w_joined).astype(jnp.bfloat16),
-        "mp",
-        scatter_dimension=1,
-        tiled=True,
-    ).astype(jnp.float32)
+    grad_n1 = sum_scatter(project_back(grad_joined, w_joined))
     norm_pull = jax.vjp(layer_norm, own_rows, gain_one, bias_one)[1]
     grad_x_norm, d_gain_one, d_bias_one = norm_pull(grad_n1)
     d_tokens = grad_h1 + grad_x_norm
-    summed = lax.psum((d_w_joined, d_w_out, d_c_query, d_c_joined, d_c_out, d_w_up, d_w_down), "dp")
-    small = lax.psum(
-        (d_gain_one, d_bias_one, d_gain_two, d_bias_two, d_gain_three, d_bias_three, stat_extra),
-        ("dp", "mp"),
-    )
+    order_x, order_y, order_z = bit_orders()
+    cut_down, cut_up = width * 3 // 4, w_up.shape[1] * 3 // 4
+    down_sum = sum_over_items(d_w_down[:, :cut_down], order_x)
+    up_sum = sum_over_items(d_w_up[:, :cut_up], order_y)
+    rest_sum = sum_over_items(
+        jnp.concatenate([d_w_up[:, cut_up:], fold_rows(d_w_down[:, cut_down:])], 0), order_z
+    )
+    rest_rows = d_w_up.shape[0]
+    d_w_up_sum = jnp.concatenate([up_sum, rest_sum[:rest_rows]], 1)
+    d_w_down_sum = jnp.concatenate([down_sum, unfold_rows(rest_sum[rest_rows:])], 1)
+    key_value_sum = sum_over_items(d_c_joined, order_x)
+    query_out_sum = sum_over_items(
+        jnp.concatenate([d_c_query, jnp.concatenate([d_c_out[:, : width // 2], d_c_out[:, width // 2 :]], 0)], 1), order_y
+    )
+    d_c_query_sum = query_out_sum[:, :local_width]
+    folded = query_out_sum[:, local_width:]
+    d_c_out_sum = jnp.concatenate([folded[:local_width], folded[local_width:]], 1)
+    d_w_out_sum = sum_over_items(d_w_out, order_z)
+    joined_cut = d_w_joined.shape[1] // 2
+    joined_sum = jnp.concatenate(
+        [
+            sum_over_items(d_w_joined[:, :joined_cut], order_x),
+            sum_over_items(d_w_joined[:, joined_cut:], order_y),
+        ],
+        1,
+    )
+    small_rows = jnp.stack(
+        [
+            d_gain_one,
+            d_bias_one,
+            d_gain_two,
+            d_bias_two,
+            d_gain_three,
+            d_bias_three,
+            jnp.pad(stat_terms, (0, width - 5)),
+            jnp.zeros((width,), jnp.float32),
+        ]
+    )
+    small = sum_small(small_rows)
+    stat_totals = small[6]
     rms_stats = jnp.sqrt(stat_totals[:4] / (stat_totals[4] * width))
-    joined_sum = summed[0]
-    key_value_sum = summed[3]
     return (
         result,
         d_tokens,
@@ -301,13 +382,13 @@
         joined_sum[:, :local_width],
         joined_sum[:, local_width : 2 * local_width],
         joined_sum[:, 2 * local_width :],
-        summed[1],
-        summed[2],
+        d_w_out_sum,
+        d_c_query_sum,
         key_value_sum[:, :local_width],
         key_value_sum[:, local_width:],
-        summed[4],
-        summed[5],
-        summed[6],
+        d_c_out_sum,
+        d_w_up_sum,
+        d_w_down_sum,
         rms_stats,
     )
 

time: 1300 us -> 732 us (0.56)
  waiting for transfers between devices: 890 us -> 271 us
  starting transfers between devices: 1.87 us -> 87 us
  other arithmetic: 89.7 us -> 157 us
  blocking collectives: 48.5 us -> 0 us
  matrix products: 160 us -> 131 us
    psum x1 -> x0, waiting for transfers between devices: 811 us -> none  [per_device(): lax.psum((d_w_joined, d_w_out, d_c_query, d_c_joined, d_c_out, d_w_up, d_...]
    ppermute x0 -> x82, waiting for transfers between devices: none -> 271 us  [the longest x68 266 us: exchange(): return lax.ppermute(values, 'dp', pairs)]
    ppermute x0 -> x82, starting transfers between devices: none -> 87 us  [the longest x68 83.7 us: exchange(): return lax.ppermute(values, 'dp', pairs)]
    reduce_scatter x7 -> x0, waiting for transfers between devices: 49.2 us -> none  [the longest x1 13.8 us: per_device(): lax.psum_scatter(project(activated, w_down).astype(jnp.bfloat16), 'mp', s...]
    psum x1 -> x0, blocking collectives: 46.2 us -> none  [per_device(): lax.psum((d_gain_one, d_bias_one, d_gain_two, d_bias_two, d_gain_three, d...]
    select_n x0 -> x37, other arithmetic: none -> 30.2 us  [the longest x32 20.5 us: sum_over_items(): jnp.where(lower, kept, received)]
    all_gather x5 -> x0, waiting for transfers between devices: 28.6 us -> none  [the longest x1 11.8 us: per_device(): lax.all_gather(grad_h2.astype(jnp.bfloat16), 'mp', axis=1, tiled=True)]
    unnamed x163 -> x290, local copies, waits for them, and re-layouts: 36.9 us -> 13.1 us
  transfers between devices with their start and end apart: 13 -> 82, of which waited for: 10 -> 37; matrix products, arithmetic and copies ran while one was open for 12% -> 30% of each run, Pallas kernels for 0% -> 0%
where the time goes in v1:
time: 732 us; the launch traced here: 723 us
  waiting for transfers between devices  271 us (37%)
  other arithmetic  157 us (21%)
  matrix products  131 us (18%)
  starting transfers between devices  87 us (12%)
  local copies, waits for them, and re-layouts  71.9 us (10%)
    ppermute x68, waiting for transfers between devices, exchange(): return lax.ppermute(values, 'dp', pairs)  266 us
    ppermute x68, starting transfers between devices, exchange(): return lax.ppermute(values, 'dp', pairs)  83.7 us
    dot_general x7, matrix products, project_back(): jnp.einsum('bfe,de->bfd', gradients, weight, preferred_element_type=jnp.f...  35.6 us
    dot_general x7, matrix products, project(): jnp.einsum('bfd,de->bfe', inputs, weight, preferred_element_type=jnp.floa...  30.6 us
    dot_general x7, matrix products, weight_grad(): jnp.einsum('bfd,bfe->de', inputs, gradients, preferred_element_type=jnp.f...  23.2 us
    select_n x32, other arithmetic, sum_over_items(): jnp.where(lower, kept, received)  20.5 us
    convert_element_type x1, other arithmetic, per_device(): activated = jax.nn.gelu(up_rows, approximate=False).astype(jnp.bfloat16)  19.9 us
  transfers between devices with their start and end apart: 82, of which 37 were waited for; matrix products, arithmetic and copies ran while one was open for 30% of the time, Pallas kernels for 0%

profile of v1, /device:TPU:0, one launch (start us, length us, event | category | flops | bytes accessed | tf_op | source)
XLA Modules:
  0.0 723.1 jit_solution(10223637381061514672)
XLA Ops:
  16.0 16.4 %while.56 = (s32[]{:T(128)}, bf16[2,512,8,64]{1,3,2,0:T(8,128)(2,1)}, f32[2,8,512,1]{2,1,3,0:T(8,128)S(1)}, bf16[2,512,8,64]{1,3,2,0:T(8,128)(2,1)}, s32[2]{0:T(...) while((s32[]{:T(128)}, ...), condition=%wide.region_5.6_spmd.clone, body=%wide.region_2.5_spmd.clone.sunk | while | flops 562819584 | bytes 41028804 | solution.py:238
  67.2 14.1 %while.57 = (s32[]{:T(128)}, bf16[2,512,8,64]{1,3,2,0:T(8,128)(2,1)}, f32[2,8,512,1]{2,1,3,0:T(8,128)S(1)}, bf16[2,256,8,64]{1,3,2,0:T(8,128)(2,1)}, s32[2]{0:T(...) while((s32[]{:T(128)}, ...), condition=%wide.region_11.12_spmd.clone, body=%wide.region_8.11_spmd.clone.sunk | while | flops 281276672 | bytes 24776132 | solution.py:251
  100.9 19.9 %multiply_convert_fusion.2 = (bf16[2,512,2048]{2,1,0:T(8,128)(2,1)S(1)}, f32[2,512,2048]{2,1,0:T(8,128)}) fusion(f32[2,512,2048]{2,1,0:T(8,128)S(1)} %get-tuple-element.630, u8[512,2048]{1,0:T(8,128)(4,1)S(1)} %get-tuple-element.419, u8[512,2048]{1,0:T(8,128)(4,1)S(1)} %get-tuple-element.418), kind=kLoop, calls=%fused_computation.150 | loop fusion | flops 146800640 | bytes 23068672 | tf_op jit(solution)/shard_map/convert_element_type | solution.py:259
  132.2 12.1 %add_convert_fusion = bf16[2,512,2048]{2,1,0:T(8,128)(2,1)} fusion(f32[2,512,2048]{2,1,0:T(8,128)} %get-tuple-element.511, f32[2,512,2048]{2,1,0:T(8,128)S(1)} %get-tuple-element.630, bf16[2048,1024]{1,0:T(8,128)(2,1)} %param.48, bf16[2,256,1024]{2,1,0:T(8,128)(2,1)} %get-tuple-element.555, bf16[2,256,1024]{2,1,0:T(8,128)(2,1)} %get-tuple-element.554), kind=kOutput, calls=%fused_computation.149 | convolution fusion | flops 4328521728 | bytes 27262976 | tf_op jit(solution)/shard_map/bfe,de->bfd/dot_general | solution.py:28
  144.5 7.4 %bitcast_convert_fusion.1 = bf16[1024,2048]{1,0:T(8,128)(2,1)S(1)} fusion(bf16[2,512,2048]{2,1,0:T(8,128)(2,1)} %add_convert_fusion, bf16[2,256,1024]{2,1,0:T(8,128)(2,1)} %copy-done.110, bf16[2,256,1024]{2,1,0:T(8,128)(2,1)} %copy-done.109), kind=kOutput, calls=%fused_computation.148 | convolution fusion | flops 4301258752 | bytes 10485760 | tf_op jit(solution)/shard_map/bfd,bfe->de/dot_general | solution.py:32
  155.3 7.6 %fusion.141 = f32[2,512,1024]{2,1,0:T(8,128)S(1)} fusion(bf16[2,512,2048]{2,1,0:T(8,128)(2,1)} %add_convert_fusion, bf16[1024,2048]{1,0:T(8,128)(2,1)} %param.47), kind=kOutput, calls=%fused_computation.167 | convolution fusion | flops 4294967296 | bytes 12582912 | tf_op jit(solution)/shard_map/bfe,de->bfd/dot_general | solution.py:28
  194.6 10.3 %collective-permute-done.67 = bf16[512,512]{1,0:T(8,128)(2,1)S(1)} collective-permute-done((bf16[512,512]{1,0:T(8,128)(2,1)S(1)}, bf16[512,512]{1,0:T(8,128)(2,1)S(1)}, u32[]{:S(2)}, u32[]{:S(2)}) %collective-permute-start.67) | collective-permute-done | bytes 524320 | tf_op jit(solution)/shard_map/ppermute | solution.py:124
  229.5 16.6 %while.58 = (s32[]{:T(128)}, bf16[2,512,8,64]{1,3,2,0:T(8,128)(2,1)}, bf16[2,256,8,64]{1,3,2,0:T(8,128)(2,1)}, bf16[2,256,8,64]{1,3,2,0:T(8,128)(2,1)}, bf16[2,2...) while((s32[]{:T(128)}, ...), condition=%wide.region_18.19_spmd.clone, body=%wide.region_16.18_spmd.clone.sunk | while | flops 687730944 | bytes 56482636 | solution.py:293
  265.2 20.0 %collective-permute-done.71 = bf16[256,512]{1,0:T(8,128)(2,1)S(1)} collective-permute-done((bf16[256,512]{1,0:T(8,128)(2,1)S(1)}, bf16[256,512]{1,0:T(8,128)(2,1)S(1)}, u32[]{:S(2)}, u32[]{:S(2)}) %collective-permute-start.71) | collective-permute-done | bytes 262176 | tf_op jit(solution)/shard_map/ppermute | solution.py:124
  290.9 12.1 %collective-permute-done.60 = bf16[128,1536]{1,0:T(8,128)(2,1)S(1)} collective-permute-done((bf16[128,1536]{1,0:T(8,128)(2,1)S(1)}, bf16[128,1536]{1,0:T(8,128)(2,1)S(1)}, u32[]{:S(2)}, u32[]{:S(2)}) %collective-permute-start.60) | collective-permute-done | bytes 393248 | tf_op jit(solution)/shard_map/ppermute | solution.py:124
  303.1 12.1 %collective-permute-done.76 = bf16[256,768]{1,0:T(8,128)(2,1)S(1)} collective-permute-done((bf16[256,768]{1,0:T(8,128)(2,1)S(1)}, bf16[256,768]{1,0:T(8,128)(2,1)S(1)}, u32[]{:S(2)}, u32[]{:S(2)}) %collective-permute-start.76) | collective-permute-done | bytes 393248 | tf_op jit(solution)/shard_map/ppermute | solution.py:124
  321.2 11.2 %collective-permute-done.61 = bf16[64,1536]{1,0:T(8,128)(2,1)S(1)} collective-permute-done((bf16[64,1536]{1,0:T(8,128)(2,1)S(1)}, bf16[64,1536]{1,0:T(8,128)(2,1)S(1)}, u32[]{:S(2)}, u32[]{:S(2)}) %collective-permute-start.61) | collective-permute-done | bytes 196640 | tf_op jit(solution)/shard_map/ppermute | solution.py:124
  344.2 15.7 %collective-permute-done.62 = bf16[64,1536]{1,0:T(8,128)(2,1)S(1)} collective-permute-done((bf16[64,1536]{1,0:T(8,128)(2,1)S(1)}, bf16[64,1536]{1,0:T(8,128)(2,1)S(1)}, u32[]{:S(2)}, u32[]{:S(2)}) %collective-permute-start.62) | collective-permute-done | bytes 196640 | tf_op jit(solution)/shard_map/ppermute | solution.py:124
  367.0 11.1 %collective-permute-done.52 = bf16[96,1024]{1,0:T(8,128)(2,1)S(1)} collective-permute-done((bf16[96,1024]{1,0:T(8,128)(2,1)S(1)}, bf16[96,1024]{1,0:T(8,128)(2,1)S(1)}, u32[]{:S(2)}, u32[]{:S(2)}) %collective-permute-start.52) | collective-permute-done | bytes 196640 | tf_op jit(solution)/shard_map/ppermute | solution.py:124
  417.8 12.8 %collective-permute-done.45 = bf16[64,1024]{0,1:T(8,128)(2,1)S(1)} collective-permute-done((bf16[64,1024]{0,1:T(8,128)(2,1)S(1)}, bf16[64,1024]{0,1:T(8,128)(2,1)S(1)}, u32[]{:S(2)}, u32[]{:S(2)}) %collective-permute-start.45) | collective-permute-done | bytes 131104 | tf_op jit(solution)/shard_map/ppermute | solution.py:124
  438.1 29.0 %while.59 = (s32[]{:T(128)}, bf16[2,512,8,64]{1,3,2,0:T(8,128)(2,1)}, bf16[2,512,8,64]{1,3,2,0:T(8,128)(2,1)}, bf16[2,512,8,64]{1,3,2,0:T(8,128)(2,1)}, bf16[2,5...) while((s32[]{:T(128)}, ...), condition=%wide.region_23.24_spmd.clone, body=%wide.region_21.23_spmd.clone.sunk | while | flops 1375465984 | bytes 98818424 | solution.py:315
  494.0 7.1 collective-permute-done.34
  509.6 11.4 %collective-permute-done.35 = bf16[128,1024]{1,0:T(8,128)(2,1)S(1)} collective-permute-done((bf16[128,1024]{1,0:T(8,128)(2,1)S(1)}, bf16[128,1024]{1,0:T(8,128)(2,1)S(1)}, u32[]{:S(2)}, u32[]{:S(2)}) %collective-permute-start.35) | collective-permute-done | bytes 262176 | tf_op jit(solution)/shard_map/ppermute | solution.py:124
  526.0 11.5 %collective-permute-done.48 = bf16[256,1024]{0,1:T(8,128)(2,1)S(1)} collective-permute-done((bf16[256,1024]{0,1:T(8,128)(2,1)S(1)}, bf16[256,1024]{0,1:T(8,128)(2,1)S(1)}, u32[]{:S(2)}, u32[]{:S(2)}) %collective-permute-start.48) | collective-permute-done | bytes 524320 | tf_op jit(solution)/shard_map/ppermute | solution.py:124
  542.4 38.7 %collective-permute-done.36 = bf16[64,1024]{1,0:T(8,128)(2,1)S(1)} collective-permute-done((bf16[64,1024]{1,0:T(8,128)(2,1)S(1)}, bf16[64,1024]{1,0:T(8,128)(2,1)S(1)}, u32[]{:S(2)}, u32[]{:S(2)}) %collective-permute-start.36) | collective-permute-done | bytes 131104 | tf_op jit(solution)/shard_map/ppermute | solution.py:124
  602.6 8.6 %collective-permute-done.15 = f32[8,1024]{1,0:T(8,128)S(1)} collective-permute-done((f32[8,1024]{1,0:T(8,128)S(1)}, f32[8,1024]{1,0:T(8,128)S(1)}, u32[]{:S(2)}, u32[]{:S(2)}) %collective-permute-start.15) | collective-permute-done | bytes 32800 | tf_op jit(solution)/shard_map/ppermute | solution.py:124
  635.4 9.2 %collective-permute-done.40 = bf16[128,1024]{1,0:T(8,128)(2,1)S(1)} collective-permute-done((bf16[128,1024]{1,0:T(8,128)(2,1)S(1)}, bf16[128,1024]{1,0:T(8,128)(2,1)S(1)}, u32[]{:S(2)}, u32[]{:S(2)}) %collective-permute-start.40) | collective-permute-done | bytes 262176 | tf_op jit(solution)/shard_map/ppermute | solution.py:124
  650.6 7.8 %collective-permute-done.30 = bf16[64,768]{1,0:T(8,128)(2,1)S(1)} collective-permute-done((bf16[64,768]{1,0:T(8,128)(2,1)S(1)}, bf16[64,768]{1,0:T(8,128)(2,1)S(1)}, u32[]{:S(2)}, u32[]{:S(2)}) %collective-permute-start.30) | collective-permute-done | bytes 98336 | tf_op jit(solution)/shard_map/ppermute | solution.py:124
  681.1 7.5 %maximum_maximum_fusion = f32[2048,1024]{1,0:T(8,128)} fusion(f32[1024,256]{1,0:T(8,128)S(1)} %copy-done.52, f32[1024,256]{1,0:T(8,128)S(1)} %copy-done.51, f32[2048,768]{1,0:T(8,128)} %maximum_convert_fusion.1), kind=kLoop, calls=%fused_computation.146 | loop fusion | flops 4194304 | bytes 16777216 | tf_op jit(solution)/shard_map/concatenate | solution.py:340
  (837 shorter events, 462.9 us)
Async XLA Ops:
  167.7 39.8 %collective-permute-start.58 = (bf16[512,1536]{1,0:T(8,128)(2,1)}, bf16[512,1536]{1,0:T(8,128)(2,1)}, u32[]{:S(2)}, u32[]{:S(2)}) collective-permute-start(bf16[512,1536]{1,0:T(8,128)(2,1)} %constant_dynamic-slice_fusion.11), channel_id=1, source_target_pairs={{0,4},{2,6},{4,0},{6,2},{8,12},{10,14},{12,8},{14,10},{16,20},{18,... | collective-permute-start | bytes 4718600 | tf_op jit(solution)/shard_map/ppermute | solution.py:124
  170.5 41.2 %collective-permute-start.74 = (bf16[1024,768]{1,0:T(8,128)(2,1)}, bf16[1024,768]{1,0:T(8,128)(2,1)}, u32[]{:S(2)}, u32[]{:S(2)}) collective-permute-start(bf16[1024,768]{1,0:T(8,128)(2,1)} %constant_dynamic-slice_fusion.3), channel_id=1, source_target_pairs={{0,2},{2,0},{4,6},{6,4},{8,10},{10,8},{12,14},{14,12},{16,18},{18,... | collective-permute-start | bytes 4718600 | tf_op jit(solution)/shard_map/ppermute | solution.py:124
  210.9 49.4 %collective-permute-start.59 = (bf16[256,1536]{1,0:T(8,128)(2,1)}, bf16[256,1536]{1,0:T(8,128)(2,1)}, u32[]{:S(2)}, u32[]{:S(2)}) collective-permute-start(bf16[256,1536]{1,0:T(8,128)(2,1)} %constant_dynamic-slice_fusion.10), channel_id=1, source_target_pairs={{0,2},{2,0},{4,6},{6,4},{8,10},{10,8},{12,14},{14,12},{16,18},{18,... | collective-permute-start | bytes 2359304 | tf_op jit(solution)/shard_map/ppermute | solution.py:124
  216.7 46.3 %collective-permute-start.75 = (bf16[512,768]{1,0:T(8,128)(2,1)}, bf16[512,768]{1,0:T(8,128)(2,1)}, u32[]{:S(2)}, u32[]{:S(2)}) collective-permute-start(bf16[512,768]{1,0:T(8,128)(2,1)} %constant_dynamic-slice_fusion.2), channel_id=1, source_target_pairs={{0,4},{2,6},{4,0},{6,2},{8,12},{10,14},{12,8},{14,10},{16,20},{18,... | collective-permute-start | bytes 2359304 | tf_op jit(solution)/shard_map/ppermute | solution.py:124
  252.6 82.0 %collective-permute-start.9 = (bf16[2,256,1024]{2,1,0:T(8,128)(2,1)}, bf16[2,256,1024]{2,1,0:T(8,128)(2,1)}, u32[]{:S(2)}, u32[]{:S(2)}) collective-permute-start(bf16[2,256,1024]{2,1,0:T(8,128)(2,1)} %dynamic-slice_convert_fusion.1), channel_id=1, source_target_pairs={{0,1},{1,0},{2,3},{3,2},{4,5},{5,4},{6,7},{7,6},{8,9},{9,8},{10,11... | collective-permute-start | bytes 3145736 | tf_op jit(solution)/shard_map/ppermute | solution.py:93
  259.0 84.7 %collective-permute-start.42 = (bf16[512,1024]{0,1:T(8,128)(2,1)S(1)}, bf16[512,1024]{0,1:T(8,128)(2,1)S(1)}, u32[]{:S(2)}, u32[]{:S(2)}) collective-permute-start(bf16[512,1024]{0,1:T(8,128)(2,1)S(1)} %constant_dynamic-slice_fusion.19), channel_id=1, source_target_pairs={{0,4},{2,6},{4,0},{6,2},{8,12},{10,14},{12,8},{14,10},{16,20},{18,... | collective-permute-start | bytes 3145736 | tf_op jit(solution)/shard_map/ppermute | solution.py:124
  260.3 57.9 %collective-permute-start.50 = (bf16[384,1024]{1,0:T(8,128)(2,1)S(1)}, bf16[384,1024]{1,0:T(8,128)(2,1)S(1)}, u32[]{:S(2)}, u32[]{:S(2)}) collective-permute-start(bf16[384,1024]{1,0:T(8,128)(2,1)S(1)} %constant_dynamic-slice_fusion.15), channel_id=1, source_target_pairs={{0,2},{2,0},{4,6},{6,4},{8,10},{10,8},{12,14},{14,12},{16,18},{18,... | collective-permute-start | bytes 2359304 | tf_op jit(solution)/shard_map/ppermute | solution.py:124
  318.8 42.9 %collective-permute-start.51 = (bf16[192,1024]{1,0:T(8,128)(2,1)S(1)}, bf16[192,1024]{1,0:T(8,128)(2,1)S(1)}, u32[]{:S(2)}, u32[]{:S(2)}) collective-permute-start(bf16[192,1024]{1,0:T(8,128)(2,1)S(1)} %constant_dynamic-slice_fusion.14), channel_id=1, source_target_pairs={{0,4},{2,6},{4,0},{6,2},{8,12},{10,14},{12,8},{14,10},{16,20},{18,... | collective-permute-start | bytes 1179656 | tf_op jit(solution)/shard_map/ppermute | solution.py:124
  332.4 77.2 %collective-permute-start.73 = (bf16[1024,512]{1,0:T(8,128)(2,1)S(1)}, bf16[1024,512]{1,0:T(8,128)(2,1)S(1)}, u32[]{:S(2)}, u32[]{:S(2)}) collective-permute-start(bf16[1024,512]{1,0:T(8,128)(2,1)S(1)} %pad_maximum_fusion.25), channel_id=1, source_target_pairs={{0,8},{2,10},{4,12},{6,14},{8,0},{10,2},{12,4},{14,6},{16,24},{18,... | collective-permute-start | bytes 3145736 | tf_op jit(solution)/shard_map/ppermute | solution.py:124
  343.8 87.7 %collective-permute-start.10 = (bf16[2,256,1024]{2,1,0:T(8,128)(2,1)S(1)}, bf16[2,256,1024]{2,1,0:T(8,128)(2,1)S(1)}, u32[]{:S(2)}, u32[]{:S(2)}) collective-permute-start(bf16[2,256,1024]{2,1,0:T(8,128)(2,1)S(1)} %get-tuple-element.505), channel_id=1, source_target_pairs={{0,1},{1,0},{2,3},{3,2},{4,5},{5,4},{6,7},{7,6},{8,9},{9,8},{10,11... | collective-permute-start | bytes 3145736 | tf_op jit(solution)/shard_map/ppermute | solution.py:93
  359.9 41.2 %collective-permute-start.43 = (bf16[256,1024]{0,1:T(8,128)(2,1)S(1)}, bf16[256,1024]{0,1:T(8,128)(2,1)S(1)}, u32[]{:S(2)}, u32[]{:S(2)}) collective-permute-start(bf16[256,1024]{0,1:T(8,128)(2,1)S(1)} %constant_dynamic-slice_fusion.18), channel_id=1, source_target_pairs={{0,2},{2,0},{4,6},{6,4},{8,10},{10,8},{12,14},{14,12},{16,18},{18,... | collective-permute-start | bytes 1572872 | tf_op jit(solution)/shard_map/ppermute | solution.py:124
  389.7 96.6 %collective-permute-start.64 = (bf16[256,1536]{1,0:T(8,128)(2,1)}, bf16[256,1536]{1,0:T(8,128)(2,1)}, u32[]{:S(2)}, u32[]{:S(2)}) collective-permute-start(bf16[256,1536]{1,0:T(8,128)(2,1)} %pad_maximum_fusion.30), channel_id=1, source_target_pairs={{0,2},{2,0},{4,6},{6,4},{8,10},{10,8},{12,14},{14,12},{16,18},{18,... | collective-permute-start | bytes 2359304 | tf_op jit(solution)/shard_map/ppermute | solution.py:124
  399.4 89.8 %collective-permute-start.80 = (bf16[512,768]{1,0:T(8,128)(2,1)}, bf16[512,768]{1,0:T(8,128)(2,1)}, u32[]{:S(2)}, u32[]{:S(2)}) collective-permute-start(bf16[512,768]{1,0:T(8,128)(2,1)} %pad_maximum_fusion.31), channel_id=1, source_target_pairs={{0,4},{2,6},{4,0},{6,2},{8,12},{10,14},{12,8},{14,10},{16,20},{18,... | collective-permute-start | bytes 2359304 | tf_op jit(solution)/shard_map/ppermute | solution.py:124
  409.6 75.3 %collective-permute-start.56 = (bf16[192,1024]{1,0:T(8,128)(2,1)}, bf16[192,1024]{1,0:T(8,128)(2,1)}, u32[]{:S(2)}, u32[]{:S(2)}) collective-permute-start(bf16[192,1024]{1,0:T(8,128)(2,1)} %pad_maximum_fusion.41), channel_id=1, source_target_pairs={{0,4},{2,6},{4,0},{6,2},{8,12},{10,14},{12,8},{14,10},{16,20},{18,... | collective-permute-start | bytes 1179656 | tf_op jit(solution)/shard_map/ppermute | solution.py:124
  431.5 52.1 %collective-permute-start.46 = (bf16[64,1024]{0,1:T(8,128)(2,1)}, bf16[64,1024]{0,1:T(8,128)(2,1)}, u32[]{:S(2)}, u32[]{:S(2)}) collective-permute-start(bf16[64,1024]{0,1:T(8,128)(2,1)} %add_convert_fusion.24), channel_id=1, source_target_pairs={{0,16},{2,18},{4,20},{6,22},{8,24},{10,26},{12,28},{14,30},{16,0},... | collective-permute-start | bytes 393224 | tf_op jit(solution)/shard_map/ppermute | solution.py:124
  483.1 103.6 %collective-permute-start.11 = (bf16[2,256,1024]{2,1,0:T(8,128)(2,1)S(1)}, bf16[2,256,1024]{2,1,0:T(8,128)(2,1)S(1)}, u32[]{:S(2)}, u32[]{:S(2)}) collective-permute-start(bf16[2,256,1024]{2,1,0:T(8,128)(2,1)S(1)} %dynamic-slice_convert_fusion), channel_id=1, source_target_pairs={{0,1},{1,0},{2,3},{3,2},{4,5},{5,4},{6,7},{7,6},{8,9},{9,8},{10,11... | collective-permute-start | bytes 3145736 | tf_op jit(solution)/shard_map/ppermute | solution.py:93
  485.0 40.1 %collective-permute-start.18 = (bf16[512,768]{1,0:T(8,128)(2,1)S(1)}, bf16[512,768]{1,0:T(8,128)(2,1)S(1)}, u32[]{:S(2)}, u32[]{:S(2)}) collective-permute-start(bf16[512,768]{1,0:T(8,128)(2,1)S(1)} %constant_dynamic-slice_fusion.31), channel_id=1, source_target_pairs={{0,2},{2,0},{4,6},{6,4},{8,10},{10,8},{12,14},{14,12},{16,18},{18,... | collective-permute-start | bytes 2359304 | tf_op jit(solution)/shard_map/ppermute | solution.py:124
  501.2 39.7 %collective-permute-start.57 = (bf16[384,1024]{1,0:T(8,128)(2,1)S(1)}, bf16[384,1024]{1,0:T(8,128)(2,1)S(1)}, u32[]{:S(2)}, u32[]{:S(2)}) collective-permute-start(bf16[384,1024]{1,0:T(8,128)(2,1)S(1)} %pad_maximum_fusion.29), channel_id=1, source_target_pairs={{0,2},{2,0},{4,6},{6,4},{8,10},{10,8},{12,14},{14,12},{16,18},{18,... | collective-permute-start | bytes 2359304 | tf_op jit(solution)/shard_map/ppermute | solution.py:124
  521.0 146.8 %collective-permute-start.65 = (bf16[512,1536]{1,0:T(8,128)(2,1)}, bf16[512,1536]{1,0:T(8,128)(2,1)}, u32[]{:S(2)}, u32[]{:S(2)}) collective-permute-start(bf16[512,1536]{1,0:T(8,128)(2,1)} %pad_maximum_fusion.9), channel_id=1, source_target_pairs={{0,4},{2,6},{4,0},{6,2},{8,12},{10,14},{12,8},{14,10},{16,20},{18,... | collective-permute-start | bytes 4718600 | tf_op jit(solution)/shard_map/ppermute | solution.py:124
  525.1 150.6 %collective-permute-start.81 = (bf16[1024,768]{1,0:T(8,128)(2,1)}, bf16[1024,768]{1,0:T(8,128)(2,1)}, u32[]{:S(2)}, u32[]{:S(2)}) collective-permute-start(bf16[1024,768]{1,0:T(8,128)(2,1)} %pad_maximum_fusion.10), channel_id=1, source_target_pairs={{0,2},{2,0},{4,6},{6,4},{8,10},{10,8},{12,14},{14,12},{16,18},{18,... | collective-permute-start | bytes 4718600 | tf_op jit(solution)/shard_map/ppermute | solution.py:124
  537.5 79.0 %collective-permute-start.27 = (bf16[256,768]{1,0:T(8,128)(2,1)}, bf16[256,768]{1,0:T(8,128)(2,1)}, u32[]{:S(2)}, u32[]{:S(2)}) collective-permute-start(bf16[256,768]{1,0:T(8,128)(2,1)} %constant_dynamic-slice_fusion.26), channel_id=1, source_target_pairs={{0,2},{2,0},{4,6},{6,4},{8,10},{10,8},{12,14},{14,12},{16,18},{18,... | collective-permute-start | bytes 1179656 | tf_op jit(solution)/shard_map/ppermute | solution.py:124
  540.9 40.2 %collective-permute-start.36 = (bf16[64,1024]{1,0:T(8,128)(2,1)S(1)}, bf16[64,1024]{1,0:T(8,128)(2,1)S(1)}, u32[]{:S(2)}, u32[]{:S(2)}) collective-permute-start(bf16[64,1024]{1,0:T(8,128)(2,1)S(1)} %constant_dynamic-slice_fusion.21), channel_id=1, source_target_pairs={{0,2},{2,0},{4,6},{6,4},{8,10},{10,8},{12,14},{14,12},{16,18},{18,... | collective-permute-start | bytes 393224 | tf_op jit(solution)/shard_map/ppermute | solution.py:124
  615.1 79.2 %collective-permute-start.49 = (bf16[512,1024]{0,1:T(8,128)(2,1)}, bf16[512,1024]{0,1:T(8,128)(2,1)}, u32[]{:S(2)}, u32[]{:S(2)}) collective-permute-start(bf16[512,1024]{0,1:T(8,128)(2,1)} %pad_maximum_fusion.24), channel_id=1, source_target_pairs={{0,4},{2,6},{4,0},{6,2},{8,12},{10,14},{12,8},{14,10},{16,20},{18,... | collective-permute-start | bytes 3145736 | tf_op jit(solution)/shard_map/ppermute | solution.py:124
  645.6 63.0 %collective-permute-start.41 = (bf16[256,1024]{1,0:T(8,128)(2,1)}, bf16[256,1024]{1,0:T(8,128)(2,1)}, u32[]{:S(2)}, u32[]{:S(2)}) collective-permute-start(bf16[256,1024]{1,0:T(8,128)(2,1)} %pad_maximum_fusion.34), channel_id=1, source_target_pairs={{0,8},{2,10},{4,12},{6,14},{8,0},{10,2},{12,4},{14,6},{16,24},{18,... | collective-permute-start | bytes 1572872 | tf_op jit(solution)/shard_map/ppermute | solution.py:124
  (245 other events, 2067.8 us)

commit v2 on v0

v2 whole, which is shorter than its diff:
```python
import math
from collections import namedtuple

import jax
import jax.numpy as jnp
from jax import lax
from jax.experimental import pallas as pl
from jax.experimental.pallas import tpu as pltpu
from jax.sharding import PartitionSpec as P

HD = 64
PAIR = 2 * HD
norm_eps = 1e-05
score_scale = 0.125
masked_fill = -1e30
F32 = jnp.float32
BF16 = jnp.bfloat16
SLACK_BYTES = 6 * 1024 * 1024
SMEM_SPEC = pl.BlockSpec(memory_space=pltpu.SMEM)


def dot(a, b):
    return lax.dot_general(a, b, (((1,), (0,)), ((), ())), preferred_element_type=F32)


def dot_rt(a, b):
    return lax.dot_general(a, b, (((1,), (1,)), ((), ())), preferred_element_type=F32)


def dot_lt(a, b):
    return lax.dot_general(a, b, (((0,), (0,)), ((), ())), preferred_element_type=F32)


def whole(shape):
    zeros = (0,) * len(shape)
    return pl.BlockSpec(tuple(shape), lambda *_: zeros)


def shape_of(shape, kind):
    return jax.ShapeDtypeStruct(tuple(shape), kind)


def vmem_bytes(specs, arrays, scratch=()):
    total = SLACK_BYTES
    for spec, array in zip(specs, arrays):
        if spec.block_shape is not None:
            total += 2 * math.prod(spec.block_shape) * jnp.dtype(array.dtype).itemsize
    for buffer in scratch:
        total += math.prod(buffer.shape) * jnp.dtype(buffer.dtype).itemsize
    return min(total, 60 * 1024 * 1024)


def call(body, grid, in_specs, out_specs, out_shape, args, scratch=(), flops=0):
    return pl.pallas_call(
        body,
        grid=grid,
        in_specs=in_specs,
        out_specs=out_specs,
        out_shape=out_shape,
        scratch_shapes=list(scratch),
        compiler_params=pltpu.CompilerParams(
            vmem_limit_bytes=vmem_bytes(
                [*in_specs, *out_specs], [*args, *out_shape], scratch
            )
        ),
        cost_estimate=pl.CostEstimate(flops=flops, bytes_accessed=1024, transcendentals=0),
    )(*args)


def norm_parts(values):
    average = jnp.mean(values, -1, keepdims=True)
    centered = values - average
    variance = jnp.mean(centered * centered, -1, keepdims=True)
    scale = lax.rsqrt(variance + norm_eps)
    return centered * scale, scale


def layer_norm(values, gain_ref, bias_ref):
    normed, _ = norm_parts(values)
    return normed * gain_ref[...].astype(F32) + bias_ref[...].astype(F32)


ROW_BLOCK = 256


def add_row(ref, row):
    first = (pl.program_id(0) == 0) & (pl.program_id(1) == 0)

    @pl.when(first)
    def _():
        ref[...] = row

    @pl.when(jnp.logical_not(first))
    def _():
        ref[...] += row


def column_sum(values):
    return jnp.sum(values, 0, keepdims=True)


def row_mask(rank_ref, half, count):
    first_row = rank_ref[0] * half + pl.program_id(1) * ROW_BLOCK
    place = first_row + lax.broadcasted_iota(jnp.int32, (ROW_BLOCK, 1), 0)
    return (place < count).astype(F32)


def project_tokens(tokens, gain, bias, w_query, w_key, w_value):
    rows, width = tokens.shape
    local = w_query.shape[1]
    block = 256

    def body(x, g, b, wq, wk, wv, n, q, k, v):
        normed = layer_norm(x[...].astype(F32), g, b).astype(BF16)
        n[...] = normed
        q[...] = dot(normed, wq[...]).astype(BF16)
        k[...] = dot(normed, wk[...]).astype(BF16)
        v[...] = dot(normed, wv[...]).astype(BF16)

    wide = pl.BlockSpec((block, width), lambda i: (i, 0))
    slim = pl.BlockSpec((block, local), lambda i: (i, 0))
    return call(
        body,
        (rows // block,),
        [wide, whole((1, width)), whole((1, width))] + [whole(w_query.shape)] * 3,
        [wide, slim, slim, slim],
        [shape_of((rows, width), BF16)] + [shape_of((rows, local), BF16)] * 3,
        (tokens, gain, bias, w_query, w_key, w_value),
    )


def project_text(text_own, text_other, c_key, c_value):
    items, text_half, depth = text_own.shape
    local = c_key.shape[1]

    def body(own, other, wk, wv, k, v):
        for half, rows in enumerate((own, other)):
            for item in range(items):
                k[item, half] = dot(rows[item], wk[...]).astype(BF16)
                v[item, half] = dot(rows[item], wv[...]).astype(BF16)

    shape = (items, 2, text_half, local)
    return call(
        body,
        (1,),
        [whole(text_own.shape)] * 2 + [whole(c_key.shape)] * 2,
        [whole(shape)] * 2,
        [shape_of(shape, BF16)] * 2,
        (text_own, text_other, c_key, c_value),
    )


def head_mask(rows, head):
    lane = lax.broadcasted_iota(jnp.int32, (rows, PAIR), 1)
    return lane < HD if head == 0 else lane >= HD


def pick(first, second):
    return jnp.where(head_mask(first.shape[0], 0), first, second)


def only(values, head):
    return jnp.where(head_mask(values.shape[0], head), values, jnp.zeros_like(values))


def scores_t(query_pair, key_pair, head, allowed):
    scores = dot_rt(key_pair, only(query_pair, head)) * score_scale
    return jnp.where(allowed, scores, masked_fill)


def attend_pair(query_pair, key_pair, value_pair, allowed, lse_ref, lse_at):
    mixed = []
    for head in range(2):
        scores = scores_t(query_pair, key_pair, head, allowed)
        highest = jnp.max(scores, 0, keepdims=True)
        powers = jnp.exp(scores - highest)
        total = jnp.sum(powers, 0, keepdims=True)
        probs = (powers / total).astype(BF16)
        mixed.append(dot_lt(probs, value_pair))
        row, columns = lse_at(head)
        lse_ref[0, row : row + 1, columns] = highest + jnp.log(total)
    return pick(mixed[0], mixed[1]).astype(BF16)


def attend_pair_back(query_pair, key_pair, value_pair, allowed, lse_rows, grad_pair):
    grads = []
    for head in range(2):
        probs = jnp.exp(scores_t(query_pair, key_pair, head, allowed) - lse_rows[head])
        grad_probs = dot_rt(value_pair, only(grad_pair, head))
        inner = jnp.sum(grad_probs * probs, 0, keepdims=True)
        grad_scores = (probs * (grad_probs - inner)).astype(BF16)
        grads.append(
            (
                dot_lt(grad_scores, key_pair),
                dot(grad_scores, query_pair),
                dot(probs.astype(BF16), grad_pair),
            )
        )
    return [pick(one, two) for one, two in zip(grads[0], grads[1])]


def causal_mask(keys, queries, first_query, count):
    key_at = lax.broadcasted_iota(jnp.int32, (keys, queries), 0)
    query_at = first_query + lax.broadcasted_iota(jnp.int32, (keys, queries), 1)
    return (key_at <= query_at) & (key_at < count)


def text_mask(text_half, queries, rank, count):
    key_at = lax.broadcasted_iota(jnp.int32, (2 * text_half, queries), 0)
    swapped = jnp.where(key_at < text_half, key_at + text_half, key_at - text_half)
    return jnp.where(rank == 0, key_at, swapped) < count


def self_forward(rank, valid, query, key, value, w_out):
    items, frames, local = query.shape
    width = w_out.shape[1]
    half = frames // 2
    heads = local // HD

    def body(rank_ref, valid_ref, q, k, v, w, mix, lse, own, send):
        me = rank_ref[0]
        count = valid_ref[pl.program_id(0)]
        for part in range(2):
            keys = (part + 1) * half
            allowed = causal_mask(keys, half, part * half, count)
            rows = slice(part * half, (part + 1) * half)
            for pair in range(local // PAIR):
                columns = slice(pair * PAIR, (pair + 1) * PAIR)
                mix[part ^ me, 0, :, columns] = attend_pair(
                    q[0, rows, columns],
                    k[0, :keys, columns],
                    v[0, :keys, columns],
                    allowed,
                    lse,
                    lambda head: (2 * pair + head, rows),
                )
        send[0] = dot(mix[1, 0], w[...]).astype(BF16)
        own[0] = dot(mix[0, 0], w[...])

    tall = pl.BlockSpec((1, frames, local), lambda i: (i, 0, 0))
    out = pl.BlockSpec((1, half, width), lambda i: (i, 0, 0))
    return call(
        body,
        (items,),
        [SMEM_SPEC, SMEM_SPEC, tall, tall, tall, whole(w_out.shape)],
        [
            pl.BlockSpec((2, 1, half, local), lambda i: (0, i, 0, 0)),
            pl.BlockSpec((1, heads, frames), lambda i: (i, 0, 0)),
            out,
            out,
        ],
        [
            shape_of((2, items, half, local), BF16),
            shape_of((items, heads, frames), F32),
            shape_of((items, half, width), F32),
            shape_of((items, half, width), BF16),
        ],
        (rank, valid, query, key, value, w_out),
    )


def cross_forward(rank, text_len, normed_own, normed_other, c_query, key, value, c_out):
    items, half, width = normed_own.shape
    text_half = key.shape[2]
    local = c_query.shape[1]
    heads = local // HD

    def body(rank_ref, len_ref, own_n, other_n, wq, k, v, w, q, mix, lse, own, send):
        allowed = text_mask(text_half, half, rank_ref[0], len_ref[pl.program_id(0)])
        for part, normed in enumerate((own_n, other_n)):
            q[part, 0] = dot(normed[0], wq[...]).astype(BF16)
            for pair in range(local // PAIR):
                columns = slice(pair * PAIR, (pair + 1) * PAIR)
                mix[part, 0, :, columns] = attend_pair(
                    q[part, 0, :, columns],
                    k[0, :, :, columns].reshape(2 * text_half, PAIR),
                    v[0, :, :, columns].reshape(2 * text_half, PAIR),
                    allowed,
                    lse,
                    lambda head: (2 * pair + head, slice(part * half, (part + 1) * half)),
                )
        send[0] = dot(mix[1, 0], w[...]).astype(BF16)
        own[0] = dot(mix[0, 0], w[...])

    out = pl.BlockSpec((1, half, width), lambda i: (i, 0, 0))
    text = pl.BlockSpec((1, 2, text_half, local), lambda i: (i, 0, 0, 0))
    both = pl.BlockSpec((2, 1, half, local), lambda i: (0, i, 0, 0))
    return call(
        body,
        (items,),
        [SMEM_SPEC, SMEM_SPEC, out, out, whole(c_query.shape), text, text, whole(c_out.shape)],
        [both, both, pl.BlockSpec((1, heads, 2 * half), lambda i: (i, 0, 0)), out, out],
        [
            shape_of((2, items, half, local), BF16),
            shape_of((2, items, half, local), BF16),
            shape_of((items, heads, 2 * half), F32),
            shape_of((items, half, width), F32),
            shape_of((items, half, width), BF16),
        ],
        (rank, text_len, normed_own, normed_other, c_query, key, value, c_out),
    )


def residual_norm(rank, valid, base, own, received, gain, bias):
    items, half, width = own.shape

    def body(rank_ref, valid_ref, x, part, other, g, b, hidden, normed, square):
        item = pl.program_id(0)
        branch = part[0] + other[0].astype(F32)
        total = x[0].astype(F32) + branch
        hidden[0] = total
        normed[0] = layer_norm(total, g, b).astype(BF16)
        mask = row_mask(rank_ref, half, valid_ref[item])
        add_row(square, column_sum(mask * branch * branch))

    steps = half // ROW_BLOCK
    block = pl.BlockSpec((1, ROW_BLOCK, width), lambda i, r, *_: (i, r, 0))
    row = whole((1, width))
    if base.shape[1] == half:
        base_spec = block
    else:
        base_spec = pl.BlockSpec(
            (1, ROW_BLOCK, width), lambda i, r, me, _: (i, me[0] * steps + r, 0)
        )
    return pl.pallas_call(
        body,
        grid_spec=pltpu.PrefetchScalarGridSpec(
            num_scalar_prefetch=2,
            grid=(items, steps),
            in_specs=[base_spec, block, block, row, row],
            out_specs=[block, block, row],
        ),
        out_shape=[
            shape_of(own.shape, F32),
            shape_of(own.shape, BF16),
            shape_of((1, width), F32),
        ],
        compiler_params=pltpu.CompilerParams(vmem_limit_bytes=3 * SLACK_BYTES),
        cost_estimate=pl.CostEstimate(flops=0, bytes_accessed=1024, transcendentals=0),
    )(rank, valid, base, own, received, gain, bias)


def gelu_parts(values):
    normal = 0.5 * (1.0 + lax.erf(values * (0.5**0.5)))
    density = jnp.exp(-0.5 * values * values) * 0.3989422804014327
    return values * normal, normal + values * density


def feed_forward(
    block_index, orders, normed_own, normed_other, grad_own, grad_other, w_up, w_down
):
    rows, width = normed_own.shape
    units = w_up.shape[1]
    steps = units // LANES
    down_each, up_each = units // BLOCKS, width // BLOCKS
    sizes = dict(down=down_each, up=up_each * (steps - 1), rest=down_each + up_each)

    def body(me_ref, n_own, n_other, g_own, g_other, up_w, down_w, act, grad, *rest):
        me = me_ref[0]
        packets = {name: rest[2 * k : 2 * k + 2] for k, name in enumerate(sizes)}
        down_part, up_part = rest[2 * len(sizes) :]
        step = pl.program_id(0)
        down_sum, up_sum = 0.0, 0.0
        for half, (n, g) in enumerate(((n_own, g_own), (n_other, g_other))):
            value, slope = gelu_parts(dot(n[...], up_w[...]))
            act[half] = value.astype(BF16)
            grad[half] = (dot_rt(g[...], down_w[...]) * slope).astype(BF16)
            down_sum = down_sum + dot_lt(act[half], g[...])
            up_sum = up_sum + dot_lt(n[...], grad[half])
        down_part[...] = down_sum.astype(BF16)
        up_part[...] = up_sum.astype(BF16)

        def put(name, block, first, values):
            place = place_of(block ^ me, orders[name])
            keep, send = packets[name]
            where = pl.ds(first, values.shape[0])

            @pl.when(place < BLOCKS // 2)
            def _():
                keep[place, where, :] = values

            @pl.when(place >= BLOCKS // 2)
            def _():
                send[place - BLOCKS // 2, where, :] = values

        for sub in range(LANES // down_each):
            part = slice(sub * down_each, (sub + 1) * down_each)
            block = step * (LANES // down_each) + sub
            put("down", block, 0, down_part[part, :LANES])
            put("rest", block, 0, down_part[part, LANES:])

        @pl.when(step < steps - 1)
        def _():
            for block in range(BLOCKS):
                part = slice(block * up_each, (block + 1) * up_each)
                put("up", block, step * up_each, up_part[part, :])

        @pl.when(step == steps - 1)
        def _():
            for block in range(BLOCKS):
                part = slice(block * up_each, (block + 1) * up_each)
                put("rest", block, down_each, up_part[part, :])

    out = pl.BlockSpec((2, rows, LANES), lambda j: (0, 0, j))
    shapes = [(BLOCKS // 2, sizes[name], LANES) for name in sizes for _ in range(2)]
    results = call(
        body,
        (steps,),
        [SMEM_SPEC]
        + [whole(normed_own.shape)] * 4
        + [
            pl.BlockSpec((width, LANES), lambda j: (0, j)),
            pl.BlockSpec((LANES, width), lambda j: (j, 0)),
        ],
        [out, out] + [whole(shape) for shape in shapes],
        [shape_of((2, rows, units), BF16)] * 2 + [shape_of(shape, BF16) for shape in shapes],
        (block_index, normed_own, normed_other, grad_own, grad_other, w_up, w_down),
        scratch=[pltpu.VMEM((LANES, width), BF16), pltpu.VMEM((width, LANES), BF16)],
    )
    pairs = {name: results[2 + 2 * k : 4 + 2 * k] for k, name in enumerate(sizes)}
    return results[0], results[1], pairs


def project_halves(values, weight, transposed):
    _, rows, depth = values.shape
    width = weight.shape[0] if transposed else weight.shape[1]

    def body(a, w, own, send):
        multiply = dot_rt if transposed else dot
        product = multiply(a[0], w[...])

        @pl.when(pl.program_id(0) == 0)
        def _():
            send[...] = product.astype(BF16)

        @pl.when(pl.program_id(0) == 1)
        def _():
            own[...] = product

    return call(
        body,
        (2,),
        [pl.BlockSpec((1, rows, depth), lambda j: (1 - j, 0, 0)), whole(weight.shape)],
        [whole((rows, width))] * 2,
        [shape_of((rows, width), F32), shape_of((rows, width), BF16)],
        (values, weight),
    )


def finish_output(rank, valid, hidden, own, received):
    items, half, width = hidden.shape

    def body(rank_ref, valid_ref, x, part, other, out, square, branch_square):
        branch = part[0] + other[0].astype(F32)
        total = x[0] + branch
        out[0] = total.astype(BF16)
        mask = row_mask(rank_ref, half, valid_ref[pl.program_id(0)])
        add_row(square, column_sum(mask * total * total))
        add_row(branch_square, column_sum(mask * branch * branch))

    steps = half // ROW_BLOCK
    block = pl.BlockSpec((1, ROW_BLOCK, width), lambda i, r: (i, r, 0))
    return call(
        body,
        (items, steps),
        [SMEM_SPEC, SMEM_SPEC, block, block, block],
        [block, whole((1, width)), whole((1, width))],
        [shape_of(hidden.shape, BF16)] + [shape_of((1, width), F32)] * 2,
        (rank, valid, hidden, own, received),
    )


def norm_backward(rank, values, gain, own, received, grad_base, last):
    items, half, width = own.shape

    def body(rank_ref, x, g, part, other, base, *outs):
        normed, scale = norm_parts(x[0].astype(F32))
        grad = part[0] + other[0].astype(F32)
        add_row(outs[1], column_sum(grad * normed))
        add_row(outs[2], column_sum(grad))
        scaled = grad * g[...].astype(F32)
        first = jnp.mean(scaled, -1, keepdims=True)
        second = jnp.mean(scaled * normed, -1, keepdims=True)
        total = base[0].astype(F32) + scale * (scaled - first - normed * second)
        outs[0][0] = total
        if not last:
            outs[3][0] = total.astype(BF16)

    steps = half // ROW_BLOCK
    block = pl.BlockSpec((1, ROW_BLOCK, width), lambda i, r, *_: (i, r, 0))
    row = whole((1, width))
    if values.shape[1] == half:
        values_spec = block
    else:
        values_spec = pl.BlockSpec(
            (1, ROW_BLOCK, width), lambda i, r, me: (i, me[0] * steps + r, 0)
        )
    out_specs = [block, row, row]
    out_shape = [
        shape_of(own.shape, F32),
        shape_of((1, width), F32),
        shape_of((1, width), F32),
    ]
    if not last:
        out_specs.append(block)
        out_shape.append(shape_of(own.shape, BF16))
    return pl.pallas_call(
        body,
        grid_spec=pltpu.PrefetchScalarGridSpec(
            num_scalar_prefetch=1,
            grid=(items, steps),
            in_specs=[values_spec, row, block, block, block],
            out_specs=out_specs,
        ),
        out_shape=out_shape,
        compiler_params=pltpu.CompilerParams(vmem_limit_bytes=3 * SLACK_BYTES),
        cost_estimate=pl.CostEstimate(flops=0, bytes_accessed=1024, transcendentals=0),
    )(rank, values, gain, own, received, grad_base)


def cross_backward(
    rank, text_len, grad_own, grad_other, c_out, query, key, value, lse, c_query, c_key, c_value
):
    items, half, width = grad_own.shape
    text_half = key.shape[2]
    depth, local = c_key.shape
    heads = local // HD

    def body(
        rank_ref, len_ref, g_own, g_other, w, q, k, v, stats, wq, wk, wv,
        dq, dk, dv, own, send, text_own, text_send, grad_mix,
    ):
        allowed = text_mask(text_half, half, rank_ref[0], len_ref[pl.program_id(0)])
        for part, grad in enumerate((g_own, g_other)):
            grad_mix[part] = dot_rt(grad[0], w[...]).astype(BF16)
        for pair in range(local // PAIR):
            columns = slice(pair * PAIR, (pair + 1) * PAIR)
            key_sum, value_sum = 0.0, 0.0
            for part in range(2):
                rows = slice(part * half, (part + 1) * half)
                one, two, three = attend_pair_back(
                    q[part, 0, :, columns],
                    k[0, :, :, columns].reshape(2 * text_half, PAIR),
                    v[0, :, :, columns].reshape(2 * text_half, PAIR),
                    allowed,
                    [stats[0, 2 * pair + head : 2 * pair + head + 1, rows] for head in range(2)],
                    grad_mix[part, :, columns],
                )
                dq[part, 0, :, columns] = (one * score_scale).astype(BF16)
                key_sum, value_sum = key_sum + two, value_sum + three
            key_sum = (key_sum * score_scale).astype(BF16)
            value_sum = value_sum.astype(BF16)
            for part in range(2):
                rows = slice(part * text_half, (part + 1) * text_half)
                dk[0, part, :, columns] = key_sum[rows]
                dv[0, part, :, columns] = value_sum[rows]
        send[0] = dot_rt(dq[1, 0], wq[...]).astype(BF16)
        own[0] = dot_rt(dq[0, 0], wq[...])
        text_send[0] = (dot_rt(dk[0, 1], wk[...]) + dot_rt(dv[0, 1], wv[...])).astype(BF16)
        text_own[0] = dot_rt(dk[0, 0], wk[...]) + dot_rt(dv[0, 0], wv[...])

    out = pl.BlockSpec((1, half, width), lambda i: (i, 0, 0))
    text = pl.BlockSpec((1, 2, text_half, local), lambda i: (i, 0, 0, 0))
    both = pl.BlockSpec((2, 1, half, local), lambda i: (0, i, 0, 0))
    deep = pl.BlockSpec((1, text_half, depth), lambda i: (i, 0, 0))
    return call(
        body,
        (items,),
        [
            SMEM_SPEC, SMEM_SPEC, out, out, whole(c_out.shape), both, text, text,
            pl.BlockSpec((1, heads, 2 * half), lambda i: (i, 0, 0)),
            whole(c_query.shape), whole(c_key.shape), whole(c_value.shape),
        ],
        [both, text, text, out, out, deep, deep],
        [
            shape_of(query.shape, BF16),
            shape_of(key.shape, BF16),
            shape_of(key.shape, BF16),
            shape_of(grad_own.shape, F32),
            shape_of(grad_own.shape, BF16),
            shape_of((items, text_half, depth), F32),
            shape_of((items, text_half, depth), BF16),
        ],
        (
            rank, text_len, grad_own, grad_other, c_out, query, key, value, lse,
            c_query, c_key, c_value,
        ),
        scratch=[pltpu.VMEM((2, half, local), BF16)],
    )


def self_backward(
    rank, valid, grad_own, grad_other, w_out, query, key, value, lse, w_query, w_key, w_value
):
    items, half, width = grad_own.shape
    frames, local = query.shape[1:]
    heads = local // HD

    def body(
        rank_ref, valid_ref, g_own, g_other, w, q, k, v, stats, wq, wk, wv,
        dq, dk, dv, own, send, grad_mix,
    ):
        me = rank_ref[0]
        count = valid_ref[pl.program_id(0)]
        grad_mix[me] = dot_rt(g_own[0], w[...]).astype(BF16)
        grad_mix[1 - me] = dot_rt(g_other[0], w[...]).astype(BF16)
        masks = [causal_mask((part + 1) * half, half, part * half, count) for part in range(2)]
        for pair in range(local // PAIR):
            columns = slice(pair * PAIR, (pair + 1) * PAIR)
            sums = []
            for part in range(2):
                keys = (part + 1) * half
                rows = slice(part * half, keys)
                one, two, three = attend_pair_back(
                    q[0, rows, columns],
                    k[0, :keys, columns],
                    v[0, :keys, columns],
                    masks[part],
                    [stats[0, 2 * pair + head : 2 * pair + head + 1, rows] for head in range(2)],
                    grad_mix[part, :, columns],
                )
                dq[0, rows, columns] = (one * score_scale).astype(BF16)
                sums.append((two, three))
            (key_a, value_a), (key_b, value_b) = sums
            dk[0, :half, columns] = ((key_a + key_b[:half]) * score_scale).astype(BF16)
            dk[0, half:, columns] = (key_b[half:] * score_scale).astype(BF16)
            dv[0, :half, columns] = (value_a + value_b[:half]).astype(BF16)
            dv[0, half:, columns] = value_b[half:].astype(BF16)

        def back(part):
            rows = pl.ds(pl.multiple_of(part * half, half), half)
            return (
                dot_rt(dq[0, rows, :], wq[...])
                + dot_rt(dk[0, rows, :], wk[...])
                + dot_rt(dv[0, rows, :], wv[...])
            )

        send[0] = back(1 - me).astype(BF16)
        own[0] = back(me)

    out = pl.BlockSpec((1, half, width), lambda i: (i, 0, 0))
    tall = pl.BlockSpec((1, frames, local), lambda i: (i, 0, 0))
    return call(
        body,
        (items,),
        [
            SMEM_SPEC, SMEM_SPEC, out, out, whole(w_out.shape), tall, tall, tall,
            pl.BlockSpec((1, heads, frames), lambda i: (i, 0, 0)),
            whole(w_query.shape), whole(w_key.shape), whole(w_value.shape),
        ],
        [tall, tall, tall, out, out],
        [shape_of(query.shape, BF16)] * 3
        + [shape_of(grad_own.shape, F32), shape_of(grad_own.shape, BF16)],
        (
            rank, valid, grad_own, grad_other, w_out, query, key, value, lse,
            w_query, w_key, w_value,
        ),
        scratch=[pltpu.VMEM((2, half, local), BF16)],
    )


BLOCKS = 16
LEVELS = 4
LANES = 512
Piece = namedtuple("Piece", ("terms", "rows", "first", "width", "tile", "full"))


def place_of(block, order):
    place = 0
    for k, bit in enumerate(order):
        place = place + (((block >> bit) & 1) << (LEVELS - 1 - k))
    return place


def block_at(place, order):
    return sum(((place >> (LEVELS - 1 - k)) & 1) << bit for k, bit in enumerate(order))


def gradient_packet(block_index, pieces, order, operands):
    rows_each = sum(piece.rows // BLOCKS * (piece.width // LANES) for piece in pieces)
    count = len(operands)
    starts = []
    steps = 0
    for piece in pieces:
        starts.append(steps)
        steps += piece.rows // piece.tile if piece.tile < piece.rows else piece.width // LANES

    def body(*refs):
        me = refs[0][0]
        given = refs[1 : 1 + count]
        keep, send, natural = refs[1 + count :]
        step = pl.program_id(0)
        offset = 0
        for start, piece in zip(starts, pieces):
            by_rows = piece.tile < piece.rows
            number = piece.rows // piece.tile if by_rows else piece.width // LANES
            each = piece.rows // BLOCKS

            @pl.when((step >= start) & (step < start + number))
            def _(start=start, piece=piece, by_rows=by_rows, each=each, offset=offset):
                total = None
                for (left, left_at), (right, right_at) in piece.terms:
                    term = dot_lt(given[left][left_at], given[right][right_at])
                    total = term if total is None else total + term
                natural[: piece.tile, :] = total.astype(BF16)
                at = step - start
                for sub in range(piece.tile // each):
                    block = (at * (piece.tile // each) + sub if by_rows else sub) ^ me
                    place = place_of(block, order)
                    base = offset if by_rows else offset + at * each
                    rows = pl.ds(base, each)
                    values = natural[sub * each : (sub + 1) * each, :]

                    @pl.when(place < BLOCKS // 2)
                    def _():
                        keep[place, rows, :] = values

                    @pl.when(place >= BLOCKS // 2)
                    def _():
                        send[place - BLOCKS // 2, rows, :] = values

            offset += each * (piece.width // LANES)

    def spec(array, axis, start, number, block):
        if axis is None:
            return whole(array.shape)
        shape = list(array.shape)
        shape[axis] = block
        first, at = start

        def index(i):
            place = [0] * len(shape)
            place[axis] = first + jnp.clip(i - at, 0, number - 1)
            return tuple(place)

        return pl.BlockSpec(tuple(shape), index)

    half_shape = (BLOCKS // 2, rows_each, LANES)
    return call(
        body,
        (steps,),
        [SMEM_SPEC] + [spec(*operand) for operand in operands],
        [whole(half_shape)] * 2,
        [shape_of(half_shape, BF16)] * 2,
        (block_index, *(operand[0] for operand in operands)),
        scratch=[pltpu.VMEM((max(piece.tile for piece in pieces), LANES), BF16)],
    )


def open_packet(block_index, pieces, order, kept, received, before):
    steps = 4
    group = BLOCKS // steps
    previous = [x for x in before if x is not None]

    def body(*refs):
        me = refs[0][0]
        low, high = refs[1], refs[2]
        outs = refs[3 + len(previous) :]
        for step in range(group):
            place = place_of((pl.program_id(0) * group + step) ^ me, order)
            inner = place & (BLOCKS // 2 - 1)
            upper = place >= BLOCKS // 2
            offset = 0
            for out, piece in zip(outs, pieces):
                each = piece.rows // BLOCKS
                for column in range(piece.width // LANES):
                    part = slice(offset, offset + each)
                    values = jnp.where(upper, high[inner, part, :], low[inner, part, :])
                    lanes = slice(column * LANES, (column + 1) * LANES)
                    out[step * each : (step + 1) * each, lanes] = values.astype(F32)
                    offset += each

    out_specs, out_shape, aliases = [], [], {}
    for number, (piece, old) in enumerate(zip(pieces, before)):
        at = piece.first // piece.width
        out_specs.append(
            pl.BlockSpec((piece.rows // steps, piece.width), lambda i, at=at: (i, at))
        )
        out_shape.append(shape_of((piece.rows, piece.full), F32))
        if old is not None:
            aliases[3 + len(aliases)] = number
    return pl.pallas_call(
        body,
        grid=(steps,),
        in_specs=[SMEM_SPEC, whole(kept.shape), whole(kept.shape)]
        + [pl.BlockSpec(memory_space=pl.ANY)] * len(previous),
        out_specs=out_specs,
        out_shape=out_shape,
        input_output_aliases=aliases,
        compiler_params=pltpu.CompilerParams(vmem_limit_bytes=3 * SLACK_BYTES),
        cost_estimate=pl.CostEstimate(flops=0, bytes_accessed=1024, transcendentals=0),
    )(block_index, kept, received, *previous)


def main_bits():
    bits = lax.axis_size("dp").bit_length() - 1
    along_x = (bits - 2) // 2
    main = [0, along_x, bits - 2, bits - 1]
    return main, [bit for bit in range(bits) if bit not in main]


def exchange(values, bit):
    pairs = [(d, d ^ (1 << bit)) for d in range(lax.axis_size("dp"))]
    return lax.ppermute(values, "dp", pairs)


def add_rounded(one, two):
    return (one.astype(F32) + two.astype(F32)).astype(BF16)


SWAP = [(0, 1), (1, 0)]


def swap_cores(values):
    return lax.ppermute(values, "mp", SWAP)


class Program:
    def __init__(self, given):
        self.v = dict(given)
        self.token = jnp.zeros((8, 128), F32)
        self.packets = {}

    def tie(self, values):
        values, self.token = lax.optimization_barrier((values, self.token))
        return values

    def start(self, name):
        packet = self.packets[name]
        order, step = packet["order"], packet["step"]
        bit = (order + order[::-1])[step]
        if step < LEVELS:
            values = self.tie(packet["send"])
        else:
            values = packet["keep"] = self.tie(packet["keep"])
        packet["arrived"] = exchange(values, self.main[bit])

    def finish(self, name):
        packet = self.packets[name]
        step, keep = packet["step"], packet["keep"]
        arrived = self.tie(packet["arrived"])
        packet["step"] = step + 1
        if step < LEVELS - 1:
            half = keep.shape[0] // 2
            packet["send"] = add_rounded(keep[half:], arrived[half:])
            packet["keep"] = add_rounded(keep[:half], arrived[:half])
            packet["send"] = self.tie(packet["send"])
        elif step == LEVELS - 1:
            keep = add_rounded(keep, arrived)
            for bit in self.extra:
                keep = add_rounded(keep, exchange(keep, bit))
            packet["keep"] = self.tie(keep)
        elif step < 2 * LEVELS - 1:
            packet["keep"] = self.tie(jnp.concatenate([keep, arrived], 0))
        else:
            outs = open_packet(
                self.block,
                packet["pieces"],
                packet["order"],
                keep,
                arrived,
                [self.v.get(out) for out in packet["outs"]],
            )
            for out, values in zip(packet["outs"], outs):
                self.v[out] = values
            self.v[packet["outs"][0]] = self.tie(outs[0])

    def packet(self, name, outs, pieces, operands):
        order = ORDERS[name]
        operands = [
            x if isinstance(x, tuple) else (x, None, None, None, None) for x in operands
        ]
        operands[0] = (self.tie(operands[0][0]), *operands[0][1:])
        self.add(name, gradient_packet(self.block, pieces, order, operands), pieces, outs)

    def add(self, name, halves_of, pieces, outs):
        keep, send = halves_of
        self.packets[name] = dict(
            order=ORDERS[name], step=0, keep=keep, send=self.tie(send), pieces=pieces, outs=outs
        )


def stage_text(p):
    v = p.v
    v["k_cross"], v["v_cross"] = project_text(
        v["text_own"], v["text_other"], v["c_key"], v["c_value"]
    )


def stage_tokens(p):
    v = p.v
    items, frames, width = v["tokens"].shape
    normed, *heads = project_tokens(
        v["tokens"].reshape(items * frames, width),
        v["gain_one"],
        v["bias_one"],
        v["w_query"],
        v["w_key"],
        v["w_value"],
    )
    v["normed_one"] = normed
    v["q_self"], v["k_self"], v["v_self"] = [x.reshape(items, frames, -1) for x in heads]


def stage_self(p):
    v = p.v
    v["mix_self"], v["lse_self"], v["attn_own"], send = self_forward(
        p.rank, v["frame_valid"], v["q_self"], v["k_self"], v["v_self"], v["w_out"]
    )
    v["attn_other"] = swap_cores(send)


def stage_norm_two(p):
    v = p.v
    v["hidden_one"], v["n2_own"], v["square_attn"] = residual_norm(
        p.rank, v["frame_valid"], v["tokens"], v["attn_own"], v["attn_other"],
        v["gain_two"], v["bias_two"],
    )
    v["n2_other"] = swap_cores(v["n2_own"])


def stage_cross(p):
    v = p.v
    v["q_cross"], v["mix_cross"], v["lse_cross"], v["cross_own"], send = cross_forward(
        p.rank, v["text_len"], v["n2_own"], v["n2_other"], v["c_query"],
        v["k_cross"], v["v_cross"], v["c_out"],
    )
    v["cross_other"] = swap_cores(send)


def stage_norm_three(p):
    v = p.v
    v["hidden_two"], v["n3_own"], v["square_cross"] = residual_norm(
        p.rank, v["frame_valid"], v["hidden_one"], v["cross_own"], v["cross_other"],
        v["gain_three"], v["bias_three"],
    )
    v["n3_other"] = swap_cores(v["n3_own"])


def flat(values):
    return values.reshape(-1, values.shape[-1])


def stage_units(p):
    v = p.v
    units, width = v["w_down"].shape
    v["activated"], v["grad_up"], pairs = feed_forward(
        p.block, ORDERS, flat(v["n3_own"]), flat(v["n3_other"]), flat(v["grad_own"]),
        flat(v["grad_other"]), v["w_up"], v["w_down"],
    )
    down = [Piece(None, units, at, LANES, None, width) for at in (0, LANES)]
    up = [
        Piece(None, width, 0, units - LANES, None, units),
        Piece(None, width, units - LANES, LANES, None, units),
    ]
    p.add("down", pairs["down"], down[:1], ["d_w_down"])
    p.add("up", pairs["up"], up[:1], ["d_w_up"])
    p.add("rest", pairs["rest"], [down[1], up[1]], ["d_w_down", "d_w_up"])


HALF_TERMS = [((0, (0,)), (1, ())), ((0, (1,)), (2, ()))]


def stage_back_units(p):
    v = p.v
    own, send = project_halves(v["grad_up"], v["w_up"], True)
    shape = v["hidden_two"].shape
    v["gn3_own"], v["gn3_other"] = own.reshape(shape), swap_cores(send).reshape(shape)


def stage_back_three(p):
    v = p.v
    v["g_h2"], v["d_gain_three"], v["d_bias_three"], v["g_cross_own"] = norm_backward(
        p.rank, v["hidden_two"], v["gain_three"], v["gn3_own"], v["gn3_other"],
        v["grad_own"], False,
    )
    v["g_cross_other"] = swap_cores(v["g_cross_own"])


def stage_out(p):
    v = p.v
    own, send = project_halves(v["activated"], v["w_down"], False)
    shape = v["hidden_two"].shape
    v["ff_own"], v["ff_other"] = own.reshape(shape), swap_cores(send).reshape(shape)


def stage_result(p):
    v = p.v
    v["out"], v["square_out"], v["square_ff"] = finish_output(
        p.rank, v["frame_valid"], v["hidden_two"], v["ff_own"], v["ff_other"]
    )


def stage_back_cross(p):
    v = p.v
    (
        v["dq_cross"], v["dk_cross"], v["dv_cross"], v["gn2_own"], send,
        v["text_grad_own"], text_send,
    ) = cross_backward(
        p.rank, v["text_len"], v["g_cross_own"], v["g_cross_other"], v["c_out"],
        v["q_cross"], v["k_cross"], v["v_cross"], v["lse_cross"],
        v["c_query"], v["c_key"], v["c_value"],
    )
    v["gn2_other"] = swap_cores(send)
    v["text_grad_other"] = swap_cores(text_send)


def halves(values):
    return values.reshape(2, -1, values.shape[-1])


def stage_cross_packet(p):
    v = p.v
    items, _, _, local = v["dk_cross"].shape
    depth = v["c_key"].shape[0]
    width = v["c_query"].shape[0]
    query_terms = [((1, ()), (0, (0,))), ((2, ()), (0, (1,)))]

    def text_terms(place):
        return [
            ((3 + half, (item,)), (place, (item, half))) for item in range(items) for half in (0, 1)
        ]

    p.packet(
        "cross", ["d_c_query", "d_c_key", "d_c_value"],
        [
            Piece(query_terms, width, 0, local, width, local),
            Piece(text_terms(5), depth, 0, local, depth, local),
            Piece(text_terms(6), depth, 0, local, depth, local),
        ],
        [
            halves(v["dq_cross"]), flat(v["n2_own"]), flat(v["n2_other"]),
            v["text_own"], v["text_other"], v["dk_cross"], v["dv_cross"],
        ],
    )


def stage_back_two(p):
    v = p.v
    v["g_h1"], v["d_gain_two"], v["d_bias_two"], v["g_attn_own"] = norm_backward(
        p.rank, v["hidden_one"], v["gain_two"], v["gn2_own"], v["gn2_other"], v["g_h2"], False
    )
    v["g_attn_other"] = swap_cores(v["g_attn_own"])


def stage_back_self(p):
    v = p.v
    v["dq_self"], v["dk_self"], v["dv_self"], v["gn1_own"], send = self_backward(
        p.rank, v["frame_valid"], v["g_attn_own"], v["g_attn_other"], v["w_out"],
        v["q_self"], v["k_self"], v["v_self"], v["lse_self"],
        v["w_query"], v["w_key"], v["w_value"],
    )
    v["gn1_other"] = swap_cores(send)


def stage_proj_packet(p):
    v = p.v
    local, width = v["w_out"].shape
    terms = [((3, (0,)), (4, ())), ((3, (1,)), (5, ()))]
    steps = width // LANES

    def streamed(name, first):
        return (flat(v[name]), 1, (0, first), steps, LANES)

    p.packet(
        "proj", ["d_c_out", "d_w_out"],
        [
            Piece(HALF_TERMS, local, 0, width, local, width),
            Piece(terms, local, 0, width, local, width),
        ],
        [
            halves(v["mix_cross"]), streamed("g_cross_own", 0), streamed("g_cross_other", 0),
            halves(v["mix_self"]), streamed("g_attn_own", steps),
            streamed("g_attn_other", steps),
        ],
    )


def self_packet(p, name, grad, out):
    v = p.v
    width, local = v["w_query"].shape
    piece = Piece([((0, ()), (1, ()))], width, 0, local, width, local)
    p.packet(name, [out], [piece], [v["normed_one"], flat(v[grad])])


def stage_query_packet(p):
    self_packet(p, "query", "dq_self", "d_w_query")


def stage_key_packet(p):
    self_packet(p, "key", "dk_self", "d_w_key")


def stage_value_packet(p):
    self_packet(p, "value", "dv_self", "d_w_value")


def stage_back_one(p):
    v = p.v
    v["d_tokens"], v["d_gain_one"], v["d_bias_one"] = norm_backward(
        p.rank, v["tokens"], v["gain_one"], v["gn1_own"], v["gn1_other"], v["g_h1"], True
    )


def stage_text_grad(p):
    v = p.v
    v["d_text"] = v["text_grad_own"] + v["text_grad_other"].astype(F32)


SMALL = (
    "d_gain_one", "d_bias_one", "d_gain_two", "d_bias_two", "d_gain_three", "d_bias_three",
    "square_out", "square_attn", "square_cross", "square_ff",
)


def stage_small(p):
    v = p.v
    half = v["hidden_one"].shape[1]
    width = v["hidden_one"].shape[2]
    own = jnp.clip(v["frame_valid"] - p.rank * half, 0, half).sum().astype(F32)
    rows = [v[name] for name in SMALL] + [jnp.full((1, width), own / width, F32)]
    rows.append(jnp.zeros((16 - len(rows), width), F32))
    total = p.tie(jnp.concatenate(rows, 0))
    v["small"] = total
    v["small_other"] = swap_cores(total)
    p.hops = list(range(lax.axis_size("dp").bit_length() - 1))


def stage_hop(p):
    v = p.v
    total = v["small"] = p.tie(v["small"] + v["small_other"])
    if p.hops:
        v["small_other"] = exchange(total, p.hops.pop(0))


def stage_rms(p):
    v = p.v
    while p.hops:
        stage_hop(p)
    total = v["small"] + v["small_other"]
    width = total.shape[1]
    v["small"] = total[:6]
    sums = jnp.sum(total[6:11], -1)
    v["rms"] = jnp.sqrt(sums[:4] / (sums[4] * width))


def stage_end(p):
    p.v["rms"] = p.v["rms"] + p.token[0, :4] * 0.0


ORDERS = {
    "down": [2, 0, 1, 3],
    "up": [0, 1, 2, 3],
    "rest": [1, 0, 2, 3],
    "cross": [2, 1, 0, 3],
    "proj": [1, 0, 3, 2],
    "query": [0, 1, 2, 3],
    "key": [1, 0, 3, 2],
    "value": [0, 1, 2, 3],
}

CHAIN = dict(
    text=("text_own", "k_cross"), tokens=("tokens", "q_self"), self=("q_self", "attn_own"),
    norm_two=("attn_own", "n2_own"), cross=("n2_own", "cross_own"),
    norm_three=("cross_own", "n3_own"), units=("n3_own", "grad_up"),
    back_units=("grad_up", "gn3_own"), back_three=("gn3_own", "g_cross_own"),
    out=("activated", "ff_own"), result=("ff_own", "out"), back_cross=("g_cross_own", "gn2_own"),
    back_two=("gn2_own", "g_attn_own"), back_self=("g_attn_own", "gn1_own"),
    back_one=("gn1_own", "d_tokens"), text_grad=("text_grad_own", "d_text"),
)

STAGES = dict(
    text=stage_text, tokens=stage_tokens, self=stage_self, norm_two=stage_norm_two,
    cross=stage_cross, norm_three=stage_norm_three, units=stage_units,
    back_units=stage_back_units, back_three=stage_back_three, out=stage_out,
    result=stage_result, back_cross=stage_back_cross, cross_packet=stage_cross_packet, proj_packet=stage_proj_packet,
    query_packet=stage_query_packet, key_packet=stage_key_packet,
    value_packet=stage_value_packet,
    back_two=stage_back_two, back_self=stage_back_self,
    back_one=stage_back_one, text_grad=stage_text_grad,
    small=stage_small, hop=stage_hop, rms=stage_rms, end=stage_end,
)

PLAN = [
    ("do", "tokens"), ("do", "self"), ("do", "text"), ("do", "norm_two"), ("do", "cross"),
    ("do", "norm_three"), ("do", "units"), ("send", "rest"), ("send", "up"), ("send", "down"),
    ("do", "back_units"), ("do", "back_three"), ("do", "back_cross"), ("take", "down"),
    ("take", "rest"), ("take", "up"), ("do", "cross_packet"), ("do", "back_two"),
    ("send", "rest"), ("send", "up"), ("send", "cross"), ("send", "down"), ("do", "back_self"),
    ("take", "rest"), ("take", "up"), ("take", "down"), ("take", "cross"), ("do", "proj_packet"),
    ("do", "query_packet"), ("do", "key_packet"), ("do", "value_packet"), ("send", "rest"),
    ("send", "up"), ("send", "proj"), ("send", "cross"), ("send", "key"), ("send", "query"),
    ("send", "value"), ("send", "down"), ("take", "rest"), ("send", "rest"), ("do", "out"),
    ("do", "back_one"), ("take", "up"), ("send", "up"), ("take", "query"), ("take", "rest"),
    ("send", "rest"), ("take", "proj"), ("send", "proj"), ("send", "query"), ("take", "value"),
    ("take", "up"), ("send", "up"), ("do", "result"), ("take", "cross"), ("send", "cross"),
    ("send", "value"), ("take", "rest"), ("send", "rest"), ("take", "proj"), ("send", "proj"),
    ("take", "up"), ("send", "up"), ("take", "key"), ("send", "key"), ("take", "cross"),
    ("send", "cross"), ("take", "down"), ("take", "rest"), ("send", "rest"), ("send", "down"),
    ("take", "query"), ("take", "proj"), ("send", "proj"), ("take", "key"), ("take", "up"),
    ("send", "up"), ("send", "key"), ("take", "value"), ("take", "cross"), ("send", "cross"),
    ("take", "down"), ("send", "query"), ("take", "proj"), ("send", "proj"), ("take", "rest"),
    ("send", "rest"), ("take", "key"), ("send", "key"), ("take", "query"), ("send", "value"),
    ("take", "cross"), ("send", "cross"), ("send", "query"), ("take", "proj"), ("send", "proj"),
    ("take", "up"), ("send", "up"), ("take", "key"), ("send", "key"), ("take", "value"),
    ("send", "value"), ("take", "query"), ("send", "query"), ("take", "cross"),
    ("send", "cross"), ("take", "key"), ("send", "key"), ("take", "proj"), ("send", "proj"),
    ("send", "down"), ("take", "value"), ("send", "value"), ("take", "query"), ("send", "query"),
    ("take", "key"), ("send", "key"), ("take", "rest"), ("take", "down"), ("send", "down"),
    ("take", "value"), ("send", "value"), ("take", "query"), ("send", "query"),
    ("take", "cross"), ("send", "cross"), ("take", "up"), ("take", "value"), ("send", "value"),
    ("take", "down"), ("send", "down"), ("take", "proj"), ("send", "proj"), ("take", "query"),
    ("send", "query"), ("take", "key"), ("send", "key"), ("take", "value"), ("send", "value"),
    ("do", "text_grad"), ("take", "down"), ("send", "down"), ("do", "small"), ("do", "hop"),
    ("take", "cross"), ("do", "hop"), ("take", "query"), ("take", "proj"), ("do", "hop"),
    ("do", "hop"), ("do", "rms"), ("take", "value"), ("take", "key"), ("take", "down"),
    ("do", "end"),
]

NAMES = (
    "tokens", "text_own", "text_len", "frame_valid", "gain_one", "bias_one", "gain_two",
    "bias_two", "gain_three", "bias_three", "w_query", "w_key", "w_value", "w_out", "c_query",
    "c_key", "c_value", "c_out", "w_up", "w_down", "grad_own",
)


def per_device(*args):
    given = dict(zip(NAMES, args))
    for name in NAMES[4:10]:
        given[name] = given[name].reshape(1, -1)
    p = Program(given)
    p.rank = lax.axis_index("mp").astype(jnp.int32).reshape(1)
    p.main, p.extra = main_bits()
    place = lax.axis_index("dp")
    p.block = sum(((place >> bit) & 1) << k for k, bit in enumerate(p.main))
    p.block = p.block.astype(jnp.int32).reshape(1)
    v = p.v
    v["text_other"] = swap_cores(v["text_own"])
    v["grad_other"] = swap_cores(v["grad_own"])
    for kind, name in PLAN:
        if kind == "do":
            before, after = CHAIN.get(name, (None, None))
            if before:
                v[before] = p.tie(v[before])
            STAGES[name](p)
            if after:
                v[after] = p.tie(v[after])
        elif kind == "send":
            p.start(name)
        else:
            p.finish(name)
    return (
        v["out"],
        v["d_tokens"],
        v["d_text"],
        *(v["small"][n] for n in range(6)),
        *(v["d_" + name] for name in NAMES[10:20]),
        v["rms"],
    )


def solution(mesh):
    split = P("dp", "mp", None)
    columns, rows = P(None, "mp"), P("mp", None)
    weights = (columns,) * 3 + (rows,) + (columns,) * 3 + (rows, columns, rows)
    return jax.shard_map(
        per_device,
        mesh=mesh,
        in_specs=(P("dp", None, None), split, P("dp"), P("dp"))
        + (P(),) * 6
        + weights
        + (split,),
        out_specs=(split,) * 3 + (P(),) * 6 + weights + (P(),),
        check_vma=False,
    )
```

time: 1300 us -> 435 us (0.33)
  waiting for transfers between devices: 890 us -> 168 us
  matrix products: 160 us -> 0 us
  Pallas kernels: 0 us -> 148 us
  other arithmetic: 89.7 us -> 10.8 us
  starting transfers between devices: 1.87 us -> 80.5 us
  local copies, waits for them, and re-layouts: 82.6 us -> 16 us
  blocking collectives: 48.5 us -> 0 us
    psum x1 -> x0, waiting for transfers between devices: 811 us -> none  [per_device(): lax.psum((d_w_joined, d_w_out, d_c_query, d_c_joined, d_c_out, d_w_up, d_...]
    ppermute x0 -> x82, waiting for transfers between devices: none -> 168 us  [the longest x68 157 us: exchange(): return lax.ppermute(values, 'dp', pairs)]
    dot_general x49 -> x0, matrix products: 160 us -> none  [the longest x7 41.1 us: project_back(): jnp.einsum('bfe,de->bfd', gradients, weight, preferred_element_type=jnp.f...]
    pallas_call x0 -> x28, Pallas kernels: none -> 148 us  [the longest x15 111 us: call(): pl.pallas_call(body, grid=grid, in_specs=in_specs, out_specs=out_specs, o...]
    ppermute x0 -> x82, starting transfers between devices: none -> 80.5 us  [the longest x68 77.7 us: exchange(): return lax.ppermute(values, 'dp', pairs)]
    reduce_scatter x7 -> x0, waiting for transfers between devices: 49.2 us -> none  [the longest x1 13.8 us: per_device(): lax.psum_scatter(project(activated, w_down).astype(jnp.bfloat16), 'mp', s...]
    psum x1 -> x0, blocking collectives: 46.2 us -> none  [per_device(): lax.psum((d_gain_one, d_bias_one, d_gain_two, d_bias_two, d_gain_three, d...]
    convert_element_type x18 -> x32, other arithmetic: 43.8 us -> 4.89 us  [add_rounded(): return (one.astype(F32) + two.astype(F32)).astype(BF16)]
  transfers between devices with their start and end apart: 13 -> 82, of which waited for: 10 -> 39; matrix products, arithmetic and copies ran while one was open for 12% -> 3% of each run, Pallas kernels for 0% -> 21%
where the time goes in v2:
time: 435 us; the launch traced here: 427 us
  waiting for transfers between devices  168 us (39%)
  Pallas kernels  148 us (34%)
  starting transfers between devices  80.5 us (19%)
  local copies, waits for them, and re-layouts  16 us (4%)
  other arithmetic  10.8 us (2%)
    ppermute x68, waiting for transfers between devices, exchange(): return lax.ppermute(values, 'dp', pairs)  157 us
    pallas_call x15, Pallas kernels, call(): pl.pallas_call(body, grid=grid, in_specs=in_specs, out_specs=out_specs, o...  111 us
    ppermute x68, starting transfers between devices, exchange(): return lax.ppermute(values, 'dp', pairs)  77.7 us
    pallas_call x8, Pallas kernels, open_packet(): pl.pallas_call(body, grid=(steps,), in_specs=[SMEM_SPEC, whole(kept.shape...  24.1 us
    unnamed x142, local copies, waits for them, and re-layouts  13.3 us
    ppermute x14, waiting for transfers between devices, swap_cores(): return lax.ppermute(values, 'mp', SWAP)  11.1 us
  transfers between devices with their start and end apart: 82, of which 39 were waited for; matrix products, arithmetic and copies ran while one was open for 3% of the time, Pallas kernels for 21%

profile of v2, /device:TPU:0, one launch (start us, length us, event | category | flops | bytes accessed | tf_op | source)
XLA Modules:
  0.0 426.9 jit_solution(2078267702606740759)
XLA Ops:
  7.3 5.0 %shard_map.356 = (bf16[1024,1024]{1,0:T(8,128)(2,1)S(1)}, bf16[1024,512]{1,0:T(8,128)(2,1)S(1)}, bf16[1024,512]{1,0:T(8,128)(2,1)S(1)}, bf16[1024,512]{1,0:T(8,128)(2,1)S(1)}) custom-call(bf16[1024,1024]{1,0:T(8,128)(2,1)S(1)} %bitcast.36, bf16[1,1024]{1,0:T(2,128)(2,1)S(1)} %reshape.142.g, bf16[1,1024]{1,0:T(2,128)(2,1)S(1)} %reshape.143.b, ...), custom_call_target="tpu_custom_call" | custom-call | bytes 1024 | tf_op jit(solution)/shard_map/pallas_call | solution.py:54
  13.7 8.1 %shard_map.357 = (bf16[2,2,256,512]{3,2,1,0:T(8,128)(2,1)S(1)}, f32[2,8,512]{2,1,0:T(8,128)S(1)}, f32[2,256,1024]{2,1,0:T(8,128)S(1)}, bf16[2,256,1024]{2,1,0:T(8,128)(2,1)S(1)}) custom-call(s32[1]{0:T(128)} %bitcast.rank_ref, s32[2]{0:T(128)S(1)} %copy-done.56, bf16[2,512,512]{2,1,0:T(8,128)(2,1)S(1)} %bitcast.37, bf16[2,512,512]{2,1,0:T(8,128)(2,1)S(1)} %bitcast.39, ...), custom_call_target="tpu_custom_call" | custom-call | bytes 1024 | tf_op jit(solution)/shard_map/pallas_call | solution.py:54
  30.9 7.7 %shard_map.360 = (bf16[2,2,256,512]{3,2,1,0:T(8,128)(2,1)S(1)}, bf16[2,2,256,512]{3,2,1,0:T(8,128)(2,1)S(1)}, f32[2,8,512]{2,1,0:T(8,128)S(1)}, f32[2,256,1024]{2,1,0:T(8,128)S(1)}, bf16[2,256,1024]{2,1,0:T(8,128)(2,1)S(1)}) custom-call(s32[1]{0:T(128)} %bitcast.rank_ref, s32[2]{0:T(128)S(1)} %copy-done.65, ...), custom_call_target="tpu_custom_call" | custom-call | bytes 1024 | tf_op jit(solution)/shard_map/pallas_call | solution.py:54
  49.0 24.9 %shard_map.362 = (bf16[2,512,2048]{2,1,0:T(8,128)(2,1)}, bf16[2,512,2048]{2,1,0:T(8,128)(2,1)}, bf16[8,128,512]{2,1,0:T(8,128)(2,1)S(1)}, bf16[8,128,512]{2,1,0:...) custom-call(s32[1]{0:T(128)} %bitcast.5.me_ref.refs_0_, ...), custom_call_target="tpu_custom_call" | custom-call | bytes 1024 | tf_op jit(solution)/shard_map/pallas_call | solution.py:54
  76.1 5.0 %shard_map.363 = (f32[512,1024]{1,0:T(8,128)S(1)}, bf16[512,1024]{1,0:T(8,128)(2,1)S(1)}) custom-call(bf16[2,512,2048]{2,1,0:T(8,128)(2,1)S(1)} %copy-done.24, bf16[1024,2048]{1,0:T(8,128)(2,1)S(1)} %copy-done.4), custom_call_target="tpu_custom_call" | custom-call | bytes 1024 | tf_op jit(solution)/shard_map/pallas_call | solution.py:54
  91.7 18.1 %shard_map.365 = (bf16[2,2,256,512]{3,2,1,0:T(8,128)(2,1)S(1)}, bf16[2,2,128,512]{3,2,1,0:T(8,128)(2,1)S(1)}, bf16[2,2,128,512]{3,2,1,0:T(8,128)(2,1)S(1)}, f32[...) custom-call(s32[1]{0:T(128)} %bitcast.rank_ref, ...), custom_call_target="tpu_custom_call" | custom-call | bytes 1024 | tf_op jit(solution)/shard_map/pallas_call | solution.py:54
  119.5 7.0 %collective-permute-done.10 = bf16[8,192,512]{2,1,0:T(8,128)(2,1)S(1)} collective-permute-done((bf16[8,192,512]{2,1,0:T(8,128)(2,1)S(1)}, bf16[8,192,512]{2,1,0:T(8,128)(2,1)S(1)}, u32[]{:S(2)}, u32[]{:S(2)}) %collective-permute-start.10) | collective-permute-done | bytes 1572896 | tf_op jit(solution)/shard_map/ppermute | solution.py:804
  138.6 20.9 %shard_map.368 = (bf16[2,512,512]{2,1,0:T(8,128)(2,1)S(1)}, bf16[2,512,512]{2,1,0:T(8,128)(2,1)S(1)}, bf16[2,512,512]{2,1,0:T(8,128)(2,1)S(1)}, f32[2,256,1024]{2,1,0:T(8,128)S(1)}, bf16[2,256,1024]{2,1,0:T(8,128)(2,1)S(1)}) custom-call(s32[1]{0:T(128)} %bitcast.rank_ref, s32[2]{0:T(128)S(1)} %copy-done.56, ...), custom_call_target="tpu_custom_call" | custom-call | bytes 1024 | tf_op jit(solution)/shard_map/pallas_call | solution.py:54
  160.0 5.7 %collective-permute-done.15 = bf16[4,128,512]{2,1,0:T(8,128)(2,1)S(1)} collective-permute-done((bf16[4,128,512]{2,1,0:T(8,128)(2,1)}, bf16[4,128,512]{2,1,0:T(8,128)(2,1)S(1)}, u32[]{:S(2)}, u32[]{:S(2)}) %collective-permute-start.15) | collective-permute-done | bytes 524320 | tf_op jit(solution)/shard_map/ppermute | solution.py:804
  181.6 8.0 %collective-permute-done.17 = bf16[2,192,512]{2,1,0:T(8,128)(2,1)S(1)} collective-permute-done((bf16[2,192,512]{2,1,0:T(8,128)(2,1)S(1)}, bf16[2,192,512]{2,1,0:T(8,128)(2,1)S(1)}, u32[]{:S(2)}, u32[]{:S(2)}) %collective-permute-start.17) | collective-permute-done | bytes 393248 | tf_op jit(solution)/shard_map/ppermute | solution.py:804
  191.1 5.1 %shard_map.373 = (f32[512,1024]{1,0:T(8,128)S(1)}, bf16[512,1024]{1,0:T(8,128)(2,1)S(1)}) custom-call(bf16[2,512,2048]{2,1,0:T(8,128)(2,1)S(1)} %copy-done.23, bf16[2048,1024]{1,0:T(8,128)(2,1)S(1)} %copy-done.5), custom_call_target="tpu_custom_call" | custom-call | bytes 1024 | tf_op jit(solution)/shard_map/pallas_call | solution.py:54
  202.5 7.5 %collective-permute-done.24 = bf16[1,192,512]{2,1,0:T(8,128)(2,1)S(1)} collective-permute-done((bf16[1,192,512]{2,1,0:T(8,128)(2,1)S(1)}, bf16[1,192,512]{2,1,0:T(8,128)(2,1)S(1)}, u32[]{:S(2)}, u32[]{:S(2)}) %collective-permute-start.24) | collective-permute-done | bytes 196640 | tf_op jit(solution)/shard_map/ppermute | solution.py:804
  212.8 10.1 %collective-permute-done.20 = bf16[1,192,512]{2,1,0:T(8,128)(2,1)S(1)} collective-permute-done((bf16[1,192,512]{2,1,0:T(8,128)(2,1)S(1)}, bf16[1,192,512]{2,1,0:T(8,128)(2,1)S(1)}, u32[]{:S(2)}, u32[]{:S(2)}) %collective-permute-start.20) | collective-permute-done | bytes 196640 | tf_op jit(solution)/shard_map/ppermute | solution.py:804
  225.4 12.3 %collective-permute-done.26 = bf16[4,160,512]{2,1,0:T(8,128)(2,1)S(1)} collective-permute-done((bf16[4,160,512]{2,1,0:T(8,128)(2,1)S(1)}, bf16[4,160,512]{2,1,0:T(8,128)(2,1)S(1)}, u32[]{:S(2)}, u32[]{:S(2)}) %collective-permute-start.26) | collective-permute-done | bytes 655392 | tf_op jit(solution)/shard_map/ppermute | solution.py:804
  240.3 6.5 %collective-permute-done.29 = bf16[1,192,512]{2,1,0:T(8,128)(2,1)S(1)} collective-permute-done((bf16[1,192,512]{2,1,0:T(8,128)(2,1)S(1)}, bf16[1,192,512]{2,1,0:T(8,128)(2,1)S(1)}, u32[]{:S(2)}, u32[]{:S(2)}) %collective-permute-start.29) | collective-permute-done | bytes 196640 | tf_op jit(solution)/shard_map/ppermute | solution.py:804
  247.0 8.7 %collective-permute-done.36 = bf16[2,160,512]{2,1,0:T(8,128)(2,1)S(1)} collective-permute-done((bf16[2,160,512]{2,1,0:T(8,128)(2,1)S(1)}, bf16[2,160,512]{2,1,0:T(8,128)(2,1)S(1)}, u32[]{:S(2)}, u32[]{:S(2)}) %collective-permute-start.36) | collective-permute-done | bytes 327712 | tf_op jit(solution)/shard_map/ppermute | solution.py:804
  260.8 9.0 %collective-permute-done.33 = bf16[2,128,512]{2,1,0:T(8,128)(2,1)S(1)} collective-permute-done((bf16[2,128,512]{2,1,0:T(8,128)(2,1)S(1)}, bf16[2,128,512]{2,1,0:T(8,128)(2,1)S(1)}, u32[]{:S(2)}, u32[]{:S(2)}) %collective-permute-start.33) | collective-permute-done | bytes 262176 | tf_op jit(solution)/shard_map/ppermute | solution.py:804
  271.8 5.4 %collective-permute-done.38 = bf16[2,192,512]{2,1,0:T(8,128)(2,1)S(1)} collective-permute-done((bf16[2,192,512]{2,1,0:T(8,128)(2,1)S(1)}, bf16[2,192,512]{2,1,0:T(8,128)(2,1)S(1)}, u32[]{:S(2)}, u32[]{:S(2)}) %collective-permute-start.38) | collective-permute-done | bytes 393248 | tf_op jit(solution)/shard_map/ppermute | solution.py:804
  293.1 4.6 %collective-permute-done.42 = bf16[2,64,512]{2,1,0:T(8,128)(2,1)S(1)} collective-permute-done((bf16[2,64,512]{2,1,0:T(8,128)(2,1)S(1)}, bf16[2,64,512]{2,1,0:T(8,128)(2,1)S(1)}, u32[]{:S(2)}, u32[]{:S(2)}) %collective-permute-start.42) | collective-permute-done | bytes 131104 | tf_op jit(solution)/shard_map/ppermute | solution.py:804
  311.4 6.0 %collective-permute-done.53 = bf16[2,160,512]{2,1,0:T(8,128)(2,1)S(1)} collective-permute-done((bf16[2,160,512]{2,1,0:T(8,128)(2,1)S(1)}, bf16[2,160,512]{2,1,0:T(8,128)(2,1)S(1)}, u32[]{:S(2)}, u32[]{:S(2)}) %collective-permute-start.53) | collective-permute-done | bytes 327712 | tf_op jit(solution)/shard_map/ppermute | solution.py:804
  320.5 7.3 %collective-permute-done.50 = bf16[1,64,512]{2,1,0:T(8,128)(2,1)S(1)} collective-permute-done((bf16[1,64,512]{2,1,0:T(8,128)(2,1)S(1)}, bf16[1,64,512]{2,1,0:T(8,128)(2,1)S(1)}, u32[]{:S(2)}, u32[]{:S(2)}) %collective-permute-start.50) | collective-permute-done | bytes 65568 | tf_op jit(solution)/shard_map/ppermute | solution.py:804
  333.7 9.3 %collective-permute-done.57.refs_2_ = bf16[8,192,512]{2,1,0:T(8,128)(2,1)S(1)} collective-permute-done((bf16[8,192,512]{2,1,0:T(8,128)(2,1)S(1)}, bf16[8,192,512]{2,1,0:T(8,128)(2,1)S(1)}, u32[]{:S(2)}, u32[]{:S(2)}) %collective-permute-start.57) | collective-permute-done | bytes 1572896 | tf_op jit(solution)/shard_map/ppermute | solution.py:804
  348.6 5.1 %collective-permute-start.63 = (bf16[2,64,512]{2,1,0:T(8,128)(2,1)S(1)}, bf16[2,64,512]{2,1,0:T(8,128)(2,1)S(1)}, u32[]{:S(2)}, u32[]{:S(2)}) collective-permute-start(bf16[2,64,512]{2,1,0:T(8,128)(2,1)S(1)} %pad_maximum_fusion.22), channel_id=1, source_target_pairs={{0,8},{2,10},{4,12},{6,14},{8,0},{10,2},{12,4},{14,6},{16,24},{18,... | collective-permute-start | bytes 393224 | tf_op jit(solution)/shard_map/ppermute | solution.py:804
  369.3 7.0 %collective-permute-done.66 = bf16[4,64,512]{2,1,0:T(8,128)(2,1)S(1)} collective-permute-done((bf16[4,64,512]{2,1,0:T(8,128)(2,1)S(1)}, bf16[4,64,512]{2,1,0:T(8,128)(2,1)S(1)}, u32[]{:S(2)}, u32[]{:S(2)}) %collective-permute-start.66) | collective-permute-done | bytes 262176 | tf_op jit(solution)/shard_map/ppermute | solution.py:804
  (387 shorter events, 208.6 us)
Async XLA Ops:
  81.6 37.5 %collective-permute-start.6 = (bf16[8,192,512]{2,1,0:T(8,128)(2,1)S(1)}, bf16[8,192,512]{2,1,0:T(8,128)(2,1)S(1)}, u32[]{:S(2)}, u32[]{:S(2)}) collective-permute-start(bf16[8,192,512]{2,1,0:T(8,128)(2,1)S(1)} %get-tuple-element.528), channel_id=1, source_target_pairs={{0,4},{2,6},{4,0},{6,2},{8,12},{10,14},{12,8},{14,10},{16,20},{18,... | collective-permute-start | bytes 4718600 | tf_op jit(solution)/shard_map/ppermute | solution.py:804
  87.5 26.3 %collective-permute-start.7 = (bf16[8,128,512]{2,1,0:T(8,128)(2,1)S(1)}, bf16[8,128,512]{2,1,0:T(8,128)(2,1)S(1)}, u32[]{:S(2)}, u32[]{:S(2)}) collective-permute-start(bf16[8,128,512]{2,1,0:T(8,128)(2,1)S(1)} %get-tuple-element.534), channel_id=1, source_target_pairs={{0,8},{2,10},{4,12},{6,14},{8,0},{10,2},{12,4},{14,6},{16,24},{18,... | collective-permute-start | bytes 3145736 | tf_op jit(solution)/shard_map/ppermute | solution.py:804
  90.1 36.4 %collective-permute-start.10 = (bf16[8,192,512]{2,1,0:T(8,128)(2,1)S(1)}, bf16[8,192,512]{2,1,0:T(8,128)(2,1)S(1)}, u32[]{:S(2)}, u32[]{:S(2)}) collective-permute-start(bf16[8,192,512]{2,1,0:T(8,128)(2,1)S(1)} %get-tuple-element.559), channel_id=1, source_target_pairs={{0,2},{2,0},{4,6},{6,4},{8,10},{10,8},{12,14},{14,12},{16,18},{18,... | collective-permute-start | bytes 4718600 | tf_op jit(solution)/shard_map/ppermute | solution.py:804
  109.8 22.5 %collective-permute-start.11 = (bf16[2,256,1024]{2,1,0:T(8,128)(2,1)S(1)}, bf16[2,256,1024]{2,1,0:T(8,128)(2,1)S(1)}, u32[]{:S(2)}, u32[]{:S(2)}) collective-permute-start(bf16[2,256,1024]{2,1,0:T(8,128)(2,1)S(1)} %get-tuple-element.571), channel_id=1, source_target_pairs={{0,1},{1,0},{2,3},{3,2},{4,5},{5,4},{6,7},{7,6},{8,9},{9,8},{10,11... | collective-permute-start | bytes 3145736 | tf_op jit(solution)/shard_map/ppermute | solution.py:815
  134.5 25.1 %collective-permute-start.12 = (bf16[4,192,512]{2,1,0:T(8,128)(2,1)S(1)}, bf16[4,192,512]{2,1,0:T(8,128)(2,1)S(1)}, u32[]{:S(2)}, u32[]{:S(2)}) collective-permute-start(bf16[4,192,512]{2,1,0:T(8,128)(2,1)S(1)} %get-tuple-element.576), channel_id=1, source_target_pairs={{0,2},{2,0},{4,6},{6,4},{8,10},{10,8},{12,14},{14,12},{16,18},{18,... | collective-permute-start | bytes 2359304 | tf_op jit(solution)/shard_map/ppermute | solution.py:804
  136.0 30.8 %collective-permute-start.14 = (bf16[8,160,512]{2,1,0:T(8,128)(2,1)S(1)}, bf16[8,160,512]{2,1,0:T(8,128)(2,1)S(1)}, u32[]{:S(2)}, u32[]{:S(2)}) collective-permute-start(bf16[8,160,512]{2,1,0:T(8,128)(2,1)S(1)} %get-tuple-element.596), channel_id=1, source_target_pairs={{0,8},{2,10},{4,12},{6,14},{8,0},{10,2},{12,4},{14,6},{16,24},{18,... | collective-permute-start | bytes 3932168 | tf_op jit(solution)/shard_map/ppermute | solution.py:804
  136.5 23.3 %collective-permute-start.16 = (bf16[4,192,512]{2,1,0:T(8,128)(2,1)S(1)}, bf16[4,192,512]{2,1,0:T(8,128)(2,1)S(1)}, u32[]{:S(2)}, u32[]{:S(2)}) collective-permute-start(bf16[4,192,512]{2,1,0:T(8,128)(2,1)S(1)} %get-tuple-element.598), channel_id=1, source_target_pairs={{0,4},{2,6},{4,0},{6,2},{8,12},{10,14},{12,8},{14,10},{16,20},{18,... | collective-permute-start | bytes 2359304 | tf_op jit(solution)/shard_map/ppermute | solution.py:804
  138.0 27.7 %collective-permute-start.15 = (bf16[4,128,512]{2,1,0:T(8,128)(2,1)}, bf16[4,128,512]{2,1,0:T(8,128)(2,1)S(1)}, u32[]{:S(2)}, u32[]{:S(2)}) collective-permute-start(bf16[4,128,512]{2,1,0:T(8,128)(2,1)} %get-tuple-element.597), channel_id=1, source_target_pairs={{0,2},{2,0},{4,6},{6,4},{8,10},{10,8},{12,14},{14,12},{16,18},{18,... | collective-permute-start | bytes 1572872 | tf_op jit(solution)/shard_map/ppermute | solution.py:804
  165.7 30.6 %collective-permute-start.19 = (bf16[2,256,1024]{2,1,0:T(8,128)(2,1)S(1)}, bf16[2,256,1024]{2,1,0:T(8,128)(2,1)S(1)}, u32[]{:S(2)}, u32[]{:S(2)}) collective-permute-start(bf16[2,256,1024]{2,1,0:T(8,128)(2,1)S(1)} %get-tuple-element.656), channel_id=1, source_target_pairs={{0,1},{1,0},{2,3},{3,2},{4,5},{5,4},{6,7},{7,6},{8,9},{9,8},{10,11... | collective-permute-start | bytes 3145736 | tf_op jit(solution)/shard_map/ppermute | solution.py:815
  179.5 31.2 %collective-permute-start.23 = (bf16[8,128,512]{2,1,0:T(8,128)(2,1)S(1)}, bf16[8,128,512]{2,1,0:T(8,128)(2,1)S(1)}, u32[]{:S(2)}, u32[]{:S(2)}) collective-permute-start(bf16[8,128,512]{2,1,0:T(8,128)(2,1)S(1)} %get-tuple-element.673), channel_id=1, source_target_pairs={{0,4},{2,6},{4,0},{6,2},{8,12},{10,14},{12,8},{14,10},{16,20},{18,... | collective-permute-start | bytes 3145736 | tf_op jit(solution)/shard_map/ppermute | solution.py:804
  189.5 66.5 %collective-permute-start.35 = (bf16[2,128,512]{2,1,0:T(8,128)(2,1)S(1)}, bf16[2,128,512]{2,1,0:T(8,128)(2,1)S(1)}, u32[]{:S(2)}, u32[]{:S(2)}) collective-permute-start(bf16[2,128,512]{2,1,0:T(8,128)(2,1)S(1)} %get-tuple-element.723), channel_id=1, source_target_pairs={{0,4},{2,6},{4,0},{6,2},{8,12},{10,14},{12,8},{14,10},{16,20},{18,... | collective-permute-start | bytes 786440 | tf_op jit(solution)/shard_map/ppermute | solution.py:804
  210.0 36.8 %collective-permute-start.28 = (bf16[8,64,512]{2,1,0:T(8,128)(2,1)S(1)}, bf16[8,64,512]{2,1,0:T(8,128)(2,1)S(1)}, u32[]{:S(2)}, u32[]{:S(2)}) collective-permute-start(bf16[8,64,512]{2,1,0:T(8,128)(2,1)S(1)} %get-tuple-element.704), channel_id=1, source_target_pairs={{0,4},{2,6},{4,0},{6,2},{8,12},{10,14},{12,8},{14,10},{16,20},{18,... | collective-permute-start | bytes 1572872 | tf_op jit(solution)/shard_map/ppermute | solution.py:804
  210.7 27.1 %collective-permute-start.26 = (bf16[4,160,512]{2,1,0:T(8,128)(2,1)S(1)}, bf16[4,160,512]{2,1,0:T(8,128)(2,1)S(1)}, u32[]{:S(2)}, u32[]{:S(2)}) collective-permute-start(bf16[4,160,512]{2,1,0:T(8,128)(2,1)S(1)} %get-tuple-element.697), channel_id=1, source_target_pairs={{0,4},{2,6},{4,0},{6,2},{8,12},{10,14},{12,8},{14,10},{16,20},{18,... | collective-permute-start | bytes 1966088 | tf_op jit(solution)/shard_map/ppermute | solution.py:804
  238.8 40.0 %collective-permute-start.27 = (bf16[4,64,512]{2,1,0:T(8,128)(2,1)S(1)}, bf16[4,64,512]{2,1,0:T(8,128)(2,1)S(1)}, u32[]{:S(2)}, u32[]{:S(2)}) collective-permute-start(bf16[4,64,512]{2,1,0:T(8,128)(2,1)S(1)} %get-tuple-element.702), channel_id=1, source_target_pairs={{0,4},{2,6},{4,0},{6,2},{8,12},{10,14},{12,8},{14,10},{16,20},{18,... | collective-permute-start | bytes 786440 | tf_op jit(solution)/shard_map/ppermute | solution.py:804
  305.7 37.3 %collective-permute-start.57 = (bf16[8,192,512]{2,1,0:T(8,128)(2,1)S(1)}, bf16[8,192,512]{2,1,0:T(8,128)(2,1)S(1)}, u32[]{:S(2)}, u32[]{:S(2)}) collective-permute-start(bf16[8,192,512]{2,1,0:T(8,128)(2,1)S(1)} %pad_maximum_fusion.refs_1_), channel_id=1, source_target_pairs={{0,4},{2,6},{4,0},{6,2},{8,12},{10,14},{12,8},{14,10},{16,20},{18,... | collective-permute-start | bytes 4718600 | tf_op jit(solution)/shard_map/ppermute | solution.py:804
  309.9 49.7 %collective-permute-start.61 = (bf16[8,192,512]{2,1,0:T(8,128)(2,1)S(1)}, bf16[8,192,512]{2,1,0:T(8,128)(2,1)S(1)}, u32[]{:S(2)}, u32[]{:S(2)}) collective-permute-start(bf16[8,192,512]{2,1,0:T(8,128)(2,1)S(1)} %pad_maximum_fusion.1.refs_1_), channel_id=1, source_target_pairs={{0,2},{2,0},{4,6},{6,4},{8,10},{10,8},{12,14},{14,12},{16,18},{18,... | collective-permute-start | bytes 4718600 | tf_op jit(solution)/shard_map/ppermute | solution.py:804
  327.8 29.2 %collective-permute-start.62 = (bf16[4,160,512]{2,1,0:T(8,128)(2,1)S(1)}, bf16[4,160,512]{2,1,0:T(8,128)(2,1)S(1)}, u32[]{:S(2)}, u32[]{:S(2)}) collective-permute-start(bf16[4,160,512]{2,1,0:T(8,128)(2,1)S(1)} %pad_maximum_fusion.7), channel_id=1, source_target_pairs={{0,4},{2,6},{4,0},{6,2},{8,12},{10,14},{12,8},{14,10},{16,20},{18,... | collective-permute-start | bytes 1966088 | tf_op jit(solution)/shard_map/ppermute | solution.py:804
  333.7 49.6 %collective-permute-start.69 = (bf16[2,128,768]{2,1,0:T(8,128)(2,1)S(1)}, bf16[2,128,768]{2,1,0:T(8,128)(2,1)S(1)}, u32[]{:S(2)}, u32[]{:S(2)}) collective-permute-start(bf16[2,128,768]{2,1,0:T(8,128)(2,1)S(1)} %get-tuple-element.887), channel_id=1, source_target_pairs={{0,1},{1,0},{2,3},{3,2},{4,5},{5,4},{6,7},{7,6},{8,9},{9,8},{10,11... | collective-permute-start | bytes 1179656 | tf_op jit(solution)/shard_map/ppermute | solution.py:815
  363.9 31.8 %collective-permute-start.73 = (bf16[8,160,512]{2,1,0:T(8,128)(2,1)S(1)}, bf16[8,160,512]{2,1,0:T(8,128)(2,1)}, u32[]{:S(2)}, u32[]{:S(2)}) collective-permute-start(bf16[8,160,512]{2,1,0:T(8,128)(2,1)S(1)} %pad_maximum_fusion.2.refs_1_), channel_id=1, source_target_pairs={{0,8},{2,10},{4,12},{6,14},{8,0},{10,2},{12,4},{14,6},{16,24},{18,... | collective-permute-start | bytes 3932168 | tf_op jit(solution)/shard_map/ppermute | solution.py:804
  378.1 22.6 %collective-permute-start.76 = (bf16[8,64,512]{2,1,0:T(8,128)(2,1)}, bf16[8,64,512]{2,1,0:T(8,128)(2,1)}, u32[]{:S(2)}, u32[]{:S(2)}) collective-permute-start(bf16[8,64,512]{2,1,0:T(8,128)(2,1)} %pad_maximum_fusion.10.refs_1_), channel_id=1, source_target_pairs={{0,2},{2,0},{4,6},{6,4},{8,10},{10,8},{12,14},{14,12},{16,18},{18,... | collective-permute-start | bytes 1572872 | tf_op jit(solution)/shard_map/ppermute | solution.py:804
  381.9 22.9 %collective-permute-start.75 = (bf16[8,128,512]{2,1,0:T(8,128)(2,1)S(1)}, bf16[8,128,512]{2,1,0:T(8,128)(2,1)}, u32[]{:S(2)}, u32[]{:S(2)}) collective-permute-start(bf16[8,128,512]{2,1,0:T(8,128)(2,1)S(1)} %pad_maximum_fusion.3.refs_1_), channel_id=1, source_target_pairs={{0,4},{2,6},{4,0},{6,2},{8,12},{10,14},{12,8},{14,10},{16,20},{18,... | collective-permute-start | bytes 3145736 | tf_op jit(solution)/shard_map/ppermute | solution.py:804
  386.4 35.9 %collective-permute-start.81 = (bf16[8,128,512]{2,1,0:T(8,128)(2,1)S(1)}, bf16[8,128,512]{2,1,0:T(8,128)(2,1)}, u32[]{:S(2)}, u32[]{:S(2)}) collective-permute-start(bf16[8,128,512]{2,1,0:T(8,128)(2,1)S(1)} %pad_maximum_fusion.4.refs_1_), channel_id=1, source_target_pairs={{0,8},{2,10},{4,12},{6,14},{8,0},{10,2},{12,4},{14,6},{16,24},{18,... | collective-permute-start | bytes 3145736 | tf_op jit(solution)/shard_map/ppermute | solution.py:804
  393.8 22.8 %collective-permute-start.80 = (bf16[8,64,512]{2,1,0:T(8,128)(2,1)}, bf16[8,64,512]{2,1,0:T(8,128)(2,1)S(1)}, u32[]{:S(2)}, u32[]{:S(2)}) collective-permute-start(bf16[8,64,512]{2,1,0:T(8,128)(2,1)} %pad_maximum_fusion.12.refs_1_), channel_id=1, source_target_pairs={{0,2},{2,0},{4,6},{6,4},{8,10},{10,8},{12,14},{14,12},{16,18},{18,... | collective-permute-start | bytes 1572872 | tf_op jit(solution)/shard_map/ppermute | solution.py:804
  395.7 22.7 %collective-permute-start.79 = (bf16[8,64,512]{2,1,0:T(8,128)(2,1)}, bf16[8,64,512]{2,1,0:T(8,128)(2,1)S(1)}, u32[]{:S(2)}, u32[]{:S(2)}) collective-permute-start(bf16[8,64,512]{2,1,0:T(8,128)(2,1)} %pad_maximum_fusion.11.refs_1_), channel_id=1, source_target_pairs={{0,4},{2,6},{4,0},{6,2},{8,12},{10,14},{12,8},{14,10},{16,20},{18,... | collective-permute-start | bytes 1572872 | tf_op jit(solution)/shard_map/ppermute | solution.py:804
  (129 other events, 1124.8 us)

commit v3 on v2

--- a/solution.py
+++ b/solution.py
@@ -1,5 +1,5 @@
 import math
-from collections import namedtuple
+from types import SimpleNamespace
 
 import jax
 import jax.numpy as jnp
@@ -353,7 +353,7 @@
     units = w_up.shape[1]
     steps = units // LANES
     down_each, up_each = units // BLOCKS, width // BLOCKS
-    sizes = dict(down=down_each, up=up_each * (steps - 1), rest=down_each + up_each)
+    sizes = {DOWN: down_each, UP: up_each * (steps - 1), REST: down_each + up_each}
 
     def body(me_ref, n_own, n_other, g_own, g_other, up_w, down_w, act, grad, *rest):
         me = me_ref[0]
@@ -386,20 +386,20 @@
         for sub in range(LANES // down_each):
             part = slice(sub * down_each, (sub + 1) * down_each)
             block = step * (LANES // down_each) + sub
-            put("down", block, 0, down_part[part, :LANES])
-            put("rest", block, 0, down_part[part, LANES:])
+            put(DOWN, block, 0, down_part[part, :LANES])
+            put(REST, block, 0, down_part[part, LANES:])
 
         @pl.when(step < steps - 1)
         def _():
             for block in range(BLOCKS):
                 part = slice(block * up_each, (block + 1) * up_each)
-                put("up", block, step * up_each, up_part[part, :])
+                put(UP, block, step * up_each, up_part[part, :])
 
         @pl.when(step == steps - 1)
         def _():
             for block in range(BLOCKS):
                 part = slice(block * up_each, (block + 1) * up_each)
-                put("rest", block, down_each, up_part[part, :])
+                put(REST, block, down_each, up_part[part, :])
 
     out = pl.BlockSpec((2, rows, LANES), lambda j: (0, 0, j))
     shapes = [(BLOCKS // 2, sizes[name], LANES) for name in sizes for _ in range(2)]
@@ -659,10 +659,28 @@
     )
 
 
+DOWN, UP, REST, CROSS, PROJ, QUERY, KEY, VALUE = range(8)
+(
+    D_W_QUERY,
+    D_W_KEY,
+    D_W_VALUE,
+    D_W_OUT,
+    D_C_QUERY,
+    D_C_KEY,
+    D_C_VALUE,
+    D_C_OUT,
+    D_W_UP,
+    D_W_DOWN,
+) = range(10)
 BLOCKS = 16
 LEVELS = 4
 LANES = 512
-Piece = namedtuple("Piece", ("terms", "rows", "first", "width", "tile", "full"))
+
+
+class Piece:
+    def __init__(self, terms, rows, first, width, tile, full):
+        self.terms, self.rows, self.first = terms, rows, first
+        self.width, self.tile, self.full = width, tile, full
 
 
 def place_of(block, order):
@@ -817,7 +835,8 @@
 
 class Program:
     def __init__(self, given):
-        self.v = dict(given)
+        self.v = given
+        self.out = {}
         self.token = jnp.zeros((8, 128), F32)
         self.packets = {}
 
@@ -827,43 +846,44 @@
 
     def start(self, name):
         packet = self.packets[name]
-        order, step = packet["order"], packet["step"]
+        order, step = packet.order, packet.step
         bit = (order + order[::-1])[step]
         if step < LEVELS:
-            values = self.tie(packet["send"])
+            values = self.tie(packet.send)
         else:
-            values = packet["keep"] = self.tie(packet["keep"])
-        packet["arrived"] = exchange(values, self.main[bit])
+            values = packet.keep = self.tie(packet.keep)
+        packet.arrived = exchange(values, self.main[bit])
 
     def finish(self, name):
         packet = self.packets[name]
-        step, keep = packet["step"], packet["keep"]
-        arrived = self.tie(packet["arrived"])
-        packet["step"] = step + 1
+        step, keep = packet.step, packet.keep
+        arrived = self.tie(packet.arrived)
+        packet.arrived = None
+        packet.step = step + 1
         if step < LEVELS - 1:
             half = keep.shape[0] // 2
-            packet["send"] = add_rounded(keep[half:], arrived[half:])
-            packet["keep"] = add_rounded(keep[:half], arrived[:half])
-            packet["send"] = self.tie(packet["send"])
+            packet.send = add_rounded(keep[half:], arrived[half:])
+            packet.keep = add_rounded(keep[:half], arrived[:half])
+            packet.send = self.tie(packet.send)
         elif step == LEVELS - 1:
             keep = add_rounded(keep, arrived)
             for bit in self.extra:
                 keep = add_rounded(keep, exchange(keep, bit))
-            packet["keep"] = self.tie(keep)
+            packet.keep = self.tie(keep)
         elif step < 2 * LEVELS - 1:
-            packet["keep"] = self.tie(jnp.concatenate([keep, arrived], 0))
+            packet.keep = self.tie(jnp.concatenate([keep, arrived], 0))
         else:
             outs = open_packet(
                 self.block,
-                packet["pieces"],
-                packet["order"],
+                packet.pieces,
+                packet.order,
                 keep,
                 arrived,
-                [self.v.get(out) for out in packet["outs"]],
+                [self.out.get(out) for out in packet.outs],
             )
-            for out, values in zip(packet["outs"], outs):
-                self.v[out] = values
-            self.v[packet["outs"][0]] = self.tie(outs[0])
+            for out, values in zip(packet.outs, outs):
+                self.out[out] = values
+            self.out[packet.outs[0]] = self.tie(outs[0])
 
     def packet(self, name, outs, pieces, operands):
         order = ORDERS[name]
@@ -875,66 +895,79 @@
 
     def add(self, name, halves_of, pieces, outs):
         keep, send = halves_of
-        self.packets[name] = dict(
-            order=ORDERS[name], step=0, keep=keep, send=self.tie(send), pieces=pieces, outs=outs
+        self.packets[name] = SimpleNamespace(
+            order=ORDERS[name], step=0, keep=keep, send=self.tie(send), pieces=pieces,
+            outs=outs, arrived=None,
         )
 
 
 def stage_text(p):
     v = p.v
-    v["k_cross"], v["v_cross"] = project_text(
-        v["text_own"], v["text_other"], v["c_key"], v["c_value"]
-    )
+    v.text_own = p.tie(v.text_own)
+    v.k_cross, v.v_cross = project_text(
+        v.text_own, v.text_other, v.c_key, v.c_value
+    )
+    v.k_cross = p.tie(v.k_cross)
 
 
 def stage_tokens(p):
     v = p.v
-    items, frames, width = v["tokens"].shape
+    v.tokens = p.tie(v.tokens)
+    items, frames, width = v.tokens.shape
     normed, *heads = project_tokens(
-        v["tokens"].reshape(items * frames, width),
-        v["gain_one"],
-        v["bias_one"],
-        v["w_query"],
-        v["w_key"],
-        v["w_value"],
-    )
-    v["normed_one"] = normed
-    v["q_self"], v["k_self"], v["v_self"] = [x.reshape(items, frames, -1) for x in heads]
+        v.tokens.reshape(items * frames, width),
+        v.gain_one,
+        v.bias_one,
+        v.w_query,
+        v.w_key,
+        v.w_value,
+    )
+    v.normed_one = normed
+    v.q_self, v.k_self, v.v_self = [x.reshape(items, frames, -1) for x in heads]
+    v.q_self = p.tie(v.q_self)
 
 
 def stage_self(p):
     v = p.v
-    v["mix_self"], v["lse_self"], v["attn_own"], send = self_forward(
-        p.rank, v["frame_valid"], v["q_self"], v["k_self"], v["v_self"], v["w_out"]
-    )
-    v["attn_other"] = swap_cores(send)
+    v.q_self = p.tie(v.q_self)
+    v.mix_self, v.lse_self, v.attn_own, send = self_forward(
+        p.rank, v.frame_valid, v.q_self, v.k_self, v.v_self, v.w_out
+    )
+    v.attn_other = swap_cores(send)
+    v.attn_own = p.tie(v.attn_own)
 
 
 def stage_norm_two(p):
     v = p.v
-    v["hidden_one"], v["n2_own"], v["square_attn"] = residual_norm(
-        p.rank, v["frame_valid"], v["tokens"], v["attn_own"], v["attn_other"],
-        v["gain_two"], v["bias_two"],
-    )
-    v["n2_other"] = swap_cores(v["n2_own"])
+    v.attn_own = p.tie(v.attn_own)
+    v.hidden_one, v.n2_own, v.square_attn = residual_norm(
+        p.rank, v.frame_valid, v.tokens, v.attn_own, v.attn_other,
+        v.gain_two, v.bias_two,
+    )
+    v.n2_other = swap_cores(v.n2_own)
+    v.n2_own = p.tie(v.n2_own)
 
 
 def stage_cross(p):
     v = p.v
-    v["q_cross"], v["mix_cross"], v["lse_cross"], v["cross_own"], send = cross_forward(
-        p.rank, v["text_len"], v["n2_own"], v["n2_other"], v["c_query"],
-        v["k_cross"], v["v_cross"], v["c_out"],
-    )
-    v["cross_other"] = swap_cores(send)
+    v.n2_own = p.tie(v.n2_own)
+    v.q_cross, v.mix_cross, v.lse_cross, v.cross_own, send = cross_forward(
+        p.rank, v.text_len, v.n2_own, v.n2_other, v.c_query,
+        v.k_cross, v.v_cross, v.c_out,
+    )
+    v.cross_other = swap_cores(send)
+    v.cross_own = p.tie(v.cross_own)
 
 
 def stage_norm_three(p):
     v = p.v
-    v["hidden_two"], v["n3_own"], v["square_cross"] = residual_norm(
-        p.rank, v["frame_valid"], v["hidden_one"], v["cross_own"], v["cross_other"],
-        v["gain_three"], v["bias_three"],
-    )
-    v["n3_other"] = swap_cores(v["n3_own"])
+    v.cross_own = p.tie(v.cross_own)
+    v.hidden_two, v.n3_own, v.square_cross = residual_norm(
+        p.rank, v.frame_valid, v.hidden_one, v.cross_own, v.cross_other,
+        v.gain_three, v.bias_three,
+    )
+    v.n3_other = swap_cores(v.n3_own)
+    v.n3_own = p.tie(v.n3_own)
 
 
 def flat(values):
@@ -943,19 +976,21 @@
 
 def stage_units(p):
     v = p.v
-    units, width = v["w_down"].shape
-    v["activated"], v["grad_up"], pairs = feed_forward(
-        p.block, ORDERS, flat(v["n3_own"]), flat(v["n3_other"]), flat(v["grad_own"]),
-        flat(v["grad_other"]), v["w_up"], v["w_down"],
+    v.n3_own = p.tie(v.n3_own)
+    units, width = v.w_down.shape
+    v.activated, v.grad_up, pairs = feed_forward(
+        p.block, ORDERS, flat(v.n3_own), flat(v.n3_other), flat(v.grad_own),
+        flat(v.grad_other), v.w_up, v.w_down,
     )
     down = [Piece(None, units, at, LANES, None, width) for at in (0, LANES)]
     up = [
         Piece(None, width, 0, units - LANES, None, units),
         Piece(None, width, units - LANES, LANES, None, units),
     ]
-    p.add("down", pairs["down"], down[:1], ["d_w_down"])
-    p.add("up", pairs["up"], up[:1], ["d_w_up"])
-    p.add("rest", pairs["rest"], [down[1], up[1]], ["d_w_down", "d_w_up"])
+    p.add(DOWN, pairs[DOWN], down[:1], [D_W_DOWN])
+    p.add(UP, pairs[UP], up[:1], [D_W_UP])
+    p.add(REST, pairs[REST], [down[1], up[1]], [D_W_DOWN, D_W_UP])
+    v.grad_up = p.tie(v.grad_up)
 
 
 HALF_TERMS = [((0, (0,)), (1, ())), ((0, (1,)), (2, ()))]
@@ -963,46 +998,56 @@
 
 def stage_back_units(p):
     v = p.v
-    own, send = project_halves(v["grad_up"], v["w_up"], True)
-    shape = v["hidden_two"].shape
-    v["gn3_own"], v["gn3_other"] = own.reshape(shape), swap_cores(send).reshape(shape)
+    v.grad_up = p.tie(v.grad_up)
+    own, send = project_halves(v.grad_up, v.w_up, True)
+    shape = v.hidden_two.shape
+    v.gn3_own, v.gn3_other = own.reshape(shape), swap_cores(send).reshape(shape)
+    v.gn3_own = p.tie(v.gn3_own)
 
 
 def stage_back_three(p):
     v = p.v
-    v["g_h2"], v["d_gain_three"], v["d_bias_three"], v["g_cross_own"] = norm_backward(
-        p.rank, v["hidden_two"], v["gain_three"], v["gn3_own"], v["gn3_other"],
-        v["grad_own"], False,
-    )
-    v["g_cross_other"] = swap_cores(v["g_cross_own"])
+    v.gn3_own = p.tie(v.gn3_own)
+    v.g_h2, v.d_gain_three, v.d_bias_three, v.g_cross_own = norm_backward(
+        p.rank, v.hidden_two, v.gain_three, v.gn3_own, v.gn3_other,
+        v.grad_own, False,
+    )
+    v.g_cross_other = swap_cores(v.g_cross_own)
+    v.g_cross_own = p.tie(v.g_cross_own)
 
 
 def stage_out(p):
     v = p.v
-    own, send = project_halves(v["activated"], v["w_down"], False)
-    shape = v["hidden_two"].shape
-    v["ff_own"], v["ff_other"] = own.reshape(shape), swap_cores(send).reshape(shape)
+    v.activated = p.tie(v.activated)
+    own, send = project_halves(v.activated, v.w_down, False)
+    shape = v.hidden_two.shape
+    v.ff_own, v.ff_other = own.reshape(shape), swap_cores(send).reshape(shape)
+    v.ff_own = p.tie(v.ff_own)
 
 
 def stage_result(p):
     v = p.v
-    v["out"], v["square_out"], v["square_ff"] = finish_output(
-        p.rank, v["frame_valid"], v["hidden_two"], v["ff_own"], v["ff_other"]
-    )
+    v.ff_own = p.tie(v.ff_own)
+    v.out, v.square_out, v.square_ff = finish_output(
+        p.rank, v.frame_valid, v.hidden_two, v.ff_own, v.ff_other
+    )
+    v.out = p.tie(v.out)
 
 
 def stage_back_cross(p):
     v = p.v
+    v.g_cross_own = p.tie(v.g_cross_own)
     (
-        v["dq_cross"], v["dk_cross"], v["dv_cross"], v["gn2_own"], send,
-        v["text_grad_own"], text_send,
+        v.dq_cross, v.dk_cross, v.dv_cross, v.gn2_own, send,
+        v.text_grad_own, text_send,
     ) = cross_backward(
-        p.rank, v["text_len"], v["g_cross_own"], v["g_cross_other"], v["c_out"],
-        v["q_cross"], v["k_cross"], v["v_cross"], v["lse_cross"],
-        v["c_query"], v["c_key"], v["c_value"],
-    )
-    v["gn2_other"] = swap_cores(send)
-    v["text_grad_other"] = swap_cores(text_send)
+        p.rank, v.text_len, v.g_cross_own, v.g_cross_other, v.c_out,
+        v.q_cross, v.k_cross, v.v_cross, v.lse_cross,
+        v.c_query, v.c_key, v.c_value,
+    )
+    v.gn2_other = swap_cores(send)
+    v.text_grad_other = swap_cores(text_send)
+    v.gn2_own = p.tie(v.gn2_own)
 
 
 def halves(values):
@@ -1011,9 +1056,9 @@
 
 def stage_cross_packet(p):
     v = p.v
-    items, _, _, local = v["dk_cross"].shape
-    depth = v["c_key"].shape[0]
-    width = v["c_query"].shape[0]
+    items, _, _, local = v.dk_cross.shape
+    depth = v.c_key.shape[0]
+    width = v.c_query.shape[0]
     query_terms = [((1, ()), (0, (0,))), ((2, ()), (0, (1,)))]
 
     def text_terms(place):
@@ -1022,240 +1067,233 @@
         ]
 
     p.packet(
-        "cross", ["d_c_query", "d_c_key", "d_c_value"],
+        CROSS, [D_C_QUERY, D_C_KEY, D_C_VALUE],
         [
             Piece(query_terms, width, 0, local, width, local),
             Piece(text_terms(5), depth, 0, local, depth, local),
             Piece(text_terms(6), depth, 0, local, depth, local),
         ],
         [
-            halves(v["dq_cross"]), flat(v["n2_own"]), flat(v["n2_other"]),
-            v["text_own"], v["text_other"], v["dk_cross"], v["dv_cross"],
+            halves(v.dq_cross), flat(v.n2_own), flat(v.n2_other),
+            v.text_own, v.text_other, v.dk_cross, v.dv_cross,
         ],
     )
 
 
 def stage_back_two(p):
     v = p.v
-    v["g_h1"], v["d_gain_two"], v["d_bias_two"], v["g_attn_own"] = norm_backward(
-        p.rank, v["hidden_one"], v["gain_two"], v["gn2_own"], v["gn2_other"], v["g_h2"], False
-    )
-    v["g_attn_other"] = swap_cores(v["g_attn_own"])
+    v.gn2_own = p.tie(v.gn2_own)
+    v.g_h1, v.d_gain_two, v.d_bias_two, v.g_attn_own = norm_backward(
+        p.rank, v.hidden_one, v.gain_two, v.gn2_own, v.gn2_other, v.g_h2, False
+    )
+    v.g_attn_other = swap_cores(v.g_attn_own)
+    v.g_attn_own = p.tie(v.g_attn_own)
 
 
 def stage_back_self(p):
     v = p.v
-    v["dq_self"], v["dk_self"], v["dv_self"], v["gn1_own"], send = self_backward(
-        p.rank, v["frame_valid"], v["g_attn_own"], v["g_attn_other"], v["w_out"],
-        v["q_self"], v["k_self"], v["v_self"], v["lse_self"],
-        v["w_query"], v["w_key"], v["w_value"],
-    )
-    v["gn1_other"] = swap_cores(send)
+    v.g_attn_own = p.tie(v.g_attn_own)
+    v.dq_self, v.dk_self, v.dv_self, v.gn1_own, send = self_backward(
+        p.rank, v.frame_valid, v.g_attn_own, v.g_attn_other, v.w_out,
+        v.q_self, v.k_self, v.v_self, v.lse_self,
+        v.w_query, v.w_key, v.w_value,
+    )
+    v.gn1_other = swap_cores(send)
+    v.gn1_own = p.tie(v.gn1_own)
 
 
 def stage_proj_packet(p):
     v = p.v
-    local, width = v["w_out"].shape
+    local, width = v.w_out.shape
     terms = [((3, (0,)), (4, ())), ((3, (1,)), (5, ()))]
     steps = width // LANES
 
     def streamed(name, first):
-        return (flat(v[name]), 1, (0, first), steps, LANES)
+        return (flat(name), 1, (0, first), steps, LANES)
 
     p.packet(
-        "proj", ["d_c_out", "d_w_out"],
+        PROJ, [D_C_OUT, D_W_OUT],
         [
             Piece(HALF_TERMS, local, 0, width, local, width),
             Piece(terms, local, 0, width, local, width),
         ],
         [
-            halves(v["mix_cross"]), streamed("g_cross_own", 0), streamed("g_cross_other", 0),
-            halves(v["mix_self"]), streamed("g_attn_own", steps),
-            streamed("g_attn_other", steps),
+            halves(v.mix_cross), streamed(v.g_cross_own, 0), streamed(v.g_cross_other, 0),
+            halves(v.mix_self), streamed(v.g_attn_own, steps),
+            streamed(v.g_attn_other, steps),
         ],
     )
 
 
 def self_packet(p, name, grad, out):
     v = p.v
-    width, local = v["w_query"].shape
+    width, local = v.w_query.shape
     piece = Piece([((0, ()), (1, ()))], width, 0, local, width, local)
-    p.packet(name, [out], [piece], [v["normed_one"], flat(v[grad])])
+    p.packet(name, [out], [piece], [v.normed_one, flat(grad)])
 
 
 def stage_query_packet(p):
-    self_packet(p, "query", "dq_self", "d_w_query")
+    self_packet(p, QUERY, p.v.dq_self, D_W_QUERY)
 
 
 def stage_key_packet(p):
-    self_packet(p, "key", "dk_self", "d_w_key")
+    self_packet(p, KEY, p.v.dk_self, D_W_KEY)
 
 
 def stage_value_packet(p):
-    self_packet(p, "value", "dv_self", "d_w_value")
+    self_packet(p, VALUE, p.v.dv_self, D_W_VALUE)
 
 
 def stage_back_one(p):
     v = p.v
-    v["d_tokens"], v["d_gain_one"], v["d_bias_one"] = norm_backward(
-        p.rank, v["tokens"], v["gain_one"], v["gn1_own"], v["gn1_other"], v["g_h1"], True
-    )
+    v.gn1_own = p.tie(v.gn1_own)
+    v.d_tokens, v.d_gain_one, v.d_bias_one = norm_backward(
+        p.rank, v.tokens, v.gain_one, v.gn1_own, v.gn1_other, v.g_h1, True
+    )
+    v.d_tokens = p.tie(v.d_tokens)
 
 
 def stage_text_grad(p):
     v = p.v
-    v["d_text"] = v["text_grad_own"] + v["text_grad_other"].astype(F32)
-
-
-SMALL = (
-    "d_gain_one", "d_bias_one", "d_gain_two", "d_bias_two", "d_gain_three", "d_bias_three",
-    "square_out", "square_attn", "square_cross", "square_ff",
-)
+    v.text_grad_own = p.tie(v.text_grad_own)
+    v.d_text = v.text_grad_own + v.text_grad_other.astype(F32)
+    v.d_text = p.tie(v.d_text)
 
 
 def stage_small(p):
     v = p.v
-    half = v["hidden_one"].shape[1]
-    width = v["hidden_one"].shape[2]
-    own = jnp.clip(v["frame_valid"] - p.rank * half, 0, half).sum().astype(F32)
-    rows = [v[name] for name in SMALL] + [jnp.full((1, width), own / width, F32)]
+    half = v.hidden_one.shape[1]
+    width = v.hidden_one.shape[2]
+    own = jnp.clip(v.frame_valid - p.rank * half, 0, half).sum().astype(F32)
+    rows = [
+        v.d_gain_one, v.d_bias_one, v.d_gain_two, v.d_bias_two,
+        v.d_gain_three, v.d_bias_three, v.square_out, v.square_attn,
+        v.square_cross, v.square_ff, jnp.full((1, width), own / width, F32),
+    ]
     rows.append(jnp.zeros((16 - len(rows), width), F32))
     total = p.tie(jnp.concatenate(rows, 0))
-    v["small"] = total
-    v["small_other"] = swap_cores(total)
+    v.small = total
+    v.small_other = swap_cores(total)
     p.hops = list(range(lax.axis_size("dp").bit_length() - 1))
 
 
 def stage_hop(p):
     v = p.v
-    total = v["small"] = p.tie(v["small"] + v["small_other"])
+    total = v.small = p.tie(v.small + v.small_other)
     if p.hops:
-        v["small_other"] = exchange(total, p.hops.pop(0))
+        v.small_other = exchange(total, p.hops.pop(0))
 
 
 def stage_rms(p):
     v = p.v
     while p.hops:
         stage_hop(p)
-    total = v["small"] + v["small_other"]
+    total = v.small + v.small_other
     width = total.shape[1]
-    v["small"] = total[:6]
+    v.small = total[:6]
     sums = jnp.sum(total[6:11], -1)
-    v["rms"] = jnp.sqrt(sums[:4] / (sums[4] * width))
+    v.rms = jnp.sqrt(sums[:4] / (sums[4] * width))
 
 
 def stage_end(p):
-    p.v["rms"] = p.v["rms"] + p.token[0, :4] * 0.0
+    p.v.rms = p.v.rms + p.token[0, :4] * 0.0
 
 
 ORDERS = {
-    "down": [2, 0, 1, 3],
-    "up": [0, 1, 2, 3],
-    "rest": [1, 0, 2, 3],
-    "cross": [2, 1, 0, 3],
-    "proj": [1, 0, 3, 2],
-    "query": [0, 1, 2, 3],
-    "key": [1, 0, 3, 2],
-    "value": [0, 1, 2, 3],
+    DOWN: [2, 0, 1, 3],
+    UP: [0, 1, 2, 3],
+    REST: [1, 0, 2, 3],
+    CROSS: [2, 1, 0, 3],
+    PROJ: [1, 0, 3, 2],
+    QUERY: [0, 1, 2, 3],
+    KEY: [1, 0, 3, 2],
+    VALUE: [0, 1, 2, 3],
 }
 
-CHAIN = dict(
-    text=("text_own", "k_cross"), tokens=("tokens", "q_self"), self=("q_self", "attn_own"),
-    norm_two=("attn_own", "n2_own"), cross=("n2_own", "cross_own"),
-    norm_three=("cross_own", "n3_own"), units=("n3_own", "grad_up"),
-    back_units=("grad_up", "gn3_own"), back_three=("gn3_own", "g_cross_own"),
-    out=("activated", "ff_own"), result=("ff_own", "out"), back_cross=("g_cross_own", "gn2_own"),
-    back_two=("gn2_own", "g_attn_own"), back_self=("g_attn_own", "gn1_own"),
-    back_one=("gn1_own", "d_tokens"), text_grad=("text_grad_own", "d_text"),
-)
-
-STAGES = dict(
-    text=stage_text, tokens=stage_tokens, self=stage_self, norm_two=stage_norm_two,
-    cross=stage_cross, norm_three=stage_norm_three, units=stage_units,
-    back_units=stage_back_units, back_three=stage_back_three, out=stage_out,
-    result=stage_result, back_cross=stage_back_cross, cross_packet=stage_cross_packet, proj_packet=stage_proj_packet,
-    query_packet=stage_query_packet, key_packet=stage_key_packet,
-    value_packet=stage_value_packet,
-    back_two=stage_back_two, back_self=stage_back_self,
-    back_one=stage_back_one, text_grad=stage_text_grad,
-    small=stage_small, hop=stage_hop, rms=stage_rms, end=stage_end,
-)
 
 PLAN = [
-    ("do", "tokens"), ("do", "self"), ("do", "text"), ("do", "norm_two"), ("do", "cross"),
-    ("do", "norm_three"), ("do", "units"), ("send", "rest"), ("send", "up"), ("send", "down"),
-    ("do", "back_units"), ("do", "back_three"), ("do", "back_cross"), ("take", "down"),
-    ("take", "rest"), ("take", "up"), ("do", "cross_packet"), ("do", "back_two"),
-    ("send", "rest"), ("send", "up"), ("send", "cross"), ("send", "down"), ("do", "back_self"),
-    ("take", "rest"), ("take", "up"), ("take", "down"), ("take", "cross"), ("do", "proj_packet"),
-    ("do", "query_packet"), ("do", "key_packet"), ("do", "value_packet"), ("send", "rest"),
-    ("send", "up"), ("send", "proj"), ("send", "cross"), ("send", "key"), ("send", "query"),
-    ("send", "value"), ("send", "down"), ("take", "rest"), ("send", "rest"), ("do", "out"),
-    ("do", "back_one"), ("take", "up"), ("send", "up"), ("take", "query"), ("take", "rest"),
-    ("send", "rest"), ("take", "proj"), ("send", "proj"), ("send", "query"), ("take", "value"),
-    ("take", "up"), ("send", "up"), ("do", "result"), ("take", "cross"), ("send", "cross"),
-    ("send", "value"), ("take", "rest"), ("send", "rest"), ("take", "proj"), ("send", "proj"),
-    ("take", "up"), ("send", "up"), ("take", "key"), ("send", "key"), ("take", "cross"),
-    ("send", "cross"), ("take", "down"), ("take", "rest"), ("send", "rest"), ("send", "down"),
-    ("take", "query"), ("take", "proj"), ("send", "proj"), ("take", "key"), ("take", "up"),
-    ("send", "up"), ("send", "key"), ("take", "value"), ("take", "cross"), ("send", "cross"),
-    ("take", "down"), ("send", "query"), ("take", "proj"), ("send", "proj"), ("take", "rest"),
-    ("send", "rest"), ("take", "key"), ("send", "key"), ("take", "query"), ("send", "value"),
-    ("take", "cross"), ("send", "cross"), ("send", "query"), ("take", "proj"), ("send", "proj"),
-    ("take", "up"), ("send", "up"), ("take", "key"), ("send", "key"), ("take", "value"),
-    ("send", "value"), ("take", "query"), ("send", "query"), ("take", "cross"),
-    ("send", "cross"), ("take", "key"), ("send", "key"), ("take", "proj"), ("send", "proj"),
-    ("send", "down"), ("take", "value"), ("send", "value"), ("take", "query"), ("send", "query"),
-    ("take", "key"), ("send", "key"), ("take", "rest"), ("take", "down"), ("send", "down"),
-    ("take", "value"), ("send", "value"), ("take", "query"), ("send", "query"),
-    ("take", "cross"), ("send", "cross"), ("take", "up"), ("take", "value"), ("send", "value"),
-    ("take", "down"), ("send", "down"), ("take", "proj"), ("send", "proj"), ("take", "query"),
-    ("send", "query"), ("take", "key"), ("send", "key"), ("take", "value"), ("send", "value"),
-    ("do", "text_grad"), ("take", "down"), ("send", "down"), ("do", "small"), ("do", "hop"),
-    ("take", "cross"), ("do", "hop"), ("take", "query"), ("take", "proj"), ("do", "hop"),
-    ("do", "hop"), ("do", "rms"), ("take", "value"), ("take", "key"), ("take", "down"),
-    ("do", "end"),
+    stage_tokens, stage_self, stage_text, stage_norm_two, stage_cross, stage_norm_three,
+    stage_units, REST, UP, DOWN, stage_back_units, stage_back_three, stage_back_cross, DOWN,
+    REST, UP, stage_cross_packet, stage_back_two, REST, UP, CROSS, DOWN, stage_back_self, REST,
+    UP, DOWN, CROSS, stage_proj_packet, stage_query_packet, stage_key_packet, stage_value_packet,
+    REST, UP, PROJ, CROSS, KEY, QUERY, VALUE, DOWN, REST, REST, stage_out, stage_back_one, UP,
+    UP, QUERY, REST, REST, PROJ, PROJ, QUERY, VALUE, UP, UP, stage_result, CROSS, CROSS, VALUE,
+    REST, REST, PROJ, PROJ, UP, UP, KEY, KEY, CROSS, CROSS, DOWN, REST, REST, DOWN, QUERY, PROJ,
+    PROJ, KEY, UP, UP, KEY, VALUE, CROSS, CROSS, DOWN, QUERY, PROJ, PROJ, REST, REST, KEY, KEY,
+    QUERY, VALUE, CROSS, CROSS, QUERY, PROJ, PROJ, UP, UP, KEY, KEY, VALUE, VALUE, QUERY, QUERY,
+    CROSS, CROSS, KEY, KEY, PROJ, PROJ, DOWN, VALUE, VALUE, QUERY, QUERY, KEY, KEY, REST, DOWN,
+    DOWN, VALUE, VALUE, QUERY, QUERY, CROSS, CROSS, UP, VALUE, VALUE, DOWN, DOWN, PROJ, PROJ,
+    QUERY, QUERY, KEY, KEY, VALUE, VALUE, stage_text_grad, DOWN, DOWN, stage_small, stage_hop,
+    CROSS, stage_hop, QUERY, PROJ, stage_hop, stage_hop, stage_rms, VALUE, KEY, DOWN, stage_end,
 ]
 
-NAMES = (
-    "tokens", "text_own", "text_len", "frame_valid", "gain_one", "bias_one", "gain_two",
-    "bias_two", "gain_three", "bias_three", "w_query", "w_key", "w_value", "w_out", "c_query",
-    "c_key", "c_value", "c_out", "w_up", "w_down", "grad_own",
-)
-
-
-def per_device(*args):
-    given = dict(zip(NAMES, args))
-    for name in NAMES[4:10]:
-        given[name] = given[name].reshape(1, -1)
-    p = Program(given)
+def per_device(
+    tokens,
+    text_own,
+    text_len,
+    frame_valid,
+    gain_one,
+    bias_one,
+    gain_two,
+    bias_two,
+    gain_three,
+    bias_three,
+    w_query,
+    w_key,
+    w_value,
+    w_out,
+    c_query,
+    c_key,
+    c_value,
+    c_out,
+    w_up,
+    w_down,
+    grad_own,
+):
+    v = SimpleNamespace()
+    v.tokens = tokens
+    v.text_own = text_own
+    v.text_len = text_len
+    v.frame_valid = frame_valid
+    v.gain_one = gain_one.reshape(1, -1)
+    v.bias_one = bias_one.reshape(1, -1)
+    v.gain_two = gain_two.reshape(1, -1)
+    v.bias_two = bias_two.reshape(1, -1)
+    v.gain_three = gain_three.reshape(1, -1)
+    v.bias_three = bias_three.reshape(1, -1)
+    v.w_query = w_query
+    v.w_key = w_key
+    v.w_value = w_value
+    v.w_out = w_out
+    v.c_query = c_query
+    v.c_key = c_key
+    v.c_value = c_value
+    v.c_out = c_out
+    v.w_up = w_up
+    v.w_down = w_down
+    v.grad_own = grad_own
+    p = Program(v)
     p.rank = lax.axis_index("mp").astype(jnp.int32).reshape(1)
     p.main, p.extra = main_bits()
     place = lax.axis_index("dp")
     p.block = sum(((place >> bit) & 1) << k for k, bit in enumerate(p.main))
     p.block = p.block.astype(jnp.int32).reshape(1)
-    v = p.v
-    v["text_other"] = swap_cores(v["text_own"])
-    v["grad_other"] = swap_cores(v["grad_own"])
-    for kind, name in PLAN:
-        if kind == "do":
-            before, after = CHAIN.get(name, (None, None))
-            if before:
-                v[before] = p.tie(v[before])
-            STAGES[name](p)
-            if after:
-                v[after] = p.tie(v[after])
-        elif kind == "send":
-            p.start(name)
+    v.text_other = swap_cores(v.text_own)
+    v.grad_other = swap_cores(v.grad_own)
+    for action in PLAN:
+        if callable(action):
+            action(p)
+        elif p.packets[action].arrived is None:
+            p.start(action)
         else:
-            p.finish(name)
+            p.finish(action)
     return (
-        v["out"],
-        v["d_tokens"],
-        v["d_text"],
-        *(v["small"][n] for n in range(6)),
-        *(v["d_" + name] for name in NAMES[10:20]),
-        v["rms"],
+        v.out,
+        v.d_tokens,
+        v.d_text,
+        *(v.small[n] for n in range(6)),
+        *(p.out[name] for name in range(10)),
+        v.rms,
     )
 
 

time: 435 us -> 435 us (level)
  no operation moved by 1% of the time
where the time goes in v3:
time: 435 us; the launch traced here: 427 us
  waiting for transfers between devices  168 us (39%)
  Pallas kernels  148 us (34%)
  starting transfers between devices  80.5 us (19%)
  local copies, waits for them, and re-layouts  16 us (4%)
  other arithmetic  10.8 us (2%)
    ppermute x68, waiting for transfers between devices, exchange(): return lax.ppermute(values, 'dp', pairs)  157 us
    pallas_call x15, Pallas kernels, call(): pl.pallas_call(body, grid=grid, in_specs=in_specs, out_specs=out_specs, o...  111 us
    ppermute x68, starting transfers between devices, exchange(): return lax.ppermute(values, 'dp', pairs)  77.7 us
    pallas_call x8, Pallas kernels, open_packet(): pl.pallas_call(body, grid=(steps,), in_specs=[SMEM_SPEC, whole(kept.shape...  24.1 us
    unnamed x142, local copies, waits for them, and re-layouts  13.3 us
    ppermute x14, waiting for transfers between devices, swap_cores(): return lax.ppermute(values, 'mp', SWAP)  11.1 us
  transfers between devices with their start and end apart: 82, of which 39 were waited for; matrix products, arithmetic and copies ran while one was open for 3% of the time, Pallas kernels for 21%

profile of v3, /device:TPU:0, one launch (start us, length us, event | category | flops | bytes accessed | tf_op | source)
XLA Modules:
  0.0 426.9 jit_solution(2078267702606740759)
XLA Ops:
  7.3 5.0 %shard_map.356 = (bf16[1024,1024]{1,0:T(8,128)(2,1)S(1)}, bf16[1024,512]{1,0:T(8,128)(2,1)S(1)}, bf16[1024,512]{1,0:T(8,128)(2,1)S(1)}, bf16[1024,512]{1,0:T(8,128)(2,1)S(1)}) custom-call(bf16[1024,1024]{1,0:T(8,128)(2,1)S(1)} %bitcast.36, bf16[1,1024]{1,0:T(2,128)(2,1)S(1)} %reshape.142.g, bf16[1,1024]{1,0:T(2,128)(2,1)S(1)} %reshape.143.b, ...), custom_call_target="tpu_custom_call" | custom-call | bytes 1024 | tf_op jit(solution)/shard_map/pallas_call | solution.py:54
  13.7 8.1 %shard_map.357 = (bf16[2,2,256,512]{3,2,1,0:T(8,128)(2,1)S(1)}, f32[2,8,512]{2,1,0:T(8,128)S(1)}, f32[2,256,1024]{2,1,0:T(8,128)S(1)}, bf16[2,256,1024]{2,1,0:T(8,128)(2,1)S(1)}) custom-call(s32[1]{0:T(128)} %bitcast.rank_ref, s32[2]{0:T(128)S(1)} %copy-done.56, bf16[2,512,512]{2,1,0:T(8,128)(2,1)S(1)} %bitcast.37, bf16[2,512,512]{2,1,0:T(8,128)(2,1)S(1)} %bitcast.39, ...), custom_call_target="tpu_custom_call" | custom-call | bytes 1024 | tf_op jit(solution)/shard_map/pallas_call | solution.py:54
  30.9 7.7 %shard_map.360 = (bf16[2,2,256,512]{3,2,1,0:T(8,128)(2,1)S(1)}, bf16[2,2,256,512]{3,2,1,0:T(8,128)(2,1)S(1)}, f32[2,8,512]{2,1,0:T(8,128)S(1)}, f32[2,256,1024]{2,1,0:T(8,128)S(1)}, bf16[2,256,1024]{2,1,0:T(8,128)(2,1)S(1)}) custom-call(s32[1]{0:T(128)} %bitcast.rank_ref, s32[2]{0:T(128)S(1)} %copy-done.65, ...), custom_call_target="tpu_custom_call" | custom-call | bytes 1024 | tf_op jit(solution)/shard_map/pallas_call | solution.py:54
  49.0 24.9 %shard_map.362 = (bf16[2,512,2048]{2,1,0:T(8,128)(2,1)}, bf16[2,512,2048]{2,1,0:T(8,128)(2,1)}, bf16[8,128,512]{2,1,0:T(8,128)(2,1)S(1)}, bf16[8,128,512]{2,1,0:...) custom-call(s32[1]{0:T(128)} %bitcast.5.me_ref.refs_0_, ...), custom_call_target="tpu_custom_call" | custom-call | bytes 1024 | tf_op jit(solution)/shard_map/pallas_call | solution.py:54
  76.1 5.0 %shard_map.363 = (f32[512,1024]{1,0:T(8,128)S(1)}, bf16[512,1024]{1,0:T(8,128)(2,1)S(1)}) custom-call(bf16[2,512,2048]{2,1,0:T(8,128)(2,1)S(1)} %copy-done.24, bf16[1024,2048]{1,0:T(8,128)(2,1)S(1)} %copy-done.4), custom_call_target="tpu_custom_call" | custom-call | bytes 1024 | tf_op jit(solution)/shard_map/pallas_call | solution.py:54
  91.7 18.1 %shard_map.365 = (bf16[2,2,256,512]{3,2,1,0:T(8,128)(2,1)S(1)}, bf16[2,2,128,512]{3,2,1,0:T(8,128)(2,1)S(1)}, bf16[2,2,128,512]{3,2,1,0:T(8,128)(2,1)S(1)}, f32[...) custom-call(s32[1]{0:T(128)} %bitcast.rank_ref, ...), custom_call_target="tpu_custom_call" | custom-call | bytes 1024 | tf_op jit(solution)/shard_map/pallas_call | solution.py:54
  119.5 7.0 %collective-permute-done.10 = bf16[8,192,512]{2,1,0:T(8,128)(2,1)S(1)} collective-permute-done((bf16[8,192,512]{2,1,0:T(8,128)(2,1)S(1)}, bf16[8,192,512]{2,1,0:T(8,128)(2,1)S(1)}, u32[]{:S(2)}, u32[]{:S(2)}) %collective-permute-start.10) | collective-permute-done | bytes 1572896 | tf_op jit(solution)/shard_map/ppermute | solution.py:822
  138.6 20.9 %shard_map.368 = (bf16[2,512,512]{2,1,0:T(8,128)(2,1)S(1)}, bf16[2,512,512]{2,1,0:T(8,128)(2,1)S(1)}, bf16[2,512,512]{2,1,0:T(8,128)(2,1)S(1)}, f32[2,256,1024]{2,1,0:T(8,128)S(1)}, bf16[2,256,1024]{2,1,0:T(8,128)(2,1)S(1)}) custom-call(s32[1]{0:T(128)} %bitcast.rank_ref, s32[2]{0:T(128)S(1)} %copy-done.56, ...), custom_call_target="tpu_custom_call" | custom-call | bytes 1024 | tf_op jit(solution)/shard_map/pallas_call | solution.py:54
  160.0 5.7 %collective-permute-done.15 = bf16[4,128,512]{2,1,0:T(8,128)(2,1)S(1)} collective-permute-done((bf16[4,128,512]{2,1,0:T(8,128)(2,1)}, bf16[4,128,512]{2,1,0:T(8,128)(2,1)S(1)}, u32[]{:S(2)}, u32[]{:S(2)}) %collective-permute-start.15) | collective-permute-done | bytes 524320 | tf_op jit(solution)/shard_map/ppermute | solution.py:822
  181.6 8.0 %collective-permute-done.17 = bf16[2,192,512]{2,1,0:T(8,128)(2,1)S(1)} collective-permute-done((bf16[2,192,512]{2,1,0:T(8,128)(2,1)S(1)}, bf16[2,192,512]{2,1,0:T(8,128)(2,1)S(1)}, u32[]{:S(2)}, u32[]{:S(2)}) %collective-permute-start.17) | collective-permute-done | bytes 393248 | tf_op jit(solution)/shard_map/ppermute | solution.py:822
  191.1 5.1 %shard_map.373 = (f32[512,1024]{1,0:T(8,128)S(1)}, bf16[512,1024]{1,0:T(8,128)(2,1)S(1)}) custom-call(bf16[2,512,2048]{2,1,0:T(8,128)(2,1)S(1)} %copy-done.23, bf16[2048,1024]{1,0:T(8,128)(2,1)S(1)} %copy-done.5), custom_call_target="tpu_custom_call" | custom-call | bytes 1024 | tf_op jit(solution)/shard_map/pallas_call | solution.py:54
  202.5 7.5 %collective-permute-done.24 = bf16[1,192,512]{2,1,0:T(8,128)(2,1)S(1)} collective-permute-done((bf16[1,192,512]{2,1,0:T(8,128)(2,1)S(1)}, bf16[1,192,512]{2,1,0:T(8,128)(2,1)S(1)}, u32[]{:S(2)}, u32[]{:S(2)}) %collective-permute-start.24) | collective-permute-done | bytes 196640 | tf_op jit(solution)/shard_map/ppermute | solution.py:822
  212.8 10.1 %collective-permute-done.20 = bf16[1,192,512]{2,1,0:T(8,128)(2,1)S(1)} collective-permute-done((bf16[1,192,512]{2,1,0:T(8,128)(2,1)S(1)}, bf16[1,192,512]{2,1,0:T(8,128)(2,1)S(1)}, u32[]{:S(2)}, u32[]{:S(2)}) %collective-permute-start.20) | collective-permute-done | bytes 196640 | tf_op jit(solution)/shard_map/ppermute | solution.py:822
  225.4 12.3 %collective-permute-done.26 = bf16[4,160,512]{2,1,0:T(8,128)(2,1)S(1)} collective-permute-done((bf16[4,160,512]{2,1,0:T(8,128)(2,1)S(1)}, bf16[4,160,512]{2,1,0:T(8,128)(2,1)S(1)}, u32[]{:S(2)}, u32[]{:S(2)}) %collective-permute-start.26) | collective-permute-done | bytes 655392 | tf_op jit(solution)/shard_map/ppermute | solution.py:822
  240.3 6.5 %collective-permute-done.29 = bf16[1,192,512]{2,1,0:T(8,128)(2,1)S(1)} collective-permute-done((bf16[1,192,512]{2,1,0:T(8,128)(2,1)S(1)}, bf16[1,192,512]{2,1,0:T(8,128)(2,1)S(1)}, u32[]{:S(2)}, u32[]{:S(2)}) %collective-permute-start.29) | collective-permute-done | bytes 196640 | tf_op jit(solution)/shard_map/ppermute | solution.py:822
  247.0 8.7 %collective-permute-done.36 = bf16[2,160,512]{2,1,0:T(8,128)(2,1)S(1)} collective-permute-done((bf16[2,160,512]{2,1,0:T(8,128)(2,1)S(1)}, bf16[2,160,512]{2,1,0:T(8,128)(2,1)S(1)}, u32[]{:S(2)}, u32[]{:S(2)}) %collective-permute-start.36) | collective-permute-done | bytes 327712 | tf_op jit(solution)/shard_map/ppermute | solution.py:822
  260.8 9.0 %collective-permute-done.33 = bf16[2,128,512]{2,1,0:T(8,128)(2,1)S(1)} collective-permute-done((bf16[2,128,512]{2,1,0:T(8,128)(2,1)S(1)}, bf16[2,128,512]{2,1,0:T(8,128)(2,1)S(1)}, u32[]{:S(2)}, u32[]{:S(2)}) %collective-permute-start.33) | collective-permute-done | bytes 262176 | tf_op jit(solution)/shard_map/ppermute | solution.py:822
  271.8 5.4 %collective-permute-done.38 = bf16[2,192,512]{2,1,0:T(8,128)(2,1)S(1)} collective-permute-done((bf16[2,192,512]{2,1,0:T(8,128)(2,1)S(1)}, bf16[2,192,512]{2,1,0:T(8,128)(2,1)S(1)}, u32[]{:S(2)}, u32[]{:S(2)}) %collective-permute-start.38) | collective-permute-done | bytes 393248 | tf_op jit(solution)/shard_map/ppermute | solution.py:822
  293.1 4.6 %collective-permute-done.42 = bf16[2,64,512]{2,1,0:T(8,128)(2,1)S(1)} collective-permute-done((bf16[2,64,512]{2,1,0:T(8,128)(2,1)S(1)}, bf16[2,64,512]{2,1,0:T(8,128)(2,1)S(1)}, u32[]{:S(2)}, u32[]{:S(2)}) %collective-permute-start.42) | collective-permute-done | bytes 131104 | tf_op jit(solution)/shard_map/ppermute | solution.py:822
  311.4 6.0 %collective-permute-done.53 = bf16[2,160,512]{2,1,0:T(8,128)(2,1)S(1)} collective-permute-done((bf16[2,160,512]{2,1,0:T(8,128)(2,1)S(1)}, bf16[2,160,512]{2,1,0:T(8,128)(2,1)S(1)}, u32[]{:S(2)}, u32[]{:S(2)}) %collective-permute-start.53) | collective-permute-done | bytes 327712 | tf_op jit(solution)/shard_map/ppermute | solution.py:822
  320.5 7.3 %collective-permute-done.50 = bf16[1,64,512]{2,1,0:T(8,128)(2,1)S(1)} collective-permute-done((bf16[1,64,512]{2,1,0:T(8,128)(2,1)S(1)}, bf16[1,64,512]{2,1,0:T(8,128)(2,1)S(1)}, u32[]{:S(2)}, u32[]{:S(2)}) %collective-permute-start.50) | collective-permute-done | bytes 65568 | tf_op jit(solution)/shard_map/ppermute | solution.py:822
  333.7 9.3 %collective-permute-done.57.refs_2_ = bf16[8,192,512]{2,1,0:T(8,128)(2,1)S(1)} collective-permute-done((bf16[8,192,512]{2,1,0:T(8,128)(2,1)S(1)}, bf16[8,192,512]{2,1,0:T(8,128)(2,1)S(1)}, u32[]{:S(2)}, u32[]{:S(2)}) %collective-permute-start.57) | collective-permute-done | bytes 1572896 | tf_op jit(solution)/shard_map/ppermute | solution.py:822
  348.6 5.1 %collective-permute-start.63 = (bf16[2,64,512]{2,1,0:T(8,128)(2,1)S(1)}, bf16[2,64,512]{2,1,0:T(8,128)(2,1)S(1)}, u32[]{:S(2)}, u32[]{:S(2)}) collective-permute-start(bf16[2,64,512]{2,1,0:T(8,128)(2,1)S(1)} %pad_maximum_fusion.22), channel_id=1, source_target_pairs={{0,8},{2,10},{4,12},{6,14},{8,0},{10,2},{12,4},{14,6},{16,24},{18,... | collective-permute-start | bytes 393224 | tf_op jit(solution)/shard_map/ppermute | solution.py:822
  369.3 7.0 %collective-permute-done.66 = bf16[4,64,512]{2,1,0:T(8,128)(2,1)S(1)} collective-permute-done((bf16[4,64,512]{2,1,0:T(8,128)(2,1)S(1)}, bf16[4,64,512]{2,1,0:T(8,128)(2,1)S(1)}, u32[]{:S(2)}, u32[]{:S(2)}) %collective-permute-start.66) | collective-permute-done | bytes 262176 | tf_op jit(solution)/shard_map/ppermute | solution.py:822
  (387 shorter events, 208.6 us)
Async XLA Ops:
  81.6 37.5 %collective-permute-start.6 = (bf16[8,192,512]{2,1,0:T(8,128)(2,1)S(1)}, bf16[8,192,512]{2,1,0:T(8,128)(2,1)S(1)}, u32[]{:S(2)}, u32[]{:S(2)}) collective-permute-start(bf16[8,192,512]{2,1,0:T(8,128)(2,1)S(1)} %get-tuple-element.528), channel_id=1, source_target_pairs={{0,4},{2,6},{4,0},{6,2},{8,12},{10,14},{12,8},{14,10},{16,20},{18,... | collective-permute-start | bytes 4718600 | tf_op jit(solution)/shard_map/ppermute | solution.py:822
  87.5 26.3 %collective-permute-start.7 = (bf16[8,128,512]{2,1,0:T(8,128)(2,1)S(1)}, bf16[8,128,512]{2,1,0:T(8,128)(2,1)S(1)}, u32[]{:S(2)}, u32[]{:S(2)}) collective-permute-start(bf16[8,128,512]{2,1,0:T(8,128)(2,1)S(1)} %get-tuple-element.534), channel_id=1, source_target_pairs={{0,8},{2,10},{4,12},{6,14},{8,0},{10,2},{12,4},{14,6},{16,24},{18,... | collective-permute-start | bytes 3145736 | tf_op jit(solution)/shard_map/ppermute | solution.py:822
  90.1 36.4 %collective-permute-start.10 = (bf16[8,192,512]{2,1,0:T(8,128)(2,1)S(1)}, bf16[8,192,512]{2,1,0:T(8,128)(2,1)S(1)}, u32[]{:S(2)}, u32[]{:S(2)}) collective-permute-start(bf16[8,192,512]{2,1,0:T(8,128)(2,1)S(1)} %get-tuple-element.559), channel_id=1, source_target_pairs={{0,2},{2,0},{4,6},{6,4},{8,10},{10,8},{12,14},{14,12},{16,18},{18,... | collective-permute-start | bytes 4718600 | tf_op jit(solution)/shard_map/ppermute | solution.py:822
  109.8 22.5 %collective-permute-start.11 = (bf16[2,256,1024]{2,1,0:T(8,128)(2,1)S(1)}, bf16[2,256,1024]{2,1,0:T(8,128)(2,1)S(1)}, u32[]{:S(2)}, u32[]{:S(2)}) collective-permute-start(bf16[2,256,1024]{2,1,0:T(8,128)(2,1)S(1)} %get-tuple-element.571), channel_id=1, source_target_pairs={{0,1},{1,0},{2,3},{3,2},{4,5},{5,4},{6,7},{7,6},{8,9},{9,8},{10,11... | collective-permute-start | bytes 3145736 | tf_op jit(solution)/shard_map/ppermute | solution.py:833
  134.5 25.1 %collective-permute-start.12 = (bf16[4,192,512]{2,1,0:T(8,128)(2,1)S(1)}, bf16[4,192,512]{2,1,0:T(8,128)(2,1)S(1)}, u32[]{:S(2)}, u32[]{:S(2)}) collective-permute-start(bf16[4,192,512]{2,1,0:T(8,128)(2,1)S(1)} %get-tuple-element.576), channel_id=1, source_target_pairs={{0,2},{2,0},{4,6},{6,4},{8,10},{10,8},{12,14},{14,12},{16,18},{18,... | collective-permute-start | bytes 2359304 | tf_op jit(solution)/shard_map/ppermute | solution.py:822
  136.0 30.8 %collective-permute-start.14 = (bf16[8,160,512]{2,1,0:T(8,128)(2,1)S(1)}, bf16[8,160,512]{2,1,0:T(8,128)(2,1)S(1)}, u32[]{:S(2)}, u32[]{:S(2)}) collective-permute-start(bf16[8,160,512]{2,1,0:T(8,128)(2,1)S(1)} %get-tuple-element.596), channel_id=1, source_target_pairs={{0,8},{2,10},{4,12},{6,14},{8,0},{10,2},{12,4},{14,6},{16,24},{18,... | collective-permute-start | bytes 3932168 | tf_op jit(solution)/shard_map/ppermute | solution.py:822
  136.5 23.3 %collective-permute-start.16 = (bf16[4,192,512]{2,1,0:T(8,128)(2,1)S(1)}, bf16[4,192,512]{2,1,0:T(8,128)(2,1)S(1)}, u32[]{:S(2)}, u32[]{:S(2)}) collective-permute-start(bf16[4,192,512]{2,1,0:T(8,128)(2,1)S(1)} %get-tuple-element.598), channel_id=1, source_target_pairs={{0,4},{2,6},{4,0},{6,2},{8,12},{10,14},{12,8},{14,10},{16,20},{18,... | collective-permute-start | bytes 2359304 | tf_op jit(solution)/shard_map/ppermute | solution.py:822
  138.0 27.7 %collective-permute-start.15 = (bf16[4,128,512]{2,1,0:T(8,128)(2,1)}, bf16[4,128,512]{2,1,0:T(8,128)(2,1)S(1)}, u32[]{:S(2)}, u32[]{:S(2)}) collective-permute-start(bf16[4,128,512]{2,1,0:T(8,128)(2,1)} %get-tuple-element.597), channel_id=1, source_target_pairs={{0,2},{2,0},{4,6},{6,4},{8,10},{10,8},{12,14},{14,12},{16,18},{18,... | collective-permute-start | bytes 1572872 | tf_op jit(solution)/shard_map/ppermute | solution.py:822
  165.7 30.6 %collective-permute-start.19 = (bf16[2,256,1024]{2,1,0:T(8,128)(2,1)S(1)}, bf16[2,256,1024]{2,1,0:T(8,128)(2,1)S(1)}, u32[]{:S(2)}, u32[]{:S(2)}) collective-permute-start(bf16[2,256,1024]{2,1,0:T(8,128)(2,1)S(1)} %get-tuple-element.656), channel_id=1, source_target_pairs={{0,1},{1,0},{2,3},{3,2},{4,5},{5,4},{6,7},{7,6},{8,9},{9,8},{10,11... | collective-permute-start | bytes 3145736 | tf_op jit(solution)/shard_map/ppermute | solution.py:833
  179.5 31.2 %collective-permute-start.23 = (bf16[8,128,512]{2,1,0:T(8,128)(2,1)S(1)}, bf16[8,128,512]{2,1,0:T(8,128)(2,1)S(1)}, u32[]{:S(2)}, u32[]{:S(2)}) collective-permute-start(bf16[8,128,512]{2,1,0:T(8,128)(2,1)S(1)} %get-tuple-element.673), channel_id=1, source_target_pairs={{0,4},{2,6},{4,0},{6,2},{8,12},{10,14},{12,8},{14,10},{16,20},{18,... | collective-permute-start | bytes 3145736 | tf_op jit(solution)/shard_map/ppermute | solution.py:822
  189.5 66.5 %collective-permute-start.35 = (bf16[2,128,512]{2,1,0:T(8,128)(2,1)S(1)}, bf16[2,128,512]{2,1,0:T(8,128)(2,1)S(1)}, u32[]{:S(2)}, u32[]{:S(2)}) collective-permute-start(bf16[2,128,512]{2,1,0:T(8,128)(2,1)S(1)} %get-tuple-element.723), channel_id=1, source_target_pairs={{0,4},{2,6},{4,0},{6,2},{8,12},{10,14},{12,8},{14,10},{16,20},{18,... | collective-permute-start | bytes 786440 | tf_op jit(solution)/shard_map/ppermute | solution.py:822
  210.0 36.8 %collective-permute-start.28 = (bf16[8,64,512]{2,1,0:T(8,128)(2,1)S(1)}, bf16[8,64,512]{2,1,0:T(8,128)(2,1)S(1)}, u32[]{:S(2)}, u32[]{:S(2)}) collective-permute-start(bf16[8,64,512]{2,1,0:T(8,128)(2,1)S(1)} %get-tuple-element.704), channel_id=1, source_target_pairs={{0,4},{2,6},{4,0},{6,2},{8,12},{10,14},{12,8},{14,10},{16,20},{18,... | collective-permute-start | bytes 1572872 | tf_op jit(solution)/shard_map/ppermute | solution.py:822
  210.7 27.1 %collective-permute-start.26 = (bf16[4,160,512]{2,1,0:T(8,128)(2,1)S(1)}, bf16[4,160,512]{2,1,0:T(8,128)(2,1)S(1)}, u32[]{:S(2)}, u32[]{:S(2)}) collective-permute-start(bf16[4,160,512]{2,1,0:T(8,128)(2,1)S(1)} %get-tuple-element.697), channel_id=1, source_target_pairs={{0,4},{2,6},{4,0},{6,2},{8,12},{10,14},{12,8},{14,10},{16,20},{18,... | collective-permute-start | bytes 1966088 | tf_op jit(solution)/shard_map/ppermute | solution.py:822
  238.8 40.0 %collective-permute-start.27 = (bf16[4,64,512]{2,1,0:T(8,128)(2,1)S(1)}, bf16[4,64,512]{2,1,0:T(8,128)(2,1)S(1)}, u32[]{:S(2)}, u32[]{:S(2)}) collective-permute-start(bf16[4,64,512]{2,1,0:T(8,128)(2,1)S(1)} %get-tuple-element.702), channel_id=1, source_target_pairs={{0,4},{2,6},{4,0},{6,2},{8,12},{10,14},{12,8},{14,10},{16,20},{18,... | collective-permute-start | bytes 786440 | tf_op jit(solution)/shard_map/ppermute | solution.py:822
  305.7 37.3 %collective-permute-start.57 = (bf16[8,192,512]{2,1,0:T(8,128)(2,1)S(1)}, bf16[8,192,512]{2,1,0:T(8,128)(2,1)S(1)}, u32[]{:S(2)}, u32[]{:S(2)}) collective-permute-start(bf16[8,192,512]{2,1,0:T(8,128)(2,1)S(1)} %pad_maximum_fusion.refs_1_), channel_id=1, source_target_pairs={{0,4},{2,6},{4,0},{6,2},{8,12},{10,14},{12,8},{14,10},{16,20},{18,... | collective-permute-start | bytes 4718600 | tf_op jit(solution)/shard_map/ppermute | solution.py:822
  309.9 49.7 %collective-permute-start.61 = (bf16[8,192,512]{2,1,0:T(8,128)(2,1)S(1)}, bf16[8,192,512]{2,1,0:T(8,128)(2,1)S(1)}, u32[]{:S(2)}, u32[]{:S(2)}) collective-permute-start(bf16[8,192,512]{2,1,0:T(8,128)(2,1)S(1)} %pad_maximum_fusion.1.refs_1_), channel_id=1, source_target_pairs={{0,2},{2,0},{4,6},{6,4},{8,10},{10,8},{12,14},{14,12},{16,18},{18,... | collective-permute-start | bytes 4718600 | tf_op jit(solution)/shard_map/ppermute | solution.py:822
  327.8 29.2 %collective-permute-start.62 = (bf16[4,160,512]{2,1,0:T(8,128)(2,1)S(1)}, bf16[4,160,512]{2,1,0:T(8,128)(2,1)S(1)}, u32[]{:S(2)}, u32[]{:S(2)}) collective-permute-start(bf16[4,160,512]{2,1,0:T(8,128)(2,1)S(1)} %pad_maximum_fusion.7), channel_id=1, source_target_pairs={{0,4},{2,6},{4,0},{6,2},{8,12},{10,14},{12,8},{14,10},{16,20},{18,... | collective-permute-start | bytes 1966088 | tf_op jit(solution)/shard_map/ppermute | solution.py:822
  333.7 49.6 %collective-permute-start.69 = (bf16[2,128,768]{2,1,0:T(8,128)(2,1)S(1)}, bf16[2,128,768]{2,1,0:T(8,128)(2,1)S(1)}, u32[]{:S(2)}, u32[]{:S(2)}) collective-permute-start(bf16[2,128,768]{2,1,0:T(8,128)(2,1)S(1)} %get-tuple-element.887), channel_id=1, source_target_pairs={{0,1},{1,0},{2,3},{3,2},{4,5},{5,4},{6,7},{7,6},{8,9},{9,8},{10,11... | collective-permute-start | bytes 1179656 | tf_op jit(solution)/shard_map/ppermute | solution.py:833
  363.9 31.8 %collective-permute-start.73 = (bf16[8,160,512]{2,1,0:T(8,128)(2,1)S(1)}, bf16[8,160,512]{2,1,0:T(8,128)(2,1)}, u32[]{:S(2)}, u32[]{:S(2)}) collective-permute-start(bf16[8,160,512]{2,1,0:T(8,128)(2,1)S(1)} %pad_maximum_fusion.2.refs_1_), channel_id=1, source_target_pairs={{0,8},{2,10},{4,12},{6,14},{8,0},{10,2},{12,4},{14,6},{16,24},{18,... | collective-permute-start | bytes 3932168 | tf_op jit(solution)/shard_map/ppermute | solution.py:822
  378.1 22.6 %collective-permute-start.76 = (bf16[8,64,512]{2,1,0:T(8,128)(2,1)}, bf16[8,64,512]{2,1,0:T(8,128)(2,1)}, u32[]{:S(2)}, u32[]{:S(2)}) collective-permute-start(bf16[8,64,512]{2,1,0:T(8,128)(2,1)} %pad_maximum_fusion.10.refs_1_), channel_id=1, source_target_pairs={{0,2},{2,0},{4,6},{6,4},{8,10},{10,8},{12,14},{14,12},{16,18},{18,... | collective-permute-start | bytes 1572872 | tf_op jit(solution)/shard_map/ppermute | solution.py:822
  381.9 22.9 %collective-permute-start.75 = (bf16[8,128,512]{2,1,0:T(8,128)(2,1)S(1)}, bf16[8,128,512]{2,1,0:T(8,128)(2,1)}, u32[]{:S(2)}, u32[]{:S(2)}) collective-permute-start(bf16[8,128,512]{2,1,0:T(8,128)(2,1)S(1)} %pad_maximum_fusion.3.refs_1_), channel_id=1, source_target_pairs={{0,4},{2,6},{4,0},{6,2},{8,12},{10,14},{12,8},{14,10},{16,20},{18,... | collective-permute-start | bytes 3145736 | tf_op jit(solution)/shard_map/ppermute | solution.py:822
  386.4 35.9 %collective-permute-start.81 = (bf16[8,128,512]{2,1,0:T(8,128)(2,1)S(1)}, bf16[8,128,512]{2,1,0:T(8,128)(2,1)}, u32[]{:S(2)}, u32[]{:S(2)}) collective-permute-start(bf16[8,128,512]{2,1,0:T(8,128)(2,1)S(1)} %pad_maximum_fusion.4.refs_1_), channel_id=1, source_target_pairs={{0,8},{2,10},{4,12},{6,14},{8,0},{10,2},{12,4},{14,6},{16,24},{18,... | collective-permute-start | bytes 3145736 | tf_op jit(solution)/shard_map/ppermute | solution.py:822
  393.8 22.8 %collective-permute-start.80 = (bf16[8,64,512]{2,1,0:T(8,128)(2,1)}, bf16[8,64,512]{2,1,0:T(8,128)(2,1)S(1)}, u32[]{:S(2)}, u32[]{:S(2)}) collective-permute-start(bf16[8,64,512]{2,1,0:T(8,128)(2,1)} %pad_maximum_fusion.12.refs_1_), channel_id=1, source_target_pairs={{0,2},{2,0},{4,6},{6,4},{8,10},{10,8},{12,14},{14,12},{16,18},{18,... | collective-permute-start | bytes 1572872 | tf_op jit(solution)/shard_map/ppermute | solution.py:822
  395.7 22.7 %collective-permute-start.79 = (bf16[8,64,512]{2,1,0:T(8,128)(2,1)}, bf16[8,64,512]{2,1,0:T(8,128)(2,1)S(1)}, u32[]{:S(2)}, u32[]{:S(2)}) collective-permute-start(bf16[8,64,512]{2,1,0:T(8,128)(2,1)} %pad_maximum_fusion.11.refs_1_), channel_id=1, source_target_pairs={{0,4},{2,6},{4,0},{6,2},{8,12},{10,14},{12,8},{14,10},{16,20},{18,... | collective-permute-start | bytes 1572872 | tf_op jit(solution)/shard_map/ppermute | solution.py:822
  (129 other events, 1124.8 us)

commit v4 on v3

--- a/solution.py
+++ b/solution.py
@@ -1213,18 +1213,19 @@
 
 PLAN = [
     stage_tokens, stage_self, stage_text, stage_norm_two, stage_cross, stage_norm_three,
-    stage_units, REST, UP, DOWN, stage_back_units, stage_back_three, stage_back_cross, DOWN,
-    REST, UP, stage_cross_packet, stage_back_two, REST, UP, CROSS, DOWN, stage_back_self, REST,
-    UP, DOWN, CROSS, stage_proj_packet, stage_query_packet, stage_key_packet, stage_value_packet,
-    REST, UP, PROJ, CROSS, KEY, QUERY, VALUE, DOWN, REST, REST, stage_out, stage_back_one, UP,
-    UP, QUERY, REST, REST, PROJ, PROJ, QUERY, VALUE, UP, UP, stage_result, CROSS, CROSS, VALUE,
-    REST, REST, PROJ, PROJ, UP, UP, KEY, KEY, CROSS, CROSS, DOWN, REST, REST, DOWN, QUERY, PROJ,
-    PROJ, KEY, UP, UP, KEY, VALUE, CROSS, CROSS, DOWN, QUERY, PROJ, PROJ, REST, REST, KEY, KEY,
-    QUERY, VALUE, CROSS, CROSS, QUERY, PROJ, PROJ, UP, UP, KEY, KEY, VALUE, VALUE, QUERY, QUERY,
-    CROSS, CROSS, KEY, KEY, PROJ, PROJ, DOWN, VALUE, VALUE, QUERY, QUERY, KEY, KEY, REST, DOWN,
-    DOWN, VALUE, VALUE, QUERY, QUERY, CROSS, CROSS, UP, VALUE, VALUE, DOWN, DOWN, PROJ, PROJ,
-    QUERY, QUERY, KEY, KEY, VALUE, VALUE, stage_text_grad, DOWN, DOWN, stage_small, stage_hop,
-    CROSS, stage_hop, QUERY, PROJ, stage_hop, stage_hop, stage_rms, VALUE, KEY, DOWN, stage_end,
+    stage_units, REST, UP, DOWN, stage_back_units, stage_back_three, stage_back_cross, REST, UP,
+    stage_cross_packet, DOWN, stage_back_two, REST, UP, CROSS, DOWN, stage_back_self, REST, UP,
+    DOWN, stage_proj_packet, stage_key_packet, stage_value_packet, REST, CROSS, UP, PROJ,
+    stage_query_packet, CROSS, KEY, QUERY, VALUE, DOWN, REST, REST, stage_back_one, UP,
+    stage_out, UP, QUERY, REST, REST, PROJ, PROJ, QUERY, VALUE, UP, UP, stage_result, CROSS,
+    CROSS, REST, VALUE, REST, PROJ, PROJ, UP, KEY, KEY, UP, CROSS, CROSS, DOWN, REST, REST,
+    QUERY, DOWN, PROJ, PROJ, KEY, UP, UP, KEY, VALUE, CROSS, REST, CROSS, DOWN, QUERY, PROJ,
+    PROJ, REST, KEY, KEY, QUERY, VALUE, CROSS, CROSS, QUERY, PROJ, PROJ, UP, UP, KEY, KEY, VALUE,
+    VALUE, QUERY, QUERY, CROSS, CROSS, KEY, KEY, QUERY, PROJ, PROJ, DOWN, VALUE, VALUE, QUERY,
+    KEY, KEY, REST, DOWN, DOWN, VALUE, VALUE, QUERY, QUERY, CROSS, CROSS, UP, VALUE, VALUE, DOWN,
+    DOWN, PROJ, PROJ, QUERY, QUERY, KEY, KEY, VALUE, stage_text_grad, DOWN, DOWN, stage_small,
+    VALUE, stage_hop, CROSS, stage_hop, QUERY, stage_hop, stage_hop, VALUE, DOWN, PROJ, KEY,
+    stage_rms, stage_end,
 ]
 
 def per_device(

time: 435 us -> 417 us (0.959)
  waiting for transfers between devices: 168 us -> 159 us
  starting transfers between devices: 80.5 us -> 73.2 us
    ppermute x68, waiting for transfers between devices: 157 us -> 146 us  [exchange(): return lax.ppermute(values, 'dp', pairs)]
    ppermute x68, starting transfers between devices: 77.7 us -> 70.2 us  [exchange(): return lax.ppermute(values, 'dp', pairs)]
  transfers between devices with their start and end apart: 82 -> 82, of which waited for: 39 -> 38; matrix products, arithmetic and copies ran while one was open for 3% -> 3% of each run, Pallas kernels for 21% -> 22%
where the time goes in v4:
time: 417 us; the launch traced here: 409 us
  waiting for transfers between devices  159 us (38%)
  Pallas kernels  148 us (35%)
  starting transfers between devices  73.2 us (18%)
  local copies, waits for them, and re-layouts  16.1 us (4%)
  other arithmetic  10.1 us (2%)
    ppermute x68, waiting for transfers between devices, exchange(): return lax.ppermute(values, 'dp', pairs)  146 us
    pallas_call x15, Pallas kernels, call(): pl.pallas_call(body, grid=grid, in_specs=in_specs, out_specs=out_specs, o...  111 us
    ppermute x68, starting transfers between devices, exchange(): return lax.ppermute(values, 'dp', pairs)  70.2 us
    pallas_call x8, Pallas kernels, open_packet(): pl.pallas_call(body, grid=(steps,), in_specs=[SMEM_SPEC, whole(kept.shape...  24 us
    unnamed x142, local copies, waits for them, and re-layouts  13.4 us
    ppermute x14, waiting for transfers between devices, swap_cores(): return lax.ppermute(values, 'mp', SWAP)  12.1 us
  transfers between devices with their start and end apart: 82, of which 38 were waited for; matrix products, arithmetic and copies ran while one was open for 3% of the time, Pallas kernels for 22%

profile of v4, /device:TPU:0, one launch (start us, length us, event | category | flops | bytes accessed | tf_op | source)
XLA Modules:
  0.0 409.2 jit_solution(15206988732296425277)
XLA Ops:
  7.3 5.0 %shard_map.356 = (bf16[1024,1024]{1,0:T(8,128)(2,1)S(1)}, bf16[1024,512]{1,0:T(8,128)(2,1)S(1)}, bf16[1024,512]{1,0:T(8,128)(2,1)S(1)}, bf16[1024,512]{1,0:T(8,128)(2,1)S(1)}) custom-call(bf16[1024,1024]{1,0:T(8,128)(2,1)S(1)} %bitcast.36, bf16[1,1024]{1,0:T(2,128)(2,1)S(1)} %reshape.142.g, bf16[1,1024]{1,0:T(2,128)(2,1)S(1)} %reshape.143.b, ...), custom_call_target="tpu_custom_call" | custom-call | bytes 1024 | tf_op jit(solution)/shard_map/pallas_call | solution.py:54
  13.7 8.1 %shard_map.357 = (bf16[2,2,256,512]{3,2,1,0:T(8,128)(2,1)S(1)}, f32[2,8,512]{2,1,0:T(8,128)S(1)}, f32[2,256,1024]{2,1,0:T(8,128)S(1)}, bf16[2,256,1024]{2,1,0:T(8,128)(2,1)S(1)}) custom-call(s32[1]{0:T(128)} %bitcast.rank_ref, s32[2]{0:T(128)S(1)} %copy-done.56, bf16[2,512,512]{2,1,0:T(8,128)(2,1)S(1)} %bitcast.37, bf16[2,512,512]{2,1,0:T(8,128)(2,1)S(1)} %bitcast.39, ...), custom_call_target="tpu_custom_call" | custom-call | bytes 1024 | tf_op jit(solution)/shard_map/pallas_call | solution.py:54
  30.9 7.7 %shard_map.360 = (bf16[2,2,256,512]{3,2,1,0:T(8,128)(2,1)S(1)}, bf16[2,2,256,512]{3,2,1,0:T(8,128)(2,1)S(1)}, f32[2,8,512]{2,1,0:T(8,128)S(1)}, f32[2,256,1024]{2,1,0:T(8,128)S(1)}, bf16[2,256,1024]{2,1,0:T(8,128)(2,1)S(1)}) custom-call(s32[1]{0:T(128)} %bitcast.rank_ref, s32[2]{0:T(128)S(1)} %copy-done.65, ...), custom_call_target="tpu_custom_call" | custom-call | bytes 1024 | tf_op jit(solution)/shard_map/pallas_call | solution.py:54
  49.0 24.9 %shard_map.362 = (bf16[2,512,2048]{2,1,0:T(8,128)(2,1)}, bf16[2,512,2048]{2,1,0:T(8,128)(2,1)}, bf16[8,128,512]{2,1,0:T(8,128)(2,1)S(1)}, bf16[8,128,512]{2,1,0:...) custom-call(s32[1]{0:T(128)} %bitcast.5.me_ref.refs_0_, ...), custom_call_target="tpu_custom_call" | custom-call | bytes 1024 | tf_op jit(solution)/shard_map/pallas_call | solution.py:54
  76.1 5.0 %shard_map.363 = (f32[512,1024]{1,0:T(8,128)S(1)}, bf16[512,1024]{1,0:T(8,128)(2,1)S(1)}) custom-call(bf16[2,512,2048]{2,1,0:T(8,128)(2,1)S(1)} %copy-done.24, bf16[1024,2048]{1,0:T(8,128)(2,1)S(1)} %copy-done.4), custom_call_target="tpu_custom_call" | custom-call | bytes 1024 | tf_op jit(solution)/shard_map/pallas_call | solution.py:54
  91.6 18.1 %shard_map.365 = (bf16[2,2,256,512]{3,2,1,0:T(8,128)(2,1)S(1)}, bf16[2,2,128,512]{3,2,1,0:T(8,128)(2,1)S(1)}, bf16[2,2,128,512]{3,2,1,0:T(8,128)(2,1)S(1)}, f32[...) custom-call(s32[1]{0:T(128)} %bitcast.rank_ref, ...), custom_call_target="tpu_custom_call" | custom-call | bytes 1024 | tf_op jit(solution)/shard_map/pallas_call | solution.py:54
  109.9 9.1 %collective-permute-done.7 = bf16[8,192,512]{2,1,0:T(8,128)(2,1)S(1)} collective-permute-done((bf16[8,192,512]{2,1,0:T(8,128)(2,1)S(1)}, bf16[8,192,512]{2,1,0:T(8,128)(2,1)S(1)}, u32[]{:S(2)}, u32[]{:S(2)}) %collective-permute-start.7) | collective-permute-done | bytes 1572896 | tf_op jit(solution)/shard_map/ppermute | solution.py:822
  134.5 20.9 %shard_map.368 = (bf16[2,512,512]{2,1,0:T(8,128)(2,1)S(1)}, bf16[2,512,512]{2,1,0:T(8,128)(2,1)S(1)}, bf16[2,512,512]{2,1,0:T(8,128)(2,1)S(1)}, f32[2,256,1024]{2,1,0:T(8,128)S(1)}, bf16[2,256,1024]{2,1,0:T(8,128)(2,1)S(1)}) custom-call(s32[1]{0:T(128)} %bitcast.rank_ref, s32[2]{0:T(128)S(1)} %copy-done.56, ...), custom_call_target="tpu_custom_call" | custom-call | bytes 1024 | tf_op jit(solution)/shard_map/pallas_call | solution.py:54
  156.0 5.2 %collective-permute-done.16 = bf16[4,128,512]{2,1,0:T(8,128)(2,1)S(1)} collective-permute-done((bf16[4,128,512]{2,1,0:T(8,128)(2,1)S(1)}, bf16[4,128,512]{2,1,0:T(8,128)(2,1)S(1)}, u32[]{:S(2)}, u32[]{:S(2)}) %collective-permute-start.16) | collective-permute-done | bytes 524320 | tf_op jit(solution)/shard_map/ppermute | solution.py:822
  161.4 4.4 %shard_map.369 = (bf16[8,128,512]{2,1,0:T(8,128)(2,1)S(1)}, bf16[8,128,512]{2,1,0:T(8,128)(2,1)S(1)}) custom-call(s32[1]{0:T(128)} %bitcast.5.me_ref.refs_0_, bf16[2,512,512]{2,1,0:T(8,128)(2,1)S(1)} %bitcast.52, bf16[512,1024]{1,0:T(8,128)(2,1)S(1)} %bitcast.43, bf16[512,1024]{1,0:T(8,128)(2,1)S(1)} %bitcast.44, bf16[2,512,512]{2,1,0:T(8,128)(2,1)S(1)} %bitcast.51, ...), custom_call_target="tpu_custom_call" | custom-call | bytes 1024 | tf_op jit(solution)/shard_map/pallas_call | solution.py:54
  175.3 5.7 %collective-permute-done.18 = bf16[2,192,512]{2,1,0:T(8,128)(2,1)S(1)} collective-permute-done((bf16[2,192,512]{2,1,0:T(8,128)(2,1)S(1)}, bf16[2,192,512]{2,1,0:T(8,128)(2,1)S(1)}, u32[]{:S(2)}, u32[]{:S(2)}) %collective-permute-start.18) | collective-permute-done | bytes 393248 | tf_op jit(solution)/shard_map/ppermute | solution.py:822
  190.7 4.9 %shard_map.374 = (f32[512,1024]{1,0:T(8,128)S(1)}, bf16[512,1024]{1,0:T(8,128)(2,1)S(1)}) custom-call(bf16[2,512,2048]{2,1,0:T(8,128)(2,1)S(1)} %copy-done.23, bf16[2048,1024]{1,0:T(8,128)(2,1)S(1)} %copy-done.5), custom_call_target="tpu_custom_call" | custom-call | bytes 1024 | tf_op jit(solution)/shard_map/pallas_call | solution.py:54
  201.5 10.1 %collective-permute-done.20 = bf16[1,192,512]{2,1,0:T(8,128)(2,1)S(1)} collective-permute-done((bf16[1,192,512]{2,1,0:T(8,128)(2,1)S(1)}, bf16[1,192,512]{2,1,0:T(8,128)(2,1)S(1)}, u32[]{:S(2)}, u32[]{:S(2)}) %collective-permute-start.20) | collective-permute-done | bytes 196640 | tf_op jit(solution)/shard_map/ppermute | solution.py:822
  218.7 8.9 %collective-permute-done.26 = bf16[1,192,512]{2,1,0:T(8,128)(2,1)S(1)} collective-permute-done((bf16[1,192,512]{2,1,0:T(8,128)(2,1)S(1)}, bf16[1,192,512]{2,1,0:T(8,128)(2,1)S(1)}, u32[]{:S(2)}, u32[]{:S(2)}) %collective-permute-start.26) | collective-permute-done | bytes 196640 | tf_op jit(solution)/shard_map/ppermute | solution.py:822
  233.9 6.7 %collective-permute-done.35 = bf16[2,160,512]{2,1,0:T(8,128)(2,1)S(1)} collective-permute-done((bf16[2,160,512]{2,1,0:T(8,128)(2,1)S(1)}, bf16[2,160,512]{2,1,0:T(8,128)(2,1)S(1)}, u32[]{:S(2)}, u32[]{:S(2)}) %collective-permute-start.35) | collective-permute-done | bytes 327712 | tf_op jit(solution)/shard_map/ppermute | solution.py:822
  241.3 8.0 %collective-permute-done.37 = bf16[2,192,512]{2,1,0:T(8,128)(2,1)S(1)} collective-permute-done((bf16[2,192,512]{2,1,0:T(8,128)(2,1)S(1)}, bf16[2,192,512]{2,1,0:T(8,128)(2,1)S(1)}, u32[]{:S(2)}, u32[]{:S(2)}) %collective-permute-start.37) | collective-permute-done | bytes 393248 | tf_op jit(solution)/shard_map/ppermute | solution.py:822
  251.8 8.3 %collective-permute-done.38 = bf16[2,192,512]{2,1,0:T(8,128)(2,1)S(1)} collective-permute-done((bf16[2,192,512]{2,1,0:T(8,128)(2,1)S(1)}, bf16[2,192,512]{2,1,0:T(8,128)(2,1)S(1)}, u32[]{:S(2)}, u32[]{:S(2)}) %collective-permute-start.38) | collective-permute-done | bytes 393248 | tf_op jit(solution)/shard_map/ppermute | solution.py:822
  276.5 4.9 %collective-permute-done.42 = bf16[2,64,512]{2,1,0:T(8,128)(2,1)S(1)} collective-permute-done((bf16[2,64,512]{2,1,0:T(8,128)(2,1)S(1)}, bf16[2,64,512]{2,1,0:T(8,128)(2,1)S(1)}, u32[]{:S(2)}, u32[]{:S(2)}) %collective-permute-start.42) | collective-permute-done | bytes 131104 | tf_op jit(solution)/shard_map/ppermute | solution.py:822
  290.8 9.0 %collective-permute-done.52 = bf16[1,64,512]{2,1,0:T(8,128)(2,1)S(1)} collective-permute-done((bf16[1,64,512]{2,1,0:T(8,128)(2,1)S(1)}, bf16[1,64,512]{2,1,0:T(8,128)(2,1)S(1)}, u32[]{:S(2)}, u32[]{:S(2)}) %collective-permute-start.52) | collective-permute-done | bytes 65568 | tf_op jit(solution)/shard_map/ppermute | solution.py:822
  303.0 10.6 %collective-permute-done.53 = bf16[1,64,512]{2,1,0:T(8,128)(2,1)S(1)} collective-permute-done((bf16[1,64,512]{2,1,0:T(8,128)(2,1)S(1)}, bf16[1,64,512]{2,1,0:T(8,128)(2,1)S(1)}, u32[]{:S(2)}, u32[]{:S(2)}) %collective-permute-start.53) | collective-permute-done | bytes 65568 | tf_op jit(solution)/shard_map/ppermute | solution.py:822
  342.5 4.7 %collective-permute-done.66 = bf16[4,64,512]{2,1,0:T(8,128)(2,1)S(1)} collective-permute-done((bf16[4,64,512]{2,1,0:T(8,128)(2,1)S(1)}, bf16[4,64,512]{2,1,0:T(8,128)(2,1)S(1)}, u32[]{:S(2)}, u32[]{:S(2)}) %collective-permute-start.66) | collective-permute-done | bytes 262176 | tf_op jit(solution)/shard_map/ppermute | solution.py:822
  353.6 9.3 %collective-permute-done.70 = bf16[4,128,512]{2,1,0:T(8,128)(2,1)S(1)} collective-permute-done((bf16[4,128,512]{2,1,0:T(8,128)(2,1)S(1)}, bf16[4,128,512]{2,1,0:T(8,128)(2,1)S(1)}, u32[]{:S(2)}, u32[]{:S(2)}) %collective-permute-start.70) | collective-permute-done | bytes 524320 | tf_op jit(solution)/shard_map/ppermute | solution.py:822
  367.0 4.2 %collective-permute-done.72 = f32[16,1024]{1,0:T(8,128)S(1)} collective-permute-done((f32[16,1024]{1,0:T(8,128)S(1)}, f32[16,1024]{1,0:T(8,128)S(1)}, u32[]{:S(2)}, u32[]{:S(2)}) %collective-permute-start.72) | collective-permute-done | bytes 65568 | tf_op jit(solution)/shard_map/ppermute | solution.py:822
  382.8 9.1 %collective-permute-done.76 = f32[16,1024]{1,0:T(8,128)S(1)} collective-permute-done((f32[16,1024]{1,0:T(8,128)S(1)}, f32[16,1024]{1,0:T(8,128)S(1)}, u32[]{:S(2)}, u32[]{:S(2)}) %collective-permute-start.76) | collective-permute-done | bytes 65568 | tf_op jit(solution)/shard_map/ppermute | solution.py:822
  (387 shorter events, 192.6 us)
Async XLA Ops:
  81.6 37.5 %collective-permute-start.7 = (bf16[8,192,512]{2,1,0:T(8,128)(2,1)S(1)}, bf16[8,192,512]{2,1,0:T(8,128)(2,1)S(1)}, u32[]{:S(2)}, u32[]{:S(2)}) collective-permute-start(bf16[8,192,512]{2,1,0:T(8,128)(2,1)S(1)} %get-tuple-element.546), channel_id=1, source_target_pairs={{0,4},{2,6},{4,0},{6,2},{8,12},{10,14},{12,8},{14,10},{16,20},{18,... | collective-permute-start | bytes 4718600 | tf_op jit(solution)/shard_map/ppermute | solution.py:822
  84.1 36.4 %collective-permute-start.6 = (bf16[8,192,512]{2,1,0:T(8,128)(2,1)S(1)}, bf16[8,192,512]{2,1,0:T(8,128)(2,1)S(1)}, u32[]{:S(2)}, u32[]{:S(2)}) collective-permute-start(bf16[8,192,512]{2,1,0:T(8,128)(2,1)S(1)} %get-tuple-element.544), channel_id=1, source_target_pairs={{0,2},{2,0},{4,6},{6,4},{8,10},{10,8},{12,14},{14,12},{16,18},{18,... | collective-permute-start | bytes 4718600 | tf_op jit(solution)/shard_map/ppermute | solution.py:822
  88.9 37.4 %collective-permute-start.10 = (bf16[8,128,512]{2,1,0:T(8,128)(2,1)S(1)}, bf16[8,128,512]{2,1,0:T(8,128)(2,1)S(1)}, u32[]{:S(2)}, u32[]{:S(2)}) collective-permute-start(bf16[8,128,512]{2,1,0:T(8,128)(2,1)S(1)} %get-tuple-element.573), channel_id=1, source_target_pairs={{0,8},{2,10},{4,12},{6,14},{8,0},{10,2},{12,4},{14,6},{16,24},{18,... | collective-permute-start | bytes 3145736 | tf_op jit(solution)/shard_map/ppermute | solution.py:822
  130.0 25.5 %collective-permute-start.13 = (bf16[4,192,512]{2,1,0:T(8,128)(2,1)S(1)}, bf16[4,192,512]{2,1,0:T(8,128)(2,1)S(1)}, u32[]{:S(2)}, u32[]{:S(2)}) collective-permute-start(bf16[4,192,512]{2,1,0:T(8,128)(2,1)S(1)} %get-tuple-element.593), channel_id=1, source_target_pairs={{0,2},{2,0},{4,6},{6,4},{8,10},{10,8},{12,14},{14,12},{16,18},{18,... | collective-permute-start | bytes 2359304 | tf_op jit(solution)/shard_map/ppermute | solution.py:822
  131.6 38.9 %collective-permute-start.15 = (bf16[8,160,512]{2,1,0:T(8,128)(2,1)S(1)}, bf16[8,160,512]{2,1,0:T(8,128)(2,1)S(1)}, u32[]{:S(2)}, u32[]{:S(2)}) collective-permute-start(bf16[8,160,512]{2,1,0:T(8,128)(2,1)S(1)} %get-tuple-element.612), channel_id=1, source_target_pairs={{0,8},{2,10},{4,12},{6,14},{8,0},{10,2},{12,4},{14,6},{16,24},{18,... | collective-permute-start | bytes 3932168 | tf_op jit(solution)/shard_map/ppermute | solution.py:822
  133.2 22.5 %collective-permute-start.12 = (bf16[4,192,512]{2,1,0:T(8,128)(2,1)S(1)}, bf16[4,192,512]{2,1,0:T(8,128)(2,1)S(1)}, u32[]{:S(2)}, u32[]{:S(2)}) collective-permute-start(bf16[4,192,512]{2,1,0:T(8,128)(2,1)S(1)} %get-tuple-element.592), channel_id=1, source_target_pairs={{0,4},{2,6},{4,0},{6,2},{8,12},{10,14},{12,8},{14,10},{16,20},{18,... | collective-permute-start | bytes 2359304 | tf_op jit(solution)/shard_map/ppermute | solution.py:822
  133.9 27.3 %collective-permute-start.16 = (bf16[4,128,512]{2,1,0:T(8,128)(2,1)S(1)}, bf16[4,128,512]{2,1,0:T(8,128)(2,1)S(1)}, u32[]{:S(2)}, u32[]{:S(2)}) collective-permute-start(bf16[4,128,512]{2,1,0:T(8,128)(2,1)S(1)} %get-tuple-element.616), channel_id=1, source_target_pairs={{0,2},{2,0},{4,6},{6,4},{8,10},{10,8},{12,14},{14,12},{16,18},{18,... | collective-permute-start | bytes 1572872 | tf_op jit(solution)/shard_map/ppermute | solution.py:822
  155.7 26.8 %collective-permute-start.19 = (bf16[2,256,1024]{2,1,0:T(8,128)(2,1)S(1)}, bf16[2,256,1024]{2,1,0:T(8,128)(2,1)S(1)}, u32[]{:S(2)}, u32[]{:S(2)}) collective-permute-start(bf16[2,256,1024]{2,1,0:T(8,128)(2,1)S(1)} %get-tuple-element.665), channel_id=1, source_target_pairs={{0,1},{1,0},{2,3},{3,2},{4,5},{5,4},{6,7},{7,6},{8,9},{9,8},{10,11... | collective-permute-start | bytes 3145736 | tf_op jit(solution)/shard_map/ppermute | solution.py:833
  171.4 28.2 %collective-permute-start.23 = (bf16[8,128,512]{2,1,0:T(8,128)(2,1)S(1)}, bf16[8,128,512]{2,1,0:T(8,128)(2,1)S(1)}, u32[]{:S(2)}, u32[]{:S(2)}) collective-permute-start(bf16[8,128,512]{2,1,0:T(8,128)(2,1)S(1)} %get-tuple-element.689), channel_id=1, source_target_pairs={{0,4},{2,6},{4,0},{6,2},{8,12},{10,14},{12,8},{14,10},{16,20},{18,... | collective-permute-start | bytes 3145736 | tf_op jit(solution)/shard_map/ppermute | solution.py:822
  173.7 21.9 %collective-permute-start.22 = (bf16[8,64,512]{2,1,0:T(8,128)(2,1)S(1)}, bf16[8,64,512]{2,1,0:T(8,128)(2,1)S(1)}, u32[]{:S(2)}, u32[]{:S(2)}) collective-permute-start(bf16[8,64,512]{2,1,0:T(8,128)(2,1)S(1)} %get-tuple-element.683), channel_id=1, source_target_pairs={{0,2},{2,0},{4,6},{6,4},{8,10},{10,8},{12,14},{14,12},{16,18},{18,... | collective-permute-start | bytes 1572872 | tf_op jit(solution)/shard_map/ppermute | solution.py:822
  182.5 33.1 %collective-permute-start.27 = (bf16[4,160,512]{2,1,0:T(8,128)(2,1)S(1)}, bf16[4,160,512]{2,1,0:T(8,128)(2,1)S(1)}, u32[]{:S(2)}, u32[]{:S(2)}) collective-permute-start(bf16[4,160,512]{2,1,0:T(8,128)(2,1)S(1)} %get-tuple-element.714), channel_id=1, source_target_pairs={{0,4},{2,6},{4,0},{6,2},{8,12},{10,14},{12,8},{14,10},{16,20},{18,... | collective-permute-start | bytes 1966088 | tf_op jit(solution)/shard_map/ppermute | solution.py:822
  198.7 33.2 %collective-permute-start.29 = (bf16[8,64,512]{2,1,0:T(8,128)(2,1)S(1)}, bf16[8,64,512]{2,1,0:T(8,128)(2,1)S(1)}, u32[]{:S(2)}, u32[]{:S(2)}) collective-permute-start(bf16[8,64,512]{2,1,0:T(8,128)(2,1)S(1)} %get-tuple-element.724), channel_id=1, source_target_pairs={{0,4},{2,6},{4,0},{6,2},{8,12},{10,14},{12,8},{14,10},{16,20},{18,... | collective-permute-start | bytes 1572872 | tf_op jit(solution)/shard_map/ppermute | solution.py:822
  199.6 41.6 %collective-permute-start.34 = (bf16[2,128,512]{2,1,0:T(8,128)(2,1)S(1)}, bf16[2,128,512]{2,1,0:T(8,128)(2,1)S(1)}, u32[]{:S(2)}, u32[]{:S(2)}) collective-permute-start(bf16[2,128,512]{2,1,0:T(8,128)(2,1)S(1)} %get-tuple-element.740), channel_id=1, source_target_pairs={{0,4},{2,6},{4,0},{6,2},{8,12},{10,14},{12,8},{14,10},{16,20},{18,... | collective-permute-start | bytes 786440 | tf_op jit(solution)/shard_map/ppermute | solution.py:822
  227.6 21.9 %collective-permute-start.36 = (bf16[4,64,512]{2,1,0:T(8,128)(2,1)S(1)}, bf16[4,64,512]{2,1,0:T(8,128)(2,1)S(1)}, u32[]{:S(2)}, u32[]{:S(2)}) collective-permute-start(bf16[4,64,512]{2,1,0:T(8,128)(2,1)S(1)} %get-tuple-element.751), channel_id=1, source_target_pairs={{0,4},{2,6},{4,0},{6,2},{8,12},{10,14},{12,8},{14,10},{16,20},{18,... | collective-permute-start | bytes 786440 | tf_op jit(solution)/shard_map/ppermute | solution.py:822
  263.2 21.7 %collective-permute-start.47 = (bf16[4,192,512]{2,1,0:T(8,128)(2,1)S(1)}, bf16[4,192,512]{2,1,0:T(8,128)(2,1)S(1)}, u32[]{:S(2)}, u32[]{:S(2)}) collective-permute-start(bf16[4,192,512]{2,1,0:T(8,128)(2,1)S(1)} %pad_maximum_fusion.6), channel_id=1, source_target_pairs={{0,4},{2,6},{4,0},{6,2},{8,12},{10,14},{12,8},{14,10},{16,20},{18,... | collective-permute-start | bytes 2359304 | tf_op jit(solution)/shard_map/ppermute | solution.py:822
  281.4 39.9 %collective-permute-start.58 = (bf16[8,192,512]{2,1,0:T(8,128)(2,1)S(1)}, bf16[8,192,512]{2,1,0:T(8,128)(2,1)S(1)}, u32[]{:S(2)}, u32[]{:S(2)}) collective-permute-start(bf16[8,192,512]{2,1,0:T(8,128)(2,1)S(1)} %pad_maximum_fusion.refs_1_), channel_id=1, source_target_pairs={{0,4},{2,6},{4,0},{6,2},{8,12},{10,14},{12,8},{14,10},{16,20},{18,... | collective-permute-start | bytes 4718600 | tf_op jit(solution)/shard_map/ppermute | solution.py:822
  289.9 43.5 %collective-permute-start.61 = (bf16[8,192,512]{2,1,0:T(8,128)(2,1)S(1)}, bf16[8,192,512]{2,1,0:T(8,128)(2,1)S(1)}, u32[]{:S(2)}, u32[]{:S(2)}) collective-permute-start(bf16[8,192,512]{2,1,0:T(8,128)(2,1)S(1)} %pad_maximum_fusion.1.refs_1_), channel_id=1, source_target_pairs={{0,2},{2,0},{4,6},{6,4},{8,10},{10,8},{12,14},{14,12},{16,18},{18,... | collective-permute-start | bytes 4718600 | tf_op jit(solution)/shard_map/ppermute | solution.py:822
  321.2 31.5 %collective-permute-start.69 = (bf16[2,128,768]{2,1,0:T(8,128)(2,1)S(1)}, bf16[2,128,768]{2,1,0:T(8,128)(2,1)S(1)}, u32[]{:S(2)}, u32[]{:S(2)}) collective-permute-start(bf16[2,128,768]{2,1,0:T(8,128)(2,1)S(1)} %get-tuple-element.913), channel_id=1, source_target_pairs={{0,1},{1,0},{2,3},{3,2},{4,5},{5,4},{6,7},{7,6},{8,9},{9,8},{10,11... | collective-permute-start | bytes 1179656 | tf_op jit(solution)/shard_map/ppermute | solution.py:833
  339.2 33.6 %collective-permute-start.73 = (bf16[8,160,512]{2,1,0:T(8,128)(2,1)S(1)}, bf16[8,160,512]{2,1,0:T(8,128)(2,1)}, u32[]{:S(2)}, u32[]{:S(2)}) collective-permute-start(bf16[8,160,512]{2,1,0:T(8,128)(2,1)S(1)} %pad_maximum_fusion.2.refs_1_), channel_id=1, source_target_pairs={{0,8},{2,10},{4,12},{6,14},{8,0},{10,2},{12,4},{14,6},{16,24},{18,... | collective-permute-start | bytes 3932168 | tf_op jit(solution)/shard_map/ppermute | solution.py:822
  349.4 28.7 %collective-permute-start.75 = (bf16[8,64,512]{2,1,0:T(8,128)(2,1)}, bf16[8,64,512]{2,1,0:T(8,128)(2,1)}, u32[]{:S(2)}, u32[]{:S(2)}) collective-permute-start(bf16[8,64,512]{2,1,0:T(8,128)(2,1)} %pad_maximum_fusion.10.refs_1_), channel_id=1, source_target_pairs={{0,2},{2,0},{4,6},{6,4},{8,10},{10,8},{12,14},{14,12},{16,18},{18,... | collective-permute-start | bytes 1572872 | tf_op jit(solution)/shard_map/ppermute | solution.py:822
  350.9 51.9 %collective-permute-start.79 = (bf16[8,128,512]{2,1,0:T(8,128)(2,1)S(1)}, bf16[8,128,512]{2,1,0:T(8,128)(2,1)}, u32[]{:S(2)}, u32[]{:S(2)}) collective-permute-start(bf16[8,128,512]{2,1,0:T(8,128)(2,1)S(1)} %pad_maximum_fusion.3.refs_1_), channel_id=1, source_target_pairs={{0,4},{2,6},{4,0},{6,2},{8,12},{10,14},{12,8},{14,10},{16,20},{18,... | collective-permute-start | bytes 3145736 | tf_op jit(solution)/shard_map/ppermute | solution.py:822
  363.0 36.2 %collective-permute-start.80 = (bf16[8,128,512]{2,1,0:T(8,128)(2,1)S(1)}, bf16[8,128,512]{2,1,0:T(8,128)(2,1)}, u32[]{:S(2)}, u32[]{:S(2)}) collective-permute-start(bf16[8,128,512]{2,1,0:T(8,128)(2,1)S(1)} %pad_maximum_fusion.4.refs_1_), channel_id=1, source_target_pairs={{0,8},{2,10},{4,12},{6,14},{8,0},{10,2},{12,4},{14,6},{16,24},{18,... | collective-permute-start | bytes 3145736 | tf_op jit(solution)/shard_map/ppermute | solution.py:822
  371.3 22.7 %collective-permute-start.81 = (bf16[8,64,512]{2,1,0:T(8,128)(2,1)}, bf16[8,64,512]{2,1,0:T(8,128)(2,1)S(1)}, u32[]{:S(2)}, u32[]{:S(2)}) collective-permute-start(bf16[8,64,512]{2,1,0:T(8,128)(2,1)} %pad_maximum_fusion.12.refs_1_), channel_id=1, source_target_pairs={{0,2},{2,0},{4,6},{6,4},{8,10},{10,8},{12,14},{14,12},{16,18},{18,... | collective-permute-start | bytes 1572872 | tf_op jit(solution)/shard_map/ppermute | solution.py:822
  378.1 28.3 %collective-permute-start.78 = (bf16[8,64,512]{2,1,0:T(8,128)(2,1)S(1)}, bf16[8,64,512]{2,1,0:T(8,128)(2,1)S(1)}, u32[]{:S(2)}, u32[]{:S(2)}) collective-permute-start(bf16[8,64,512]{2,1,0:T(8,128)(2,1)S(1)} %copy-done.37), channel_id=1, source_target_pairs={{0,4},{2,6},{4,0},{6,2},{8,12},{10,14},{12,8},{14,10},{16,20},{18,... | collective-permute-start | bytes 1572872 | tf_op jit(solution)/shard_map/ppermute | solution.py:822
  (129 other events, 1110.1 us)

commit v5 on v4

--- a/solution.py
+++ b/solution.py
@@ -1213,18 +1213,18 @@
 
 PLAN = [
     stage_tokens, stage_self, stage_text, stage_norm_two, stage_cross, stage_norm_three,
-    stage_units, REST, UP, DOWN, stage_back_units, stage_back_three, stage_back_cross, REST, UP,
-    stage_cross_packet, DOWN, stage_back_two, REST, UP, CROSS, DOWN, stage_back_self, REST, UP,
-    DOWN, stage_proj_packet, stage_key_packet, stage_value_packet, REST, CROSS, UP, PROJ,
+    stage_units, REST, UP, DOWN, stage_back_units, stage_back_three, stage_back_cross, REST,
+    stage_cross_packet, DOWN, UP, stage_back_two, REST, UP, CROSS, DOWN, stage_back_self, REST,
+    UP, DOWN, stage_proj_packet, stage_value_packet, REST, CROSS, stage_key_packet, UP, PROJ,
     stage_query_packet, CROSS, KEY, QUERY, VALUE, DOWN, REST, REST, stage_back_one, UP,
     stage_out, UP, QUERY, REST, REST, PROJ, PROJ, QUERY, VALUE, UP, UP, stage_result, CROSS,
-    CROSS, REST, VALUE, REST, PROJ, PROJ, UP, KEY, KEY, UP, CROSS, CROSS, DOWN, REST, REST,
+    DOWN, CROSS, REST, KEY, VALUE, REST, PROJ, PROJ, KEY, UP, UP, CROSS, CROSS, REST, REST,
     QUERY, DOWN, PROJ, PROJ, KEY, UP, UP, KEY, VALUE, CROSS, REST, CROSS, DOWN, QUERY, PROJ,
-    PROJ, REST, KEY, KEY, QUERY, VALUE, CROSS, CROSS, QUERY, PROJ, PROJ, UP, UP, KEY, KEY, VALUE,
+    REST, PROJ, KEY, KEY, QUERY, VALUE, CROSS, CROSS, QUERY, PROJ, PROJ, UP, UP, KEY, KEY, VALUE,
     VALUE, QUERY, QUERY, CROSS, CROSS, KEY, KEY, QUERY, PROJ, PROJ, DOWN, VALUE, VALUE, QUERY,
     KEY, KEY, REST, DOWN, DOWN, VALUE, VALUE, QUERY, QUERY, CROSS, CROSS, UP, VALUE, VALUE, DOWN,
     DOWN, PROJ, PROJ, QUERY, QUERY, KEY, KEY, VALUE, stage_text_grad, DOWN, DOWN, stage_small,
-    VALUE, stage_hop, CROSS, stage_hop, QUERY, stage_hop, stage_hop, VALUE, DOWN, PROJ, KEY,
+    stage_hop, VALUE, CROSS, stage_hop, QUERY, stage_hop, stage_hop, VALUE, DOWN, PROJ, KEY,
     stage_rms, stage_end,
 ]
 

time: 417 us -> 412 us (0.988)
  waiting for transfers between devices: 159 us -> 130 us
  starting transfers between devices: 73.2 us -> 96.6 us
    ppermute x68, waiting for transfers between devices: 146 us -> 119 us  [exchange(): return lax.ppermute(values, 'dp', pairs)]
    ppermute x68, starting transfers between devices: 70.2 us -> 93.7 us  [exchange(): return lax.ppermute(values, 'dp', pairs)]
  transfers between devices with their start and end apart: 82 -> 82, of which waited for: 38 -> 36; matrix products, arithmetic and copies ran while one was open for 3% -> 3% of each run, Pallas kernels for 22% -> 23%
where the time goes in v5:
time: 412 us; the launch traced here: 404 us
  Pallas kernels  148 us (36%)
  waiting for transfers between devices  130 us (32%)
  starting transfers between devices  96.6 us (23%)
  local copies, waits for them, and re-layouts  16 us (4%)
  other arithmetic  10.1 us (2%)
    ppermute x68, waiting for transfers between devices, exchange(): return lax.ppermute(values, 'dp', pairs)  119 us
    pallas_call x15, Pallas kernels, call(): pl.pallas_call(body, grid=grid, in_specs=in_specs, out_specs=out_specs, o...  111 us
    ppermute x68, starting transfers between devices, exchange(): return lax.ppermute(values, 'dp', pairs)  93.7 us
    pallas_call x8, Pallas kernels, open_packet(): pl.pallas_call(body, grid=(steps,), in_specs=[SMEM_SPEC, whole(kept.shape...  24 us
    unnamed x142, local copies, waits for them, and re-layouts  13.2 us
    ppermute x14, waiting for transfers between devices, swap_cores(): return lax.ppermute(values, 'mp', SWAP)  11.1 us
  transfers between devices with their start and end apart: 82, of which 36 were waited for; matrix products, arithmetic and copies ran while one was open for 3% of the time, Pallas kernels for 23%

profile of v5, /device:TPU:0, one launch (start us, length us, event | category | flops | bytes accessed | tf_op | source)
XLA Modules:
  0.0 403.8 jit_solution(10208967336840526203)
XLA Ops:
  7.3 5.0 %shard_map.356 = (bf16[1024,1024]{1,0:T(8,128)(2,1)S(1)}, bf16[1024,512]{1,0:T(8,128)(2,1)S(1)}, bf16[1024,512]{1,0:T(8,128)(2,1)S(1)}, bf16[1024,512]{1,0:T(8,128)(2,1)S(1)}) custom-call(bf16[1024,1024]{1,0:T(8,128)(2,1)S(1)} %bitcast.36, bf16[1,1024]{1,0:T(2,128)(2,1)S(1)} %reshape.142.g, bf16[1,1024]{1,0:T(2,128)(2,1)S(1)} %reshape.143.b, ...), custom_call_target="tpu_custom_call" | custom-call | bytes 1024 | tf_op jit(solution)/shard_map/pallas_call | solution.py:54
  13.7 8.1 %shard_map.357 = (bf16[2,2,256,512]{3,2,1,0:T(8,128)(2,1)S(1)}, f32[2,8,512]{2,1,0:T(8,128)S(1)}, f32[2,256,1024]{2,1,0:T(8,128)S(1)}, bf16[2,256,1024]{2,1,0:T(8,128)(2,1)S(1)}) custom-call(s32[1]{0:T(128)} %bitcast.rank_ref, s32[2]{0:T(128)S(1)} %copy-done.56, bf16[2,512,512]{2,1,0:T(8,128)(2,1)S(1)} %bitcast.37, bf16[2,512,512]{2,1,0:T(8,128)(2,1)S(1)} %bitcast.39, ...), custom_call_target="tpu_custom_call" | custom-call | bytes 1024 | tf_op jit(solution)/shard_map/pallas_call | solution.py:54
  30.9 7.7 %shard_map.360 = (bf16[2,2,256,512]{3,2,1,0:T(8,128)(2,1)S(1)}, bf16[2,2,256,512]{3,2,1,0:T(8,128)(2,1)S(1)}, f32[2,8,512]{2,1,0:T(8,128)S(1)}, f32[2,256,1024]{2,1,0:T(8,128)S(1)}, bf16[2,256,1024]{2,1,0:T(8,128)(2,1)S(1)}) custom-call(s32[1]{0:T(128)} %bitcast.rank_ref, s32[2]{0:T(128)S(1)} %copy-done.65, ...), custom_call_target="tpu_custom_call" | custom-call | bytes 1024 | tf_op jit(solution)/shard_map/pallas_call | solution.py:54
  49.0 24.9 %shard_map.362 = (bf16[2,512,2048]{2,1,0:T(8,128)(2,1)}, bf16[2,512,2048]{2,1,0:T(8,128)(2,1)}, bf16[8,128,512]{2,1,0:T(8,128)(2,1)S(1)}, bf16[8,128,512]{2,1,0:...) custom-call(s32[1]{0:T(128)} %bitcast.5.me_ref.refs_0_, ...), custom_call_target="tpu_custom_call" | custom-call | bytes 1024 | tf_op jit(solution)/shard_map/pallas_call | solution.py:54
  76.1 5.0 %shard_map.363 = (f32[512,1024]{1,0:T(8,128)S(1)}, bf16[512,1024]{1,0:T(8,128)(2,1)S(1)}) custom-call(bf16[2,512,2048]{2,1,0:T(8,128)(2,1)S(1)} %copy-done.24, bf16[1024,2048]{1,0:T(8,128)(2,1)S(1)} %copy-done.4), custom_call_target="tpu_custom_call" | custom-call | bytes 1024 | tf_op jit(solution)/shard_map/pallas_call | solution.py:54
  91.7 18.1 %shard_map.365 = (bf16[2,2,256,512]{3,2,1,0:T(8,128)(2,1)S(1)}, bf16[2,2,128,512]{3,2,1,0:T(8,128)(2,1)S(1)}, bf16[2,2,128,512]{3,2,1,0:T(8,128)(2,1)S(1)}, f32[...) custom-call(s32[1]{0:T(128)} %bitcast.rank_ref, ...), custom_call_target="tpu_custom_call" | custom-call | bytes 1024 | tf_op jit(solution)/shard_map/pallas_call | solution.py:54
  109.9 9.2 %collective-permute-done.10 = bf16[8,192,512]{2,1,0:T(8,128)(2,1)S(1)} collective-permute-done((bf16[8,192,512]{2,1,0:T(8,128)(2,1)S(1)}, bf16[8,192,512]{2,1,0:T(8,128)(2,1)S(1)}, u32[]{:S(2)}, u32[]{:S(2)}) %collective-permute-start.10) | collective-permute-done | bytes 1572896 | tf_op jit(solution)/shard_map/ppermute | solution.py:822
  120.7 4.1 %shard_map.366 = (bf16[8,160,512]{2,1,0:T(8,128)(2,1)S(1)}, bf16[8,160,512]{2,1,0:T(8,128)(2,1)S(1)}) custom-call(s32[1]{0:T(128)} %bitcast.5.me_ref.refs_0_, bf16[2,512,512]{2,1,0:T(8,128)(2,1)S(1)} %bitcast.53, bf16[512,1024]{1,0:T(8,128)(2,1)S(1)} %bitcast.47, bf16[512,1024]{1,0:T(8,128)(2,1)S(1)} %bitcast.48, bf16[2,128,768]{2,1,0:T(8,128)(2,1)S(1)} %copy-done.43, ...), custom_call_target="tpu_custom_call" | custom-call | bytes 1024 | tf_op jit(solution)/shard_map/pallas_call | solution.py:54
  134.4 20.9 %shard_map.368 = (bf16[2,512,512]{2,1,0:T(8,128)(2,1)S(1)}, bf16[2,512,512]{2,1,0:T(8,128)(2,1)S(1)}, bf16[2,512,512]{2,1,0:T(8,128)(2,1)S(1)}, f32[2,256,1024]{2,1,0:T(8,128)S(1)}, bf16[2,256,1024]{2,1,0:T(8,128)(2,1)S(1)}) custom-call(s32[1]{0:T(128)} %bitcast.rank_ref, s32[2]{0:T(128)S(1)} %copy-done.56, ...), custom_call_target="tpu_custom_call" | custom-call | bytes 1024 | tf_op jit(solution)/shard_map/pallas_call | solution.py:54
  155.9 4.2 %collective-permute-done.16 = bf16[4,128,512]{2,1,0:T(8,128)(2,1)S(1)} collective-permute-done((bf16[4,128,512]{2,1,0:T(8,128)(2,1)S(1)}, bf16[4,128,512]{2,1,0:T(8,128)(2,1)S(1)}, u32[]{:S(2)}, u32[]{:S(2)}) %collective-permute-start.16) | collective-permute-done | bytes 524320 | tf_op jit(solution)/shard_map/ppermute | solution.py:822
  160.3 4.4 %shard_map.369 = (bf16[8,128,512]{2,1,0:T(8,128)(2,1)S(1)}, bf16[8,128,512]{2,1,0:T(8,128)(2,1)S(1)}) custom-call(s32[1]{0:T(128)} %bitcast.5.me_ref.refs_0_, bf16[2,512,512]{2,1,0:T(8,128)(2,1)S(1)} %bitcast.52, bf16[512,1024]{1,0:T(8,128)(2,1)S(1)} %bitcast.43, bf16[512,1024]{1,0:T(8,128)(2,1)S(1)} %bitcast.44, bf16[2,512,512]{2,1,0:T(8,128)(2,1)S(1)} %bitcast.51, ...), custom_call_target="tpu_custom_call" | custom-call | bytes 1024 | tf_op jit(solution)/shard_map/pallas_call | solution.py:54
  188.3 4.9 %shard_map.374 = (f32[512,1024]{1,0:T(8,128)S(1)}, bf16[512,1024]{1,0:T(8,128)(2,1)S(1)}) custom-call(bf16[2,512,2048]{2,1,0:T(8,128)(2,1)S(1)} %copy-done.23, bf16[2048,1024]{1,0:T(8,128)(2,1)S(1)} %copy-done.5), custom_call_target="tpu_custom_call" | custom-call | bytes 1024 | tf_op jit(solution)/shard_map/pallas_call | solution.py:54
  201.3 9.9 %collective-permute-done.20 = bf16[1,192,512]{2,1,0:T(8,128)(2,1)S(1)} collective-permute-done((bf16[1,192,512]{2,1,0:T(8,128)(2,1)S(1)}, bf16[1,192,512]{2,1,0:T(8,128)(2,1)S(1)}, u32[]{:S(2)}, u32[]{:S(2)}) %collective-permute-start.20) | collective-permute-done | bytes 196640 | tf_op jit(solution)/shard_map/ppermute | solution.py:822
  217.9 8.1 %collective-permute-done.27 = bf16[1,192,512]{2,1,0:T(8,128)(2,1)S(1)} collective-permute-done((bf16[1,192,512]{2,1,0:T(8,128)(2,1)S(1)}, bf16[1,192,512]{2,1,0:T(8,128)(2,1)S(1)}, u32[]{:S(2)}, u32[]{:S(2)}) %collective-permute-start.27) | collective-permute-done | bytes 196640 | tf_op jit(solution)/shard_map/ppermute | solution.py:822
  239.3 6.3 %collective-permute-done.35 = bf16[2,192,512]{2,1,0:T(8,128)(2,1)S(1)} collective-permute-done((bf16[2,192,512]{2,1,0:T(8,128)(2,1)S(1)}, bf16[2,192,512]{2,1,0:T(8,128)(2,1)S(1)}, u32[]{:S(2)}, u32[]{:S(2)}) %collective-permute-start.35) | collective-permute-done | bytes 393248 | tf_op jit(solution)/shard_map/ppermute | solution.py:822
  272.5 3.8 collective-permute-done.42
  285.4 8.6 %collective-permute-done.52 = bf16[1,64,512]{2,1,0:T(8,128)(2,1)S(1)} collective-permute-done((bf16[1,64,512]{2,1,0:T(8,128)(2,1)S(1)}, bf16[1,64,512]{2,1,0:T(8,128)(2,1)S(1)}, u32[]{:S(2)}, u32[]{:S(2)}) %collective-permute-start.52) | collective-permute-done | bytes 65568 | tf_op jit(solution)/shard_map/ppermute | solution.py:822
  297.2 7.3 %collective-permute-done.53 = bf16[1,64,512]{2,1,0:T(8,128)(2,1)S(1)} collective-permute-done((bf16[1,64,512]{2,1,0:T(8,128)(2,1)S(1)}, bf16[1,64,512]{2,1,0:T(8,128)(2,1)S(1)}, u32[]{:S(2)}, u32[]{:S(2)}) %collective-permute-start.53) | collective-permute-done | bytes 65568 | tf_op jit(solution)/shard_map/ppermute | solution.py:822
  310.6 5.0 %collective-permute-done.59 = bf16[2,64,512]{2,1,0:T(8,128)(2,1)S(1)} collective-permute-done((bf16[2,64,512]{2,1,0:T(8,128)(2,1)S(1)}, bf16[2,64,512]{2,1,0:T(8,128)(2,1)S(1)}, u32[]{:S(2)}, u32[]{:S(2)}) %collective-permute-start.59) | collective-permute-done | bytes 131104 | tf_op jit(solution)/shard_map/ppermute | solution.py:822
  348.5 8.2 %collective-permute-done.70 = bf16[4,128,512]{2,1,0:T(8,128)(2,1)S(1)} collective-permute-done((bf16[4,128,512]{2,1,0:T(8,128)(2,1)S(1)}, bf16[4,128,512]{2,1,0:T(8,128)(2,1)S(1)}, u32[]{:S(2)}, u32[]{:S(2)}) %collective-permute-start.70) | collective-permute-done | bytes 524320 | tf_op jit(solution)/shard_map/ppermute | solution.py:822
  361.6 4.4 %collective-permute-done.72 = f32[16,1024]{1,0:T(8,128)S(1)} collective-permute-done((f32[16,1024]{1,0:T(8,128)S(1)}, f32[16,1024]{1,0:T(8,128)S(1)}, u32[]{:S(2)}, u32[]{:S(2)}) %collective-permute-start.72) | collective-permute-done | bytes 65568 | tf_op jit(solution)/shard_map/ppermute | solution.py:822
  367.0 4.0 shard_map.378
  377.1 9.5 %collective-permute-done.76 = f32[16,1024]{1,0:T(8,128)S(1)} collective-permute-done((f32[16,1024]{1,0:T(8,128)S(1)}, f32[16,1024]{1,0:T(8,128)S(1)}, u32[]{:S(2)}, u32[]{:S(2)}) %collective-permute-start.76) | collective-permute-done | bytes 65568 | tf_op jit(solution)/shard_map/ppermute | solution.py:822
  393.8 3.7 shard_map.381
  (387 shorter events, 204.8 us)
Async XLA Ops:
  81.6 37.5 %collective-permute-start.10 = (bf16[8,192,512]{2,1,0:T(8,128)(2,1)S(1)}, bf16[8,192,512]{2,1,0:T(8,128)(2,1)S(1)}, u32[]{:S(2)}, u32[]{:S(2)}) collective-permute-start(bf16[8,192,512]{2,1,0:T(8,128)(2,1)S(1)} %get-tuple-element.567), channel_id=1, source_target_pairs={{0,4},{2,6},{4,0},{6,2},{8,12},{10,14},{12,8},{14,10},{16,20},{18,... | collective-permute-start | bytes 4718600 | tf_op jit(solution)/shard_map/ppermute | solution.py:822
  87.5 37.7 %collective-permute-start.6 = (bf16[8,192,512]{2,1,0:T(8,128)(2,1)S(1)}, bf16[8,192,512]{2,1,0:T(8,128)(2,1)S(1)}, u32[]{:S(2)}, u32[]{:S(2)}) collective-permute-start(bf16[8,192,512]{2,1,0:T(8,128)(2,1)S(1)} %get-tuple-element.548), channel_id=1, source_target_pairs={{0,2},{2,0},{4,6},{6,4},{8,10},{10,8},{12,14},{14,12},{16,18},{18,... | collective-permute-start | bytes 4718600 | tf_op jit(solution)/shard_map/ppermute | solution.py:822
  90.0 34.8 %collective-permute-start.7 = (bf16[8,128,512]{2,1,0:T(8,128)(2,1)S(1)}, bf16[8,128,512]{2,1,0:T(8,128)(2,1)S(1)}, u32[]{:S(2)}, u32[]{:S(2)}) collective-permute-start(bf16[8,128,512]{2,1,0:T(8,128)(2,1)S(1)} %get-tuple-element.552), channel_id=1, source_target_pairs={{0,8},{2,10},{4,12},{6,14},{8,0},{10,2},{12,4},{14,6},{16,24},{18,... | collective-permute-start | bytes 3145736 | tf_op jit(solution)/shard_map/ppermute | solution.py:822
  128.9 26.4 %collective-permute-start.13 = (bf16[4,192,512]{2,1,0:T(8,128)(2,1)S(1)}, bf16[4,192,512]{2,1,0:T(8,128)(2,1)S(1)}, u32[]{:S(2)}, u32[]{:S(2)}) collective-permute-start(bf16[4,192,512]{2,1,0:T(8,128)(2,1)S(1)} %get-tuple-element.597), channel_id=1, source_target_pairs={{0,2},{2,0},{4,6},{6,4},{8,10},{10,8},{12,14},{14,12},{16,18},{18,... | collective-permute-start | bytes 2359304 | tf_op jit(solution)/shard_map/ppermute | solution.py:822
  130.7 37.4 %collective-permute-start.15 = (bf16[8,160,512]{2,1,0:T(8,128)(2,1)S(1)}, bf16[8,160,512]{2,1,0:T(8,128)(2,1)S(1)}, u32[]{:S(2)}, u32[]{:S(2)}) collective-permute-start(bf16[8,160,512]{2,1,0:T(8,128)(2,1)S(1)} %get-tuple-element.617), channel_id=1, source_target_pairs={{0,8},{2,10},{4,12},{6,14},{8,0},{10,2},{12,4},{14,6},{16,24},{18,... | collective-permute-start | bytes 3932168 | tf_op jit(solution)/shard_map/ppermute | solution.py:822
  132.3 23.3 %collective-permute-start.12 = (bf16[4,192,512]{2,1,0:T(8,128)(2,1)S(1)}, bf16[4,192,512]{2,1,0:T(8,128)(2,1)S(1)}, u32[]{:S(2)}, u32[]{:S(2)}) collective-permute-start(bf16[4,192,512]{2,1,0:T(8,128)(2,1)S(1)} %get-tuple-element.596), channel_id=1, source_target_pairs={{0,4},{2,6},{4,0},{6,2},{8,12},{10,14},{12,8},{14,10},{16,20},{18,... | collective-permute-start | bytes 2359304 | tf_op jit(solution)/shard_map/ppermute | solution.py:822
  133.8 26.3 %collective-permute-start.16 = (bf16[4,128,512]{2,1,0:T(8,128)(2,1)S(1)}, bf16[4,128,512]{2,1,0:T(8,128)(2,1)S(1)}, u32[]{:S(2)}, u32[]{:S(2)}) collective-permute-start(bf16[4,128,512]{2,1,0:T(8,128)(2,1)S(1)} %get-tuple-element.620), channel_id=1, source_target_pairs={{0,2},{2,0},{4,6},{6,4},{8,10},{10,8},{12,14},{14,12},{16,18},{18,... | collective-permute-start | bytes 1572872 | tf_op jit(solution)/shard_map/ppermute | solution.py:822
  155.6 24.5 %collective-permute-start.19 = (bf16[2,256,1024]{2,1,0:T(8,128)(2,1)S(1)}, bf16[2,256,1024]{2,1,0:T(8,128)(2,1)S(1)}, u32[]{:S(2)}, u32[]{:S(2)}) collective-permute-start(bf16[2,256,1024]{2,1,0:T(8,128)(2,1)S(1)} %get-tuple-element.669), channel_id=1, source_target_pairs={{0,1},{1,0},{2,3},{3,2},{4,5},{5,4},{6,7},{7,6},{8,9},{9,8},{10,11... | collective-permute-start | bytes 3145736 | tf_op jit(solution)/shard_map/ppermute | solution.py:833
  170.3 27.6 %collective-permute-start.23 = (bf16[8,128,512]{2,1,0:T(8,128)(2,1)S(1)}, bf16[8,128,512]{2,1,0:T(8,128)(2,1)S(1)}, u32[]{:S(2)}, u32[]{:S(2)}) collective-permute-start(bf16[8,128,512]{2,1,0:T(8,128)(2,1)S(1)} %get-tuple-element.693), channel_id=1, source_target_pairs={{0,4},{2,6},{4,0},{6,2},{8,12},{10,14},{12,8},{14,10},{16,20},{18,... | collective-permute-start | bytes 3145736 | tf_op jit(solution)/shard_map/ppermute | solution.py:822
  178.3 20.5 %collective-permute-start.21 = (bf16[8,64,512]{2,1,0:T(8,128)(2,1)S(1)}, bf16[8,64,512]{2,1,0:T(8,128)(2,1)S(1)}, u32[]{:S(2)}, u32[]{:S(2)}) collective-permute-start(bf16[8,64,512]{2,1,0:T(8,128)(2,1)S(1)} %get-tuple-element.685), channel_id=1, source_target_pairs={{0,2},{2,0},{4,6},{6,4},{8,10},{10,8},{12,14},{14,12},{16,18},{18,... | collective-permute-start | bytes 1572872 | tf_op jit(solution)/shard_map/ppermute | solution.py:822
  180.1 33.6 %collective-permute-start.28 = (bf16[4,160,512]{2,1,0:T(8,128)(2,1)S(1)}, bf16[4,160,512]{2,1,0:T(8,128)(2,1)S(1)}, u32[]{:S(2)}, u32[]{:S(2)}) collective-permute-start(bf16[4,160,512]{2,1,0:T(8,128)(2,1)S(1)} %get-tuple-element.720), channel_id=1, source_target_pairs={{0,4},{2,6},{4,0},{6,2},{8,12},{10,14},{12,8},{14,10},{16,20},{18,... | collective-permute-start | bytes 1966088 | tf_op jit(solution)/shard_map/ppermute | solution.py:822
  196.3 20.5 %collective-permute-start.29 = (bf16[2,128,512]{2,1,0:T(8,128)(2,1)S(1)}, bf16[2,128,512]{2,1,0:T(8,128)(2,1)S(1)}, u32[]{:S(2)}, u32[]{:S(2)}) collective-permute-start(bf16[2,128,512]{2,1,0:T(8,128)(2,1)S(1)} %get-tuple-element.725), channel_id=1, source_target_pairs={{0,4},{2,6},{4,0},{6,2},{8,12},{10,14},{12,8},{14,10},{16,20},{18,... | collective-permute-start | bytes 786440 | tf_op jit(solution)/shard_map/ppermute | solution.py:822
  197.9 29.4 %collective-permute-start.26 = (bf16[8,64,512]{2,1,0:T(8,128)(2,1)S(1)}, bf16[8,64,512]{2,1,0:T(8,128)(2,1)S(1)}, u32[]{:S(2)}, u32[]{:S(2)}) collective-permute-start(bf16[8,64,512]{2,1,0:T(8,128)(2,1)S(1)} %get-tuple-element.718), channel_id=1, source_target_pairs={{0,4},{2,6},{4,0},{6,2},{8,12},{10,14},{12,8},{14,10},{16,20},{18,... | collective-permute-start | bytes 1572872 | tf_op jit(solution)/shard_map/ppermute | solution.py:822
  216.8 31.0 %collective-permute-start.34 = (bf16[4,64,512]{2,1,0:T(8,128)(2,1)S(1)}, bf16[4,64,512]{2,1,0:T(8,128)(2,1)S(1)}, u32[]{:S(2)}, u32[]{:S(2)}) collective-permute-start(bf16[4,64,512]{2,1,0:T(8,128)(2,1)S(1)} %get-tuple-element.749), channel_id=1, source_target_pairs={{0,4},{2,6},{4,0},{6,2},{8,12},{10,14},{12,8},{14,10},{16,20},{18,... | collective-permute-start | bytes 786440 | tf_op jit(solution)/shard_map/ppermute | solution.py:822
  257.3 21.9 %collective-permute-start.47 = (bf16[4,192,512]{2,1,0:T(8,128)(2,1)S(1)}, bf16[4,192,512]{2,1,0:T(8,128)(2,1)S(1)}, u32[]{:S(2)}, u32[]{:S(2)}) collective-permute-start(bf16[4,192,512]{2,1,0:T(8,128)(2,1)S(1)} %pad_maximum_fusion.6), channel_id=1, source_target_pairs={{0,4},{2,6},{4,0},{6,2},{8,12},{10,14},{12,8},{14,10},{16,20},{18,... | collective-permute-start | bytes 2359304 | tf_op jit(solution)/shard_map/ppermute | solution.py:822
  276.3 39.3 %collective-permute-start.58 = (bf16[8,192,512]{2,1,0:T(8,128)(2,1)S(1)}, bf16[8,192,512]{2,1,0:T(8,128)(2,1)S(1)}, u32[]{:S(2)}, u32[]{:S(2)}) collective-permute-start(bf16[8,192,512]{2,1,0:T(8,128)(2,1)S(1)} %pad_maximum_fusion.refs_1_), channel_id=1, source_target_pairs={{0,4},{2,6},{4,0},{6,2},{8,12},{10,14},{12,8},{14,10},{16,20},{18,... | collective-permute-start | bytes 4718600 | tf_op jit(solution)/shard_map/ppermute | solution.py:822
  284.3 43.9 %collective-permute-start.61 = (bf16[8,192,512]{2,1,0:T(8,128)(2,1)S(1)}, bf16[8,192,512]{2,1,0:T(8,128)(2,1)S(1)}, u32[]{:S(2)}, u32[]{:S(2)}) collective-permute-start(bf16[8,192,512]{2,1,0:T(8,128)(2,1)S(1)} %pad_maximum_fusion.1.refs_1_), channel_id=1, source_target_pairs={{0,2},{2,0},{4,6},{6,4},{8,10},{10,8},{12,14},{14,12},{16,18},{18,... | collective-permute-start | bytes 4718600 | tf_op jit(solution)/shard_map/ppermute | solution.py:822
  315.6 32.0 %collective-permute-start.69 = (bf16[2,128,768]{2,1,0:T(8,128)(2,1)S(1)}, bf16[2,128,768]{2,1,0:T(8,128)(2,1)S(1)}, u32[]{:S(2)}, u32[]{:S(2)}) collective-permute-start(bf16[2,128,768]{2,1,0:T(8,128)(2,1)S(1)} %get-tuple-element.921), channel_id=1, source_target_pairs={{0,1},{1,0},{2,3},{3,2},{4,5},{5,4},{6,7},{7,6},{8,9},{9,8},{10,11... | collective-permute-start | bytes 1179656 | tf_op jit(solution)/shard_map/ppermute | solution.py:833
  334.5 32.4 %collective-permute-start.73 = (bf16[8,160,512]{2,1,0:T(8,128)(2,1)S(1)}, bf16[8,160,512]{2,1,0:T(8,128)(2,1)}, u32[]{:S(2)}, u32[]{:S(2)}) collective-permute-start(bf16[8,160,512]{2,1,0:T(8,128)(2,1)S(1)} %pad_maximum_fusion.2.refs_1_), channel_id=1, source_target_pairs={{0,8},{2,10},{4,12},{6,14},{8,0},{10,2},{12,4},{14,6},{16,24},{18,... | collective-permute-start | bytes 3932168 | tf_op jit(solution)/shard_map/ppermute | solution.py:822
  344.3 28.5 %collective-permute-start.75 = (bf16[8,64,512]{2,1,0:T(8,128)(2,1)}, bf16[8,64,512]{2,1,0:T(8,128)(2,1)}, u32[]{:S(2)}, u32[]{:S(2)}) collective-permute-start(bf16[8,64,512]{2,1,0:T(8,128)(2,1)} %pad_maximum_fusion.10.refs_1_), channel_id=1, source_target_pairs={{0,2},{2,0},{4,6},{6,4},{8,10},{10,8},{12,14},{14,12},{16,18},{18,... | collective-permute-start | bytes 1572872 | tf_op jit(solution)/shard_map/ppermute | solution.py:822
  345.0 52.5 %collective-permute-start.79 = (bf16[8,128,512]{2,1,0:T(8,128)(2,1)S(1)}, bf16[8,128,512]{2,1,0:T(8,128)(2,1)}, u32[]{:S(2)}, u32[]{:S(2)}) collective-permute-start(bf16[8,128,512]{2,1,0:T(8,128)(2,1)S(1)} %pad_maximum_fusion.3.refs_1_), channel_id=1, source_target_pairs={{0,4},{2,6},{4,0},{6,2},{8,12},{10,14},{12,8},{14,10},{16,20},{18,... | collective-permute-start | bytes 3145736 | tf_op jit(solution)/shard_map/ppermute | solution.py:822
  356.9 36.9 %collective-permute-start.80 = (bf16[8,128,512]{2,1,0:T(8,128)(2,1)S(1)}, bf16[8,128,512]{2,1,0:T(8,128)(2,1)}, u32[]{:S(2)}, u32[]{:S(2)}) collective-permute-start(bf16[8,128,512]{2,1,0:T(8,128)(2,1)S(1)} %pad_maximum_fusion.4.refs_1_), channel_id=1, source_target_pairs={{0,8},{2,10},{4,12},{6,14},{8,0},{10,2},{12,4},{14,6},{16,24},{18,... | collective-permute-start | bytes 3145736 | tf_op jit(solution)/shard_map/ppermute | solution.py:822
  366.0 22.7 %collective-permute-start.81 = (bf16[8,64,512]{2,1,0:T(8,128)(2,1)}, bf16[8,64,512]{2,1,0:T(8,128)(2,1)S(1)}, u32[]{:S(2)}, u32[]{:S(2)}) collective-permute-start(bf16[8,64,512]{2,1,0:T(8,128)(2,1)} %pad_maximum_fusion.12.refs_1_), channel_id=1, source_target_pairs={{0,2},{2,0},{4,6},{6,4},{8,10},{10,8},{12,14},{14,12},{16,18},{18,... | collective-permute-start | bytes 1572872 | tf_op jit(solution)/shard_map/ppermute | solution.py:822
  372.8 28.3 %collective-permute-start.78 = (bf16[8,64,512]{2,1,0:T(8,128)(2,1)S(1)}, bf16[8,64,512]{2,1,0:T(8,128)(2,1)S(1)}, u32[]{:S(2)}, u32[]{:S(2)}) collective-permute-start(bf16[8,64,512]{2,1,0:T(8,128)(2,1)S(1)} %copy-done.37), channel_id=1, source_target_pairs={{0,4},{2,6},{4,0},{6,2},{8,12},{10,14},{12,8},{14,10},{16,20},{18,... | collective-permute-start | bytes 1572872 | tf_op jit(solution)/shard_map/ppermute | solution.py:822
  (129 other events, 1110.9 us)

commit v6 on v5

--- a/solution.py
+++ b/solution.py
@@ -163,9 +163,8 @@
     return jnp.where(head_mask(values.shape[0], head), values, jnp.zeros_like(values))
 
 
-def scores_t(query_pair, key_pair, head, allowed):
-    scores = dot_rt(key_pair, only(query_pair, head)) * score_scale
-    return jnp.where(allowed, scores, masked_fill)
+def scores_t(query_pair, key_pair, head, masked):
+    return dot_rt(key_pair, only(query_pair, head) * jnp.asarray(score_scale, BF16)) + masked
 
 
 def attend_pair(query_pair, key_pair, value_pair, allowed, lse_ref, lse_at):
@@ -175,7 +174,7 @@
         highest = jnp.max(scores, 0, keepdims=True)
         powers = jnp.exp(scores - highest)
         total = jnp.sum(powers, 0, keepdims=True)
-        probs = (powers / total).astype(BF16)
+        probs = (powers * (1.0 / total)).astype(BF16)
         mixed.append(dot_lt(probs, value_pair))
         row, columns = lse_at(head)
         lse_ref[0, row : row + 1, columns] = highest + jnp.log(total)
@@ -202,13 +201,13 @@
 def causal_mask(keys, queries, first_query, count):
     key_at = lax.broadcasted_iota(jnp.int32, (keys, queries), 0)
     query_at = first_query + lax.broadcasted_iota(jnp.int32, (keys, queries), 1)
-    return (key_at <= query_at) & (key_at < count)
+    return jnp.where((key_at <= query_at) & (key_at < count), 0.0, masked_fill)
 
 
 def text_mask(text_half, queries, rank, count):
     key_at = lax.broadcasted_iota(jnp.int32, (2 * text_half, queries), 0)
     swapped = jnp.where(key_at < text_half, key_at + text_half, key_at - text_half)
-    return jnp.where(rank == 0, key_at, swapped) < count
+    return jnp.where(jnp.where(rank == 0, key_at, swapped) < count, 0.0, masked_fill)
 
 
 def self_forward(rank, valid, query, key, value, w_out):

time: 412 us -> 413 us (level)
  starting transfers between devices: 96.6 us -> 102 us
  waiting for transfers between devices: 130 us -> 125 us
    ppermute x68, starting transfers between devices: 93.7 us -> 99.4 us  [exchange(): return lax.ppermute(values, 'dp', pairs)]
    ppermute x68, waiting for transfers between devices: 119 us -> 114 us  [exchange(): return lax.ppermute(values, 'dp', pairs)]
where the time goes in v6:
time: 413 us; the launch traced here: 405 us
  Pallas kernels  148 us (36%)
  waiting for transfers between devices  125 us (30%)
  starting transfers between devices  102 us (25%)
  local copies, waits for them, and re-layouts  16 us (4%)
  other arithmetic  10.1 us (2%)
    ppermute x68, waiting for transfers between devices, exchange(): return lax.ppermute(values, 'dp', pairs)  114 us
    pallas_call x15, Pallas kernels, call(): pl.pallas_call(body, grid=grid, in_specs=in_specs, out_specs=out_specs, o...  111 us
    ppermute x68, starting transfers between devices, exchange(): return lax.ppermute(values, 'dp', pairs)  99.4 us
    pallas_call x8, Pallas kernels, open_packet(): pl.pallas_call(body, grid=(steps,), in_specs=[SMEM_SPEC, whole(kept.shape...  24.1 us
    unnamed x142, local copies, waits for them, and re-layouts  13.2 us
    ppermute x14, waiting for transfers between devices, swap_cores(): return lax.ppermute(values, 'mp', SWAP)  11.1 us
  transfers between devices with their start and end apart: 82, of which 36 were waited for; matrix products, arithmetic and copies ran while one was open for 3% of the time, Pallas kernels for 23%

profile of v6, /device:TPU:0, one launch (start us, length us, event | category | flops | bytes accessed | tf_op | source)
XLA Modules:
  0.0 405.2 jit_solution(10770814322530614781)
XLA Ops:
  7.3 5.0 %shard_map.356 = (bf16[1024,1024]{1,0:T(8,128)(2,1)S(1)}, bf16[1024,512]{1,0:T(8,128)(2,1)S(1)}, bf16[1024,512]{1,0:T(8,128)(2,1)S(1)}, bf16[1024,512]{1,0:T(8,128)(2,1)S(1)}) custom-call(bf16[1024,1024]{1,0:T(8,128)(2,1)S(1)} %bitcast.36, bf16[1,1024]{1,0:T(2,128)(2,1)S(1)} %reshape.142.g, bf16[1,1024]{1,0:T(2,128)(2,1)S(1)} %reshape.143.b, ...), custom_call_target="tpu_custom_call" | custom-call | bytes 1024 | tf_op jit(solution)/shard_map/pallas_call | solution.py:54
  13.7 8.6 %shard_map.357 = (bf16[2,2,256,512]{3,2,1,0:T(8,128)(2,1)S(1)}, f32[2,8,512]{2,1,0:T(8,128)S(1)}, f32[2,256,1024]{2,1,0:T(8,128)S(1)}, bf16[2,256,1024]{2,1,0:T(8,128)(2,1)S(1)}) custom-call(s32[1]{0:T(128)} %bitcast.rank_ref, s32[2]{0:T(128)S(1)} %copy-done.56, bf16[2,512,512]{2,1,0:T(8,128)(2,1)S(1)} %bitcast.37, bf16[2,512,512]{2,1,0:T(8,128)(2,1)S(1)} %bitcast.39, ...), custom_call_target="tpu_custom_call" | custom-call | bytes 1024 | tf_op jit(solution)/shard_map/pallas_call | solution.py:54
  31.5 7.5 %shard_map.360 = (bf16[2,2,256,512]{3,2,1,0:T(8,128)(2,1)S(1)}, bf16[2,2,256,512]{3,2,1,0:T(8,128)(2,1)S(1)}, f32[2,8,512]{2,1,0:T(8,128)S(1)}, f32[2,256,1024]{2,1,0:T(8,128)S(1)}, bf16[2,256,1024]{2,1,0:T(8,128)(2,1)S(1)}) custom-call(s32[1]{0:T(128)} %bitcast.rank_ref, s32[2]{0:T(128)S(1)} %copy-done.65, ...), custom_call_target="tpu_custom_call" | custom-call | bytes 1024 | tf_op jit(solution)/shard_map/pallas_call | solution.py:54
  49.2 24.9 %shard_map.362 = (bf16[2,512,2048]{2,1,0:T(8,128)(2,1)}, bf16[2,512,2048]{2,1,0:T(8,128)(2,1)}, bf16[8,128,512]{2,1,0:T(8,128)(2,1)S(1)}, bf16[8,128,512]{2,1,0:...) custom-call(s32[1]{0:T(128)} %bitcast.5.me_ref.refs_0_, ...), custom_call_target="tpu_custom_call" | custom-call | bytes 1024 | tf_op jit(solution)/shard_map/pallas_call | solution.py:54
  76.4 5.0 %shard_map.363 = (f32[512,1024]{1,0:T(8,128)S(1)}, bf16[512,1024]{1,0:T(8,128)(2,1)S(1)}) custom-call(bf16[2,512,2048]{2,1,0:T(8,128)(2,1)S(1)} %copy-done.24, bf16[1024,2048]{1,0:T(8,128)(2,1)S(1)} %copy-done.4), custom_call_target="tpu_custom_call" | custom-call | bytes 1024 | tf_op jit(solution)/shard_map/pallas_call | solution.py:54
  92.1 18.1 %shard_map.365 = (bf16[2,2,256,512]{3,2,1,0:T(8,128)(2,1)S(1)}, bf16[2,2,128,512]{3,2,1,0:T(8,128)(2,1)S(1)}, bf16[2,2,128,512]{3,2,1,0:T(8,128)(2,1)S(1)}, f32[...) custom-call(s32[1]{0:T(128)} %bitcast.rank_ref, ...), custom_call_target="tpu_custom_call" | custom-call | bytes 1024 | tf_op jit(solution)/shard_map/pallas_call | solution.py:54
  110.3 9.2 %collective-permute-done.10 = bf16[8,192,512]{2,1,0:T(8,128)(2,1)S(1)} collective-permute-done((bf16[8,192,512]{2,1,0:T(8,128)(2,1)S(1)}, bf16[8,192,512]{2,1,0:T(8,128)(2,1)S(1)}, u32[]{:S(2)}, u32[]{:S(2)}) %collective-permute-start.10) | collective-permute-done | bytes 1572896 | tf_op jit(solution)/shard_map/ppermute | solution.py:821
  121.1 4.1 %shard_map.366 = (bf16[8,160,512]{2,1,0:T(8,128)(2,1)S(1)}, bf16[8,160,512]{2,1,0:T(8,128)(2,1)S(1)}) custom-call(s32[1]{0:T(128)} %bitcast.5.me_ref.refs_0_, bf16[2,512,512]{2,1,0:T(8,128)(2,1)S(1)} %bitcast.53, bf16[512,1024]{1,0:T(8,128)(2,1)S(1)} %bitcast.47, bf16[512,1024]{1,0:T(8,128)(2,1)S(1)} %bitcast.48, bf16[2,128,768]{2,1,0:T(8,128)(2,1)S(1)} %copy-done.43, ...), custom_call_target="tpu_custom_call" | custom-call | bytes 1024 | tf_op jit(solution)/shard_map/pallas_call | solution.py:54
  134.8 21.0 %shard_map.368 = (bf16[2,512,512]{2,1,0:T(8,128)(2,1)S(1)}, bf16[2,512,512]{2,1,0:T(8,128)(2,1)S(1)}, bf16[2,512,512]{2,1,0:T(8,128)(2,1)S(1)}, f32[2,256,1024]{2,1,0:T(8,128)S(1)}, bf16[2,256,1024]{2,1,0:T(8,128)(2,1)S(1)}) custom-call(s32[1]{0:T(128)} %bitcast.rank_ref, s32[2]{0:T(128)S(1)} %copy-done.56, ...), custom_call_target="tpu_custom_call" | custom-call | bytes 1024 | tf_op jit(solution)/shard_map/pallas_call | solution.py:54
  156.4 4.2 %collective-permute-done.16 = bf16[4,128,512]{2,1,0:T(8,128)(2,1)S(1)} collective-permute-done((bf16[4,128,512]{2,1,0:T(8,128)(2,1)S(1)}, bf16[4,128,512]{2,1,0:T(8,128)(2,1)S(1)}, u32[]{:S(2)}, u32[]{:S(2)}) %collective-permute-start.16) | collective-permute-done | bytes 524320 | tf_op jit(solution)/shard_map/ppermute | solution.py:821
  160.7 4.4 %shard_map.369 = (bf16[8,128,512]{2,1,0:T(8,128)(2,1)S(1)}, bf16[8,128,512]{2,1,0:T(8,128)(2,1)S(1)}) custom-call(s32[1]{0:T(128)} %bitcast.5.me_ref.refs_0_, bf16[2,512,512]{2,1,0:T(8,128)(2,1)S(1)} %bitcast.52, bf16[512,1024]{1,0:T(8,128)(2,1)S(1)} %bitcast.43, bf16[512,1024]{1,0:T(8,128)(2,1)S(1)} %bitcast.44, bf16[2,512,512]{2,1,0:T(8,128)(2,1)S(1)} %bitcast.51, ...), custom_call_target="tpu_custom_call" | custom-call | bytes 1024 | tf_op jit(solution)/shard_map/pallas_call | solution.py:54
  188.7 4.9 %shard_map.374 = (f32[512,1024]{1,0:T(8,128)S(1)}, bf16[512,1024]{1,0:T(8,128)(2,1)S(1)}) custom-call(bf16[2,512,2048]{2,1,0:T(8,128)(2,1)S(1)} %copy-done.23, bf16[2048,1024]{1,0:T(8,128)(2,1)S(1)} %copy-done.5), custom_call_target="tpu_custom_call" | custom-call | bytes 1024 | tf_op jit(solution)/shard_map/pallas_call | solution.py:54
  201.7 9.9 %collective-permute-done.20 = bf16[1,192,512]{2,1,0:T(8,128)(2,1)S(1)} collective-permute-done((bf16[1,192,512]{2,1,0:T(8,128)(2,1)S(1)}, bf16[1,192,512]{2,1,0:T(8,128)(2,1)S(1)}, u32[]{:S(2)}, u32[]{:S(2)}) %collective-permute-start.20) | collective-permute-done | bytes 196640 | tf_op jit(solution)/shard_map/ppermute | solution.py:821
  218.3 8.1 %collective-permute-done.27 = bf16[1,192,512]{2,1,0:T(8,128)(2,1)S(1)} collective-permute-done((bf16[1,192,512]{2,1,0:T(8,128)(2,1)S(1)}, bf16[1,192,512]{2,1,0:T(8,128)(2,1)S(1)}, u32[]{:S(2)}, u32[]{:S(2)}) %collective-permute-start.27) | collective-permute-done | bytes 196640 | tf_op jit(solution)/shard_map/ppermute | solution.py:821
  239.7 6.3 %collective-permute-done.35 = bf16[2,192,512]{2,1,0:T(8,128)(2,1)S(1)} collective-permute-done((bf16[2,192,512]{2,1,0:T(8,128)(2,1)S(1)}, bf16[2,192,512]{2,1,0:T(8,128)(2,1)S(1)}, u32[]{:S(2)}, u32[]{:S(2)}) %collective-permute-start.35) | collective-permute-done | bytes 393248 | tf_op jit(solution)/shard_map/ppermute | solution.py:821
  273.0 3.8 collective-permute-done.42
  285.8 5.8 %collective-permute-done.52 = bf16[1,64,512]{2,1,0:T(8,128)(2,1)S(1)} collective-permute-done((bf16[1,64,512]{2,1,0:T(8,128)(2,1)S(1)}, bf16[1,64,512]{2,1,0:T(8,128)(2,1)S(1)}, u32[]{:S(2)}, u32[]{:S(2)}) %collective-permute-start.52) | collective-permute-done | bytes 65568 | tf_op jit(solution)/shard_map/ppermute | solution.py:821
  296.6 6.5 %collective-permute-done.53 = bf16[1,64,512]{2,1,0:T(8,128)(2,1)S(1)} collective-permute-done((bf16[1,64,512]{2,1,0:T(8,128)(2,1)S(1)}, bf16[1,64,512]{2,1,0:T(8,128)(2,1)S(1)}, u32[]{:S(2)}, u32[]{:S(2)}) %collective-permute-start.53) | collective-permute-done | bytes 65568 | tf_op jit(solution)/shard_map/ppermute | solution.py:821
  306.7 4.3 %collective-permute-start.62 = (bf16[4,160,512]{2,1,0:T(8,128)(2,1)S(1)}, bf16[4,160,512]{2,1,0:T(8,128)(2,1)S(1)}, u32[]{:S(2)}, u32[]{:S(2)}) collective-permute-start(bf16[4,160,512]{2,1,0:T(8,128)(2,1)S(1)} %pad_maximum_fusion.7), channel_id=1, source_target_pairs={{0,4},{2,6},{4,0},{6,2},{8,12},{10,14},{12,8},{14,10},{16,20},{18,... | collective-permute-start | bytes 1966088 | tf_op jit(solution)/shard_map/ppermute | solution.py:821
  349.0 7.8 %collective-permute-done.70 = bf16[4,128,512]{2,1,0:T(8,128)(2,1)S(1)} collective-permute-done((bf16[4,128,512]{2,1,0:T(8,128)(2,1)S(1)}, bf16[4,128,512]{2,1,0:T(8,128)(2,1)S(1)}, u32[]{:S(2)}, u32[]{:S(2)}) %collective-permute-start.70) | collective-permute-done | bytes 524320 | tf_op jit(solution)/shard_map/ppermute | solution.py:821
  362.0 3.9 collective-permute-done.72
  367.3 4.0 shard_map.378
  377.4 9.8 %collective-permute-done.76 = f32[16,1024]{1,0:T(8,128)S(1)} collective-permute-done((f32[16,1024]{1,0:T(8,128)S(1)}, f32[16,1024]{1,0:T(8,128)S(1)}, u32[]{:S(2)}, u32[]{:S(2)}) %collective-permute-start.76) | collective-permute-done | bytes 65568 | tf_op jit(solution)/shard_map/ppermute | solution.py:821
  395.1 3.7 shard_map.381
  (387 shorter events, 210.8 us)
Async XLA Ops:
  81.8 37.7 %collective-permute-start.10 = (bf16[8,192,512]{2,1,0:T(8,128)(2,1)S(1)}, bf16[8,192,512]{2,1,0:T(8,128)(2,1)S(1)}, u32[]{:S(2)}, u32[]{:S(2)}) collective-permute-start(bf16[8,192,512]{2,1,0:T(8,128)(2,1)S(1)} %get-tuple-element.567), channel_id=1, source_target_pairs={{0,4},{2,6},{4,0},{6,2},{8,12},{10,14},{12,8},{14,10},{16,20},{18,... | collective-permute-start | bytes 4718600 | tf_op jit(solution)/shard_map/ppermute | solution.py:821
  87.9 37.7 %collective-permute-start.6 = (bf16[8,192,512]{2,1,0:T(8,128)(2,1)S(1)}, bf16[8,192,512]{2,1,0:T(8,128)(2,1)S(1)}, u32[]{:S(2)}, u32[]{:S(2)}) collective-permute-start(bf16[8,192,512]{2,1,0:T(8,128)(2,1)S(1)} %get-tuple-element.548), channel_id=1, source_target_pairs={{0,2},{2,0},{4,6},{6,4},{8,10},{10,8},{12,14},{14,12},{16,18},{18,... | collective-permute-start | bytes 4718600 | tf_op jit(solution)/shard_map/ppermute | solution.py:821
  90.4 34.8 %collective-permute-start.7 = (bf16[8,128,512]{2,1,0:T(8,128)(2,1)S(1)}, bf16[8,128,512]{2,1,0:T(8,128)(2,1)S(1)}, u32[]{:S(2)}, u32[]{:S(2)}) collective-permute-start(bf16[8,128,512]{2,1,0:T(8,128)(2,1)S(1)} %get-tuple-element.552), channel_id=1, source_target_pairs={{0,8},{2,10},{4,12},{6,14},{8,0},{10,2},{12,4},{14,6},{16,24},{18,... | collective-permute-start | bytes 3145736 | tf_op jit(solution)/shard_map/ppermute | solution.py:821
  129.3 26.5 %collective-permute-start.13 = (bf16[4,192,512]{2,1,0:T(8,128)(2,1)S(1)}, bf16[4,192,512]{2,1,0:T(8,128)(2,1)S(1)}, u32[]{:S(2)}, u32[]{:S(2)}) collective-permute-start(bf16[4,192,512]{2,1,0:T(8,128)(2,1)S(1)} %get-tuple-element.597), channel_id=1, source_target_pairs={{0,2},{2,0},{4,6},{6,4},{8,10},{10,8},{12,14},{14,12},{16,18},{18,... | collective-permute-start | bytes 2359304 | tf_op jit(solution)/shard_map/ppermute | solution.py:821
  131.1 37.4 %collective-permute-start.15 = (bf16[8,160,512]{2,1,0:T(8,128)(2,1)S(1)}, bf16[8,160,512]{2,1,0:T(8,128)(2,1)S(1)}, u32[]{:S(2)}, u32[]{:S(2)}) collective-permute-start(bf16[8,160,512]{2,1,0:T(8,128)(2,1)S(1)} %get-tuple-element.617), channel_id=1, source_target_pairs={{0,8},{2,10},{4,12},{6,14},{8,0},{10,2},{12,4},{14,6},{16,24},{18,... | collective-permute-start | bytes 3932168 | tf_op jit(solution)/shard_map/ppermute | solution.py:821
  132.7 23.3 %collective-permute-start.12 = (bf16[4,192,512]{2,1,0:T(8,128)(2,1)S(1)}, bf16[4,192,512]{2,1,0:T(8,128)(2,1)S(1)}, u32[]{:S(2)}, u32[]{:S(2)}) collective-permute-start(bf16[4,192,512]{2,1,0:T(8,128)(2,1)S(1)} %get-tuple-element.596), channel_id=1, source_target_pairs={{0,4},{2,6},{4,0},{6,2},{8,12},{10,14},{12,8},{14,10},{16,20},{18,... | collective-permute-start | bytes 2359304 | tf_op jit(solution)/shard_map/ppermute | solution.py:821
  134.2 26.3 %collective-permute-start.16 = (bf16[4,128,512]{2,1,0:T(8,128)(2,1)S(1)}, bf16[4,128,512]{2,1,0:T(8,128)(2,1)S(1)}, u32[]{:S(2)}, u32[]{:S(2)}) collective-permute-start(bf16[4,128,512]{2,1,0:T(8,128)(2,1)S(1)} %get-tuple-element.620), channel_id=1, source_target_pairs={{0,2},{2,0},{4,6},{6,4},{8,10},{10,8},{12,14},{14,12},{16,18},{18,... | collective-permute-start | bytes 1572872 | tf_op jit(solution)/shard_map/ppermute | solution.py:821
  156.1 24.5 %collective-permute-start.19 = (bf16[2,256,1024]{2,1,0:T(8,128)(2,1)S(1)}, bf16[2,256,1024]{2,1,0:T(8,128)(2,1)S(1)}, u32[]{:S(2)}, u32[]{:S(2)}) collective-permute-start(bf16[2,256,1024]{2,1,0:T(8,128)(2,1)S(1)} %get-tuple-element.669), channel_id=1, source_target_pairs={{0,1},{1,0},{2,3},{3,2},{4,5},{5,4},{6,7},{7,6},{8,9},{9,8},{10,11... | collective-permute-start | bytes 3145736 | tf_op jit(solution)/shard_map/ppermute | solution.py:832
  170.7 27.6 %collective-permute-start.23 = (bf16[8,128,512]{2,1,0:T(8,128)(2,1)S(1)}, bf16[8,128,512]{2,1,0:T(8,128)(2,1)S(1)}, u32[]{:S(2)}, u32[]{:S(2)}) collective-permute-start(bf16[8,128,512]{2,1,0:T(8,128)(2,1)S(1)} %get-tuple-element.693), channel_id=1, source_target_pairs={{0,4},{2,6},{4,0},{6,2},{8,12},{10,14},{12,8},{14,10},{16,20},{18,... | collective-permute-start | bytes 3145736 | tf_op jit(solution)/shard_map/ppermute | solution.py:821
  178.7 20.5 %collective-permute-start.21 = (bf16[8,64,512]{2,1,0:T(8,128)(2,1)S(1)}, bf16[8,64,512]{2,1,0:T(8,128)(2,1)S(1)}, u32[]{:S(2)}, u32[]{:S(2)}) collective-permute-start(bf16[8,64,512]{2,1,0:T(8,128)(2,1)S(1)} %get-tuple-element.685), channel_id=1, source_target_pairs={{0,2},{2,0},{4,6},{6,4},{8,10},{10,8},{12,14},{14,12},{16,18},{18,... | collective-permute-start | bytes 1572872 | tf_op jit(solution)/shard_map/ppermute | solution.py:821
  180.5 33.6 %collective-permute-start.28 = (bf16[4,160,512]{2,1,0:T(8,128)(2,1)S(1)}, bf16[4,160,512]{2,1,0:T(8,128)(2,1)S(1)}, u32[]{:S(2)}, u32[]{:S(2)}) collective-permute-start(bf16[4,160,512]{2,1,0:T(8,128)(2,1)S(1)} %get-tuple-element.720), channel_id=1, source_target_pairs={{0,4},{2,6},{4,0},{6,2},{8,12},{10,14},{12,8},{14,10},{16,20},{18,... | collective-permute-start | bytes 1966088 | tf_op jit(solution)/shard_map/ppermute | solution.py:821
  196.7 20.5 %collective-permute-start.29 = (bf16[2,128,512]{2,1,0:T(8,128)(2,1)S(1)}, bf16[2,128,512]{2,1,0:T(8,128)(2,1)S(1)}, u32[]{:S(2)}, u32[]{:S(2)}) collective-permute-start(bf16[2,128,512]{2,1,0:T(8,128)(2,1)S(1)} %get-tuple-element.725), channel_id=1, source_target_pairs={{0,4},{2,6},{4,0},{6,2},{8,12},{10,14},{12,8},{14,10},{16,20},{18,... | collective-permute-start | bytes 786440 | tf_op jit(solution)/shard_map/ppermute | solution.py:821
  198.3 29.4 %collective-permute-start.26 = (bf16[8,64,512]{2,1,0:T(8,128)(2,1)S(1)}, bf16[8,64,512]{2,1,0:T(8,128)(2,1)S(1)}, u32[]{:S(2)}, u32[]{:S(2)}) collective-permute-start(bf16[8,64,512]{2,1,0:T(8,128)(2,1)S(1)} %get-tuple-element.718), channel_id=1, source_target_pairs={{0,4},{2,6},{4,0},{6,2},{8,12},{10,14},{12,8},{14,10},{16,20},{18,... | collective-permute-start | bytes 1572872 | tf_op jit(solution)/shard_map/ppermute | solution.py:821
  217.2 31.0 %collective-permute-start.34 = (bf16[4,64,512]{2,1,0:T(8,128)(2,1)S(1)}, bf16[4,64,512]{2,1,0:T(8,128)(2,1)S(1)}, u32[]{:S(2)}, u32[]{:S(2)}) collective-permute-start(bf16[4,64,512]{2,1,0:T(8,128)(2,1)S(1)} %get-tuple-element.749), channel_id=1, source_target_pairs={{0,4},{2,6},{4,0},{6,2},{8,12},{10,14},{12,8},{14,10},{16,20},{18,... | collective-permute-start | bytes 786440 | tf_op jit(solution)/shard_map/ppermute | solution.py:821
  257.7 21.9 %collective-permute-start.47 = (bf16[4,192,512]{2,1,0:T(8,128)(2,1)S(1)}, bf16[4,192,512]{2,1,0:T(8,128)(2,1)S(1)}, u32[]{:S(2)}, u32[]{:S(2)}) collective-permute-start(bf16[4,192,512]{2,1,0:T(8,128)(2,1)S(1)} %pad_maximum_fusion.6), channel_id=1, source_target_pairs={{0,4},{2,6},{4,0},{6,2},{8,12},{10,14},{12,8},{14,10},{16,20},{18,... | collective-permute-start | bytes 2359304 | tf_op jit(solution)/shard_map/ppermute | solution.py:821
  276.8 37.9 %collective-permute-start.58 = (bf16[8,192,512]{2,1,0:T(8,128)(2,1)S(1)}, bf16[8,192,512]{2,1,0:T(8,128)(2,1)S(1)}, u32[]{:S(2)}, u32[]{:S(2)}) collective-permute-start(bf16[8,192,512]{2,1,0:T(8,128)(2,1)S(1)} %pad_maximum_fusion.refs_1_), channel_id=1, source_target_pairs={{0,4},{2,6},{4,0},{6,2},{8,12},{10,14},{12,8},{14,10},{16,20},{18,... | collective-permute-start | bytes 4718600 | tf_op jit(solution)/shard_map/ppermute | solution.py:821
  284.7 44.0 %collective-permute-start.61 = (bf16[8,192,512]{2,1,0:T(8,128)(2,1)S(1)}, bf16[8,192,512]{2,1,0:T(8,128)(2,1)S(1)}, u32[]{:S(2)}, u32[]{:S(2)}) collective-permute-start(bf16[8,192,512]{2,1,0:T(8,128)(2,1)S(1)} %pad_maximum_fusion.1.refs_1_), channel_id=1, source_target_pairs={{0,2},{2,0},{4,6},{6,4},{8,10},{10,8},{12,14},{14,12},{16,18},{18,... | collective-permute-start | bytes 4718600 | tf_op jit(solution)/shard_map/ppermute | solution.py:821
  314.7 33.3 %collective-permute-start.69 = (bf16[2,128,768]{2,1,0:T(8,128)(2,1)S(1)}, bf16[2,128,768]{2,1,0:T(8,128)(2,1)S(1)}, u32[]{:S(2)}, u32[]{:S(2)}) collective-permute-start(bf16[2,128,768]{2,1,0:T(8,128)(2,1)S(1)} %get-tuple-element.921), channel_id=1, source_target_pairs={{0,1},{1,0},{2,3},{3,2},{4,5},{5,4},{6,7},{7,6},{8,9},{9,8},{10,11... | collective-permute-start | bytes 1179656 | tf_op jit(solution)/shard_map/ppermute | solution.py:832
  335.0 32.3 %collective-permute-start.73 = (bf16[8,160,512]{2,1,0:T(8,128)(2,1)S(1)}, bf16[8,160,512]{2,1,0:T(8,128)(2,1)}, u32[]{:S(2)}, u32[]{:S(2)}) collective-permute-start(bf16[8,160,512]{2,1,0:T(8,128)(2,1)S(1)} %pad_maximum_fusion.2.refs_1_), channel_id=1, source_target_pairs={{0,8},{2,10},{4,12},{6,14},{8,0},{10,2},{12,4},{14,6},{16,24},{18,... | collective-permute-start | bytes 3932168 | tf_op jit(solution)/shard_map/ppermute | solution.py:821
  344.7 28.5 %collective-permute-start.75 = (bf16[8,64,512]{2,1,0:T(8,128)(2,1)}, bf16[8,64,512]{2,1,0:T(8,128)(2,1)}, u32[]{:S(2)}, u32[]{:S(2)}) collective-permute-start(bf16[8,64,512]{2,1,0:T(8,128)(2,1)} %pad_maximum_fusion.10.refs_1_), channel_id=1, source_target_pairs={{0,2},{2,0},{4,6},{6,4},{8,10},{10,8},{12,14},{14,12},{16,18},{18,... | collective-permute-start | bytes 1572872 | tf_op jit(solution)/shard_map/ppermute | solution.py:821
  345.4 53.4 %collective-permute-start.79 = (bf16[8,128,512]{2,1,0:T(8,128)(2,1)S(1)}, bf16[8,128,512]{2,1,0:T(8,128)(2,1)}, u32[]{:S(2)}, u32[]{:S(2)}) collective-permute-start(bf16[8,128,512]{2,1,0:T(8,128)(2,1)S(1)} %pad_maximum_fusion.3.refs_1_), channel_id=1, source_target_pairs={{0,4},{2,6},{4,0},{6,2},{8,12},{10,14},{12,8},{14,10},{16,20},{18,... | collective-permute-start | bytes 3145736 | tf_op jit(solution)/shard_map/ppermute | solution.py:821
  356.9 38.3 %collective-permute-start.80 = (bf16[8,128,512]{2,1,0:T(8,128)(2,1)S(1)}, bf16[8,128,512]{2,1,0:T(8,128)(2,1)}, u32[]{:S(2)}, u32[]{:S(2)}) collective-permute-start(bf16[8,128,512]{2,1,0:T(8,128)(2,1)S(1)} %pad_maximum_fusion.4.refs_1_), channel_id=1, source_target_pairs={{0,8},{2,10},{4,12},{6,14},{8,0},{10,2},{12,4},{14,6},{16,24},{18,... | collective-permute-start | bytes 3145736 | tf_op jit(solution)/shard_map/ppermute | solution.py:821
  365.9 22.4 %collective-permute-start.81 = (bf16[8,64,512]{2,1,0:T(8,128)(2,1)}, bf16[8,64,512]{2,1,0:T(8,128)(2,1)S(1)}, u32[]{:S(2)}, u32[]{:S(2)}) collective-permute-start(bf16[8,64,512]{2,1,0:T(8,128)(2,1)} %pad_maximum_fusion.12.refs_1_), channel_id=1, source_target_pairs={{0,2},{2,0},{4,6},{6,4},{8,10},{10,8},{12,14},{14,12},{16,18},{18,... | collective-permute-start | bytes 1572872 | tf_op jit(solution)/shard_map/ppermute | solution.py:821
  373.3 29.2 %collective-permute-start.78 = (bf16[8,64,512]{2,1,0:T(8,128)(2,1)S(1)}, bf16[8,64,512]{2,1,0:T(8,128)(2,1)S(1)}, u32[]{:S(2)}, u32[]{:S(2)}) collective-permute-start(bf16[8,64,512]{2,1,0:T(8,128)(2,1)S(1)} %copy-done.37), channel_id=1, source_target_pairs={{0,4},{2,6},{4,0},{6,2},{8,12},{10,14},{12,8},{14,10},{16,20},{18,... | collective-permute-start | bytes 1572872 | tf_op jit(solution)/shard_map/ppermute | solution.py:821
  (129 other events, 1112.9 us)
